TPU v7x, 32 devices: a whole 2x2x4 slice. The times are simulated.
32 devices in a mesh: grp: 4 (over y, x), tok: 4 (over z), fs: 2 (over core).
Axes of the slice: x: 2, y: 2, z: 4, core: 2. Of those that a mesh axis runs over, the one named last changes fastest.
Arguments:
- hidden_in: bfloat16 [8192, 2304], P(('grp', 'tok', 'fs')), may hold values from -6 to 6
- cotangent: bfloat16 [8192, 2304], P(('grp', 'tok', 'fs')), may hold values from -6 to 6
- block_start: int32 [4, 16], P('grp'), may hold values from 0 to 1152, as said below
- query_weight: bfloat16 [2304, 2304], P(('tok', 'fs')), may hold values from -0.125 to 0.125
- key_weight: bfloat16 [2304, 2304], P(('tok', 'fs')), may hold values from -0.125 to 0.125
- value_weight: bfloat16 [2304, 2304], P(('tok', 'fs')), may hold values from -0.125 to 0.125
- output_weight: bfloat16 [2304, 2304], P(('tok', 'fs')), may hold values from -2 to 2
- gate_weight: bfloat16 [2304, 5760], P(('tok', 'fs')), may hold values from -0.125 to 0.125
- up_weight: bfloat16 [2304, 5760], P(('tok', 'fs')), may hold values from -0.125 to 0.125
- down_weight: bfloat16 [5760, 2304], P(('tok', 'fs')), may hold values from -0.3125 to 0.3125
- first_gain: bfloat16 [2304], P(('tok', 'fs')), may hold values from 0.099609375 to 1.8984375
- second_gain: bfloat16 [2304], P(('tok', 'fs')), may hold values from 0.099609375 to 1.8984375
Outputs:
- layer_output: bfloat16 [8192, 2304], P(('grp', 'tok', 'fs'))
- input_grad: float32 [8192, 2304], P(('grp', 'tok', 'fs'))
- query_grad: float32 [2304, 2304], P(('grp', 'tok', 'fs'))
- key_grad: float32 [2304, 2304], P(('grp', 'tok', 'fs'))
- value_grad: float32 [2304, 2304], P(('grp', 'tok', 'fs'))
- output_grad: float32 [2304, 2304], P(('grp', 'tok', 'fs'))
- gate_grad: float32 [2304, 5760], P(('grp', 'tok', 'fs'))
- up_grad: float32 [2304, 5760], P(('grp', 'tok', 'fs'))
- down_grad: float32 [5760, 2304], P(('grp', 'tok', 'fs'))
- first_gain_grad: float32 [2304], P(('grp', 'tok', 'fs'))
- second_gain_grad: float32 [2304], P(('grp', 'tok', 'fs'))
Inputs may be any that keep to these rules, and one draw needn't show every extreme that they name: `block_start`: in each group, the first 8 entries are 0, 128, ..., 896 in some order, and each following run of 2 entries holds the starts 1024 + j * 128 for j = 0 to 1, in some order.
All inputs are finite; a program needn't handle non-finite values.
Results may differ from a plain program's by a relative error of at most 0.019.
Values may be sent and summed in bfloat16 or wider, within the bound.
No kernel may reach another device: no remote copies, remote signals or barrier semaphores. Data moves between devices by JAX's collectives and lax.ppermute only.
A program may use at most 704 MiB of HBM per device.

v0:
```python
import math

import jax
import jax.numpy as jnp
from jax import lax
from jax.sharding import PartitionSpec as P

HEAD_DIM = 64
BLOCK = 128
PROMPT = 1024
CONT = 256


EPS = 1e-05
RESIDUAL = 1.4 / math.sqrt(40.0)
NEGATIVE = -1e30
GROUP_HEADS = 4


def spread(block, axis, source):
    block = jnp.where(lax.axis_index(axis) == source, block, jnp.zeros_like(block))
    return lax.psum(block, axis)


def rope_tables(positions, head_size):
    half = head_size // 2
    freq = 10000.0 ** (-(jnp.arange(half, dtype=jnp.float32) * 2.0) / head_size)
    angle = positions.astype(jnp.float32)[:, None] * freq[None, :]
    return (jnp.cos(angle)[:, None, :], jnp.sin(angle)[:, None, :])


def rotate(field, cosine, sine):
    half = field.shape[-1] // 2
    first = field[..., :half]
    second = field[..., half:]
    return jnp.concatenate(
        [first * cosine - second * sine, second * cosine + first * sine], axis=-1
    )


def unrotate(grad, cosine, sine):
    half = grad.shape[-1] // 2
    first = grad[..., :half]
    second = grad[..., half:]
    return jnp.concatenate(
        [first * cosine + second * sine, second * cosine - first * sine], axis=-1
    )


def row_norm(values):
    return values * lax.rsqrt(jnp.mean(values * values, axis=-1, keepdims=True) + EPS)


def swish_product(gate, up_val):
    return jax.nn.silu(gate) * up_val


def contract_rows(left, right):
    return lax.dot_general(
        left, right, (((0,), (0,)), ((), ())), preferred_element_type=jnp.float32
    )


def contract_cols(left, right):
    return lax.dot_general(
        left, right, (((1,), (1,)), ((), ())), preferred_element_type=jnp.float32
    )


def weight_sums(left, right):
    return lax.psum_scatter(
        contract_rows(left, right), ("grp", "tok", "fs"), scatter_dimension=0, tiled=True
    )


def local(
    hidden_in,
    cotangent,
    block_start,
    query_weight,
    key_weight,
    value_weight,
    output_weight,
    gate_weight,
    up_weight,
    down_weight,
    first_gain,
    second_gain,
):
    local_rows, width = hidden_in.shape
    ff_width = gate_weight.shape[1]
    head_size = HEAD_DIM
    heads = width // head_size
    group_width = GROUP_HEADS * head_size
    group_count = heads // GROUP_HEADS
    scale = 1.0 / math.sqrt(head_size)
    device = lax.axis_index(("tok", "fs"))
    holders = -(-PROMPT // local_rows)
    prompt_rows = holders * local_rows
    starts = block_start[0]
    offsets = jnp.arange(BLOCK, dtype=jnp.int32)
    local_starts = lax.dynamic_slice_in_dim(
        starts, device * (local_rows // BLOCK), local_rows // BLOCK
    )
    my_pos = (local_starts[:, None] + offsets[None, :]).reshape(local_rows)
    prompt_pos = (starts[: prompt_rows // BLOCK][:, None] + offsets[None, :]).reshape(prompt_rows)
    my_row = device * local_rows + jnp.arange(local_rows, dtype=jnp.int32)
    my_seg = jnp.where(my_row < PROMPT, 0, 1 + (my_row - PROMPT) // CONT)
    prompt_row = jnp.arange(prompt_rows, dtype=jnp.int32)
    prompt_seen = (prompt_row[None, :] < PROMPT) & (prompt_pos[None, :] <= my_pos[:, None])
    local_seen = (
        (my_seg[None, :] == my_seg[:, None])
        & (my_seg[None, :] > 0)
        & (my_pos[None, :] <= my_pos[:, None])
    )
    visible = jnp.concatenate([prompt_seen, local_seen], axis=1)
    cosine, sine = rope_tables(my_pos, head_size)
    hidden = hidden_in.astype(jnp.float32)
    normed_one, pull_one = jax.vjp(row_norm, hidden)
    zero_rows = jnp.zeros((local_rows, width), jnp.float32)
    pieces = (
        lax.all_gather(query_weight, ("tok", "fs"), axis=0, tiled=True),
        lax.all_gather(key_weight, ("tok", "fs"), axis=0, tiled=True),
        lax.all_gather(value_weight, ("tok", "fs"), axis=0, tiled=True),
        lax.all_gather(first_gain, ("tok", "fs"), axis=0, tiled=True),
    )
    normed = normed_one
    scaled = (normed * pieces[3].astype(jnp.float32)[None, :]).astype(jnp.bfloat16)
    kept = scaled
    query_acc = jnp.dot(scaled, pieces[0], preferred_element_type=jnp.float32)
    key_acc = jnp.dot(scaled, pieces[1], preferred_element_type=jnp.float32)
    value_acc = jnp.dot(scaled, pieces[2], preferred_element_type=jnp.float32)
    kept_one = kept
    queries = (
        rotate(query_acc.reshape(local_rows, heads, head_size), cosine, sine)
        .astype(jnp.bfloat16)
        .reshape(local_rows, width)
    )
    keys = (
        rotate(key_acc.reshape(local_rows, heads, head_size), cosine, sine)
        .astype(jnp.bfloat16)
        .reshape(local_rows, width)
    )
    values = value_acc.astype(jnp.bfloat16)
    paired = jnp.stack([keys, values])
    received = []
    for root in range(holders):
        received.append(spread(paired, ("tok", "fs"), root))
    gathered = jnp.concatenate(received, axis=1)
    all_keys = jnp.concatenate([gathered[0], keys], axis=0)
    all_values = jnp.concatenate([gathered[1], values], axis=0)
    total_keys = all_keys.shape[0]

    def head_slice(array, index):
        return lax.dynamic_slice_in_dim(array, index * group_width, group_width, 1).reshape(
            array.shape[0], GROUP_HEADS, head_size
        )

    def scores_of(index):
        raw = (
            jnp.einsum(
                "qhd,khd->hqk",
                head_slice(queries, index),
                head_slice(all_keys, index),
                preferred_element_type=jnp.float32,
            )
            * scale
        )
        return jnp.where(visible[None], raw, NEGATIVE)

    def attend_group(index, carry):
        mixed, peaks, totals = carry
        scores = scores_of(index)
        peak = jnp.max(scores, axis=-1, keepdims=True)
        expo = jnp.exp(scores - peak)
        total = jnp.sum(expo, axis=-1, keepdims=True)
        probs = (expo / total).astype(jnp.bfloat16)
        block_out = jnp.einsum(
            "hqk,khd->qhd", probs, head_slice(all_values, index), preferred_element_type=jnp.float32
        ).reshape(local_rows, group_width)
        mixed = lax.dynamic_update_slice_in_dim(mixed, block_out, index * group_width, 1)
        peaks = lax.dynamic_update_slice_in_dim(peaks, peak[None, :, :, 0], index, 0)
        totals = lax.dynamic_update_slice_in_dim(totals, total[None, :, :, 0], index, 0)
        return (mixed, peaks, totals)

    stats_zero = jnp.zeros((group_count, GROUP_HEADS, local_rows), jnp.float32)
    mixed, peaks, totals = lax.fori_loop(
        0, group_count, attend_group, (zero_rows, stats_zero, stats_zero)
    )
    attention_out = mixed.astype(jnp.bfloat16)
    branch = jnp.dot(
        attention_out,
        lax.all_gather(output_weight, ("tok", "fs"), axis=0, tiled=True),
        preferred_element_type=jnp.float32,
    )
    second_in = hidden + RESIDUAL * branch
    normed_two, pull_two = jax.vjp(row_norm, second_in)
    retained = ()
    pieces = (
        lax.all_gather(gate_weight, ("tok", "fs"), axis=0, tiled=True),
        lax.all_gather(up_weight, ("tok", "fs"), axis=0, tiled=True),
        lax.all_gather(second_gain, ("tok", "fs"), axis=0, tiled=True),
    )
    start = jnp.int32(0)
    stored = retained
    normed = normed_two
    scaled = (normed * pieces[2].astype(jnp.float32)[None, :]).astype(jnp.bfloat16)
    kept = scaled
    stored = tuple(
        (
            lax.dynamic_update_slice_in_dim(buffer, piece, start, 0)
            for buffer, piece in zip(stored, pieces)
        )
    )
    gate_acc, up_acc, kept_two, stored = (
        jnp.dot(scaled, pieces[0], preferred_element_type=jnp.float32),
        jnp.dot(scaled, pieces[1], preferred_element_type=jnp.float32),
        kept,
        stored,
    )
    swish, pull_swish = jax.vjp(swish_product, gate_acc, up_acc)
    act = swish.astype(jnp.bfloat16)
    down_store = ()
    piece = lax.all_gather(down_weight, ("tok", "fs"), axis=0, tiled=True)
    start = jnp.int32(0)
    stored_down = down_store
    total_acc = jnp.dot(act, piece, preferred_element_type=jnp.float32)
    stored_down = tuple(
        (lax.dynamic_update_slice_in_dim(buffer, piece, start, 0) for buffer in stored_down)
    )
    feed, stored_down = (total_acc, stored_down)
    layer_output = (second_in + RESIDUAL * feed).astype(jnp.bfloat16)
    grad_out = cotangent.astype(jnp.float32)
    grad_m = (RESIDUAL * grad_out).astype(jnp.bfloat16)
    grad_act = contract_cols(grad_m, lax.all_gather(down_weight, ("tok", "fs"), axis=0, tiled=True))
    down_grad = weight_sums(act, grad_m)
    grad_gate_f, grad_up_f = pull_swish(grad_act)
    grad_gate = grad_gate_f.astype(jnp.bfloat16)
    grad_up = grad_up_f.astype(jnp.bfloat16)
    pieces = (
        lax.all_gather(gate_weight, ("tok", "fs"), axis=0, tiled=True),
        lax.all_gather(up_weight, ("tok", "fs"), axis=0, tiled=True),
        lax.all_gather(second_gain, ("tok", "fs"), axis=0, tiled=True),
    )
    section = contract_cols(grad_gate, pieces[0]) + contract_cols(grad_up, pieces[1])
    normed = normed_two
    grad_normed = section * pieces[2].astype(jnp.float32)[None, :]
    gain_sum = jnp.sum(section * normed, axis=0)
    grad_n2 = grad_normed
    gain_two = gain_sum
    both_grads = jnp.concatenate([grad_gate, grad_up], axis=1)
    mixer_grad = weight_sums(kept_two, both_grads)
    grad_second = grad_out + pull_two(grad_n2)[0]
    grad_z = (RESIDUAL * grad_second).astype(jnp.bfloat16)
    output_full = contract_rows(attention_out, grad_z)
    grad_attn = contract_cols(
        grad_z, lax.all_gather(output_weight, ("tok", "fs"), axis=0, tiled=True)
    ).astype(jnp.bfloat16)

    def attend_back(index, carry):
        grad_q, grad_k, grad_v = carry
        query_g = head_slice(queries, index)
        key_g = head_slice(all_keys, index)
        value_g = head_slice(all_values, index)
        outer_g = head_slice(grad_attn, index)
        scores = scores_of(index)
        peak = lax.dynamic_index_in_dim(peaks, index, 0, keepdims=False)[:, :, None]
        total = lax.dynamic_index_in_dim(totals, index, 0, keepdims=False)[:, :, None]
        probs = jnp.exp(scores - peak) / total
        grad_probs = jnp.einsum(
            "qhd,khd->hqk", outer_g, value_g, preferred_element_type=jnp.float32
        )
        grad_scores = (
            probs * (grad_probs - jnp.sum(grad_probs * probs, axis=-1, keepdims=True))
        ).astype(jnp.bfloat16)
        query_part = (
            jnp.einsum("hqk,khd->qhd", grad_scores, key_g, preferred_element_type=jnp.float32)
            * scale
        )
        key_part = (
            jnp.einsum("hqk,qhd->khd", grad_scores, query_g, preferred_element_type=jnp.float32)
            * scale
        )
        value_part = jnp.einsum(
            "hqk,qhd->khd", probs.astype(jnp.bfloat16), outer_g, preferred_element_type=jnp.float32
        )
        grad_q = lax.dynamic_update_slice_in_dim(
            grad_q, query_part.reshape(local_rows, group_width), index * group_width, 1
        )
        grad_k = lax.dynamic_update_slice_in_dim(
            grad_k, key_part.reshape(total_keys, group_width), index * group_width, 1
        )
        grad_v = lax.dynamic_update_slice_in_dim(
            grad_v, value_part.reshape(total_keys, group_width), index * group_width, 1
        )
        return (grad_q, grad_k, grad_v)

    zero_keys = jnp.zeros((total_keys, width), jnp.float32)
    grad_q, grad_k, grad_v = lax.fori_loop(
        0, group_count, attend_back, (zero_rows, zero_keys, zero_keys)
    )
    share_k, share_v = (
        lax.psum_scatter(
            grad_k[:prompt_rows].astype(jnp.bfloat16),
            ("tok", "fs"),
            scatter_dimension=1,
            tiled=True,
        ).astype(jnp.float32),
        lax.psum_scatter(
            grad_v[:prompt_rows].astype(jnp.bfloat16),
            ("tok", "fs"),
            scatter_dimension=1,
            tiled=True,
        ).astype(jnp.float32),
    )
    prompt_dk, prompt_dv = (
        lax.all_gather(share_k.astype(jnp.bfloat16), ("tok", "fs"), axis=1, tiled=True).astype(
            share_k.dtype
        ),
        lax.all_gather(share_v.astype(jnp.bfloat16), ("tok", "fs"), axis=1, tiled=True).astype(
            share_v.dtype
        ),
    )
    holder = jnp.minimum(device, holders - 1)
    owned = device < holders
    mine_k = (
        jnp.where(
            owned, lax.dynamic_slice_in_dim(prompt_dk, holder * local_rows, local_rows, 0), 0.0
        )
        + grad_k[prompt_rows:]
    )
    mine_v = (
        jnp.where(
            owned, lax.dynamic_slice_in_dim(prompt_dv, holder * local_rows, local_rows, 0), 0.0
        )
        + grad_v[prompt_rows:]
    )
    grad_qraw = (
        unrotate(grad_q.reshape(local_rows, heads, head_size), cosine, sine)
        .reshape(local_rows, width)
        .astype(jnp.bfloat16)
    )
    grad_kraw = (
        unrotate(mine_k.reshape(local_rows, heads, head_size), cosine, sine)
        .reshape(local_rows, width)
        .astype(jnp.bfloat16)
    )
    grad_vraw = mine_v.astype(jnp.bfloat16)
    pieces = (
        lax.all_gather(query_weight, ("tok", "fs"), axis=0, tiled=True),
        lax.all_gather(key_weight, ("tok", "fs"), axis=0, tiled=True),
        lax.all_gather(value_weight, ("tok", "fs"), axis=0, tiled=True),
        lax.all_gather(first_gain, ("tok", "fs"), axis=0, tiled=True),
    )
    section = (
        contract_cols(grad_qraw, pieces[0])
        + contract_cols(grad_kraw, pieces[1])
        + contract_cols(grad_vraw, pieces[2])
    )
    normed = normed_one
    grad_normed = section * pieces[3].astype(jnp.float32)[None, :]
    gain_sum = jnp.sum(section * normed, axis=0)
    three_grads = jnp.concatenate([grad_qraw, grad_kraw, grad_vraw], axis=1)
    attention_grad = weight_sums(kept_one, three_grads)
    input_grad = grad_second + pull_one(grad_normed)[0]
    output_grad, first_gain_grad, second_gain_grad = (
        lax.psum_scatter(output_full, ("grp", "tok", "fs"), scatter_dimension=0, tiled=True),
        lax.psum_scatter(gain_sum, ("grp", "tok", "fs"), scatter_dimension=0, tiled=True),
        lax.psum_scatter(gain_two, ("grp", "tok", "fs"), scatter_dimension=0, tiled=True),
    )
    return (
        layer_output,
        input_grad,
        attention_grad[:, :width],
        attention_grad[:, width : 2 * width],
        attention_grad[:, 2 * width :],
        output_grad,
        mixer_grad[:, :ff_width],
        mixer_grad[:, ff_width:],
        down_grad,
        first_gain_grad,
        second_gain_grad,
    )


def solution(mesh):
    return jax.shard_map(
        local,
        mesh=mesh,
        in_specs=(
            P(("grp", "tok", "fs"), None),
            P(("grp", "tok", "fs"), None),
            P("grp", None),
            P(("tok", "fs"), None),
            P(("tok", "fs"), None),
            P(("tok", "fs"), None),
            P(("tok", "fs"), None),
            P(("tok", "fs"), None),
            P(("tok", "fs"), None),
            P(("tok", "fs"), None),
            P(("tok", "fs")),
            P(("tok", "fs")),
        ),
        out_specs=(
            P(("grp", "tok", "fs"), None),
            P(("grp", "tok", "fs"), None),
            P(("grp", "tok", "fs"), None),
            P(("grp", "tok", "fs"), None),
            P(("grp", "tok", "fs"), None),
            P(("grp", "tok", "fs"), None),
            P(("grp", "tok", "fs"), None),
            P(("grp", "tok", "fs"), None),
            P(("grp", "tok", "fs"), None),
            P(("grp", "tok", "fs")),
            P(("grp", "tok", "fs")),
        ),
        check_vma=False,
    )
```

profile of v0, /device:TPU:1, one launch (start us, length us, event | category | flops | bytes accessed | tf_op | source)
XLA Modules:
  0.0 4325.3 jit_solution(2861447504988151734)
XLA Ops:
  11.3 26.8 all-reduce.8
  39.4 73.7 %all-gather.10.cloned.1.call-done = bf16[2304,2304]{1,0:T(8,128)(2,1)} async-done(((bf16[288,2304]{1,0:T(8,128)(2,1)}), bf16[2304,2304]{1,0:T(8,128)(2,1)}) %all-gather.10.cloned.1.call-update) | async-done | bytes 10616848 | tf_op jit(solution)/shard_map/all_gather | solution.py:123
  113.1 7.0 fusion.50
  121.4 92.2 %all-gather.12.cloned.1.call-done = bf16[2304,2304]{1,0:T(8,128)(2,1)} async-done(((bf16[288,2304]{1,0:T(8,128)(2,1)}), bf16[2304,2304]{1,0:T(8,128)(2,1)}) %all-gather.12.cloned.1.call-update) | async-done | bytes 10616848 | tf_op jit(solution)/shard_map/all_gather | solution.py:124
  213.6 7.0 convolution_convert_fusion.1
  220.6 4.6 broadcast_select_fusion
  232.8 81.3 %all-gather.14.cloned.1.call-done = bf16[2304,2304]{1,0:T(8,128)(2,1)} async-done(((bf16[288,2304]{1,0:T(8,128)(2,1)}), bf16[2304,2304]{1,0:T(8,128)(2,1)}) %all-gather.14.cloned.1.call-update) | async-done | bytes 10616848 | tf_op jit(solution)/shard_map/all_gather | solution.py:122
  314.2 7.0 fusion.47
  322.8 188.6 %all-reduce.15.cloned.1.call-done = (bf16[2,256,2304]{2,1,0:T(8,128)(2,1)}, bf16[2,256,2304]{2,1,0:T(8,128)(2,1)}, bf16[2,256,2304]{2,1,0:T(8,128)(2,1)}, bf16[2,256,2304]{2,1,0:T(8,128)(2,1)}) async-done(((bf16[2,256,2304]{2,1,0:T(8,128)(2,1)}, bf16[2,256,2304]{2,1,0:T(8,128)(2,1)}, bf16[2,256,2304]{2,1,0:T(8,128)(2,1)}, bf16[2,256,2304]{2,1,0:T(8,128)(2,1)}), (bf16[2,256,2304]{2,1,0:T(8,128)(2,1)}, ...) | async-done | bytes 9437200 | tf_op jit(solution)/shard_map/psum | solution.py:22
  511.4 3.4 constant_dynamic-update-slice_fusion.7
  521.4 5.5 slice_bitcast_fusion
  527.0 5.7 pad_maximum_fusion
  532.7 8.9 copy.48
  541.5 9.1 copy.49
  550.6 64.2 %while.34 = (s32[]{:T(128)}, bf16[256,2304]{0,1:T(8,128)(2,1)S(1)}, f32[9,4,256]{2,1,0:T(4,128)}, f32[9,4,256]{2,1,0:T(4,128)}, bf16[1280,2304]{0,1:T(8,128)(2,1...) while((s32[]{:T(128)}, bf16[256,2304]{0,1:T(8,128)(2,1)S(1)}, ...), condition=%wide.region_8.9_spmd, body=%wide.region_5.8_spmd.sunk | while | flops 346028032 | bytes 20811968 | solution.py:187
  615.8 6.6 multiply_reduce_fusion.3
  623.2 222.0 %all-gather.18.cloned.1.call-done = bf16[2304,5760]{1,0:T(8,128)(2,1)} async-done(((bf16[288,5760]{1,0:T(8,128)(2,1)}), bf16[2304,5760]{1,0:T(8,128)(2,1)}) %all-gather.18.cloned.1.call-update) | async-done | bytes 26542096 | tf_op jit(solution)/shard_map/all_gather | solution.py:200
  845.2 16.5 fusion.55
  861.7 214.5 %all-gather.20.cloned.1.call-done = bf16[2304,5760]{1,0:T(8,128)(2,1)} async-done(((bf16[288,5760]{1,0:T(8,128)(2,1)}), bf16[2304,5760]{1,0:T(8,128)(2,1)}) %all-gather.20.cloned.1.call-update) | async-done | bytes 26542096 | tf_op jit(solution)/shard_map/all_gather | solution.py:201
  1076.2 16.3 fusion.56
  1092.5 214.7 %all-gather.22.cloned.1.call-done = bf16[5760,2304]{1,0:T(8,128)(2,1)} async-done(((bf16[720,2304]{1,0:T(8,128)(2,1)}), bf16[5760,2304]{1,0:T(8,128)(2,1)}) %all-gather.22.cloned.1.call-update) | async-done | bytes 26542096 | tf_op jit(solution)/shard_map/all_gather | solution.py:224
  1307.2 20.2 multiply_convert_fusion.1
  1327.4 14.8 fusion.57
  1342.2 14.9 multiply_reduce_fusion.1
  1357.8 7.8 convolution_convert_fusion
  1367.3 5.0 broadcast_in_dim.123
  1372.4 5.0 broadcast_in_dim.123.clone
  1377.3 146.0 %while.35 = (s32[]{:T(128)}, f32[256,2304]{0,1:T(8,128)}, f32[1280,2304]{0,1:T(8,128)}, f32[1280,2304]{0,1:T(8,128)}, bf16[1280,2304]{0,1:T(8,128)(2,1)}, /*inde...) while((s32[]{:T(128)}, f32[256,2304]{0,1:T(8,128)}, ...), condition=%wide.region_13.14_spmd, body=%wide.region_11.13_spmd.sunk | while | flops 852360192 | bytes 69959952 | solution.py:299
  1383.8 3.6 multiply_reduce_fusion.5
  1400.1 3.6 multiply_reduce_fusion.5
  1416.3 3.6 multiply_reduce_fusion.5
  1428.9 3.4 exponential_divide_fusion.2
  1432.5 3.6 multiply_reduce_fusion.5
  1448.7 3.6 multiply_reduce_fusion.5
  1461.4 3.4 exponential_divide_fusion.2
  1464.9 3.6 multiply_reduce_fusion.5
  1481.2 3.6 multiply_reduce_fusion.5
  1493.9 3.4 exponential_divide_fusion.2
  1497.4 3.6 multiply_reduce_fusion.5
  1513.6 3.6 multiply_reduce_fusion.5
  1523.3 6.6 slice.122
  1530.0 6.6 slice.121
  1536.6 44.0 %reduce-scatter.7.cloned.1.call-done = bf16[1024,288]{0,1:T(8,128)(2,1)} async-done(((bf16[1024,2304]{0,1:T(8,128)(2,1)}), bf16[1024,288]{0,1:T(8,128)(2,1)}) %reduce-scatter.7.cloned.1.call-update) | async-done | bytes 589840 | tf_op jit(solution)/shard_map/reduce_scatter | solution.py:303
  1580.7 55.4 %reduce-scatter.9.cloned.1.call-done = bf16[1024,288]{0,1:T(8,128)(2,1)} async-done(((bf16[1024,2304]{0,1:T(8,128)(2,1)}), bf16[1024,288]{0,1:T(8,128)(2,1)}) %reduce-scatter.9.cloned.1.call-update) | async-done | bytes 589840 | tf_op jit(solution)/shard_map/reduce_scatter | solution.py:309
  1636.3 54.2 %all-gather.24.cloned.1.call-done = bf16[1024,2304]{0,1:T(8,128)(2,1)} async-done(((bf16[1024,288]{0,1:T(8,128)(2,1)}), bf16[1024,2304]{0,1:T(8,128)(2,1)}) %all-gather.24.cloned.1.call-update) | async-done | bytes 4718608 | tf_op jit(solution)/shard_map/all_gather | solution.py:317
  1694.8 47.7 %all-gather.26.cloned.1.call-done = bf16[1024,2304]{0,1:T(8,128)(2,1)} async-done(((bf16[1024,288]{0,1:T(8,128)(2,1)}), bf16[1024,2304]{0,1:T(8,128)(2,1)}) %all-gather.26.cloned.1.call-update) | async-done | bytes 4718608 | tf_op jit(solution)/shard_map/all_gather | solution.py:320
  1744.8 24.6 fusion.15
  1770.6 39.8 fusion.8
  1812.5 9.9 fusion.33
  1823.7 22.0 fusion.29
  1845.7 1090.4 %fusion = f32[192,2304]{1,0:T(8,128)} fusion(f32[5760,2304]{1,0:T(8,128)} %fusion.29), kind=kCustom, calls=%all-reduce-scatter | all-reduce-scatter fusion | flops 14155777 | bytes 54853632
  2937.8 4.4 collective-permute-start
  2943.6 14.7 fusion.14
  2958.3 114.1 %collective-permute-done.1 = f32[180,2304]{1,0:T(8,128)S(1)} collective-permute-done((f32[180,2304]{1,0:T(8,128)S(1)}, f32[180,2304]{1,0:T(8,128)S(1)}, u32[]{:S(2)}, u32[]{:S(2)}) %collective-permute-start.1) | collective-permute-done | bytes 1658912
  3073.6 18.2 concatenate.43
  3095.0 9.3 fusion.58
  3104.4 8.1 convolution_add_fusion.2
  3112.6 5.4 fusion.24
  3118.0 41.0 all-reduce.7
  3162.2 3.7 fusion.26
  3165.9 58.9 %all-reduce.13.cloned.1.call-done = f32[2304,6912]{1,0:T(8,128)} async-done(((f32[2304,6912]{1,0:T(8,128)}), f32[2304,6912]{1,0:T(8,128)}) %all-reduce.13.cloned.1.call-update) | async-done | bytes 63701008
  3228.0 864.0 %reduce-scatter.13.cloned.1.call-done = f32[72,11520]{1,0:T(8,128)} async-done(((f32[2304,11520]{1,0:T(8,128)}), f32[72,11520]{1,0:T(8,128)}) %reduce-scatter.13.cloned.1.call-update) | async-done | bytes 3317776 | tf_op jit(solution)/shard_map/reduce_scatter | solution.py:71
  4092.0 3.9 fusion.54
  4095.9 222.6 %reduce-scatter.11.cloned.1.call-done = f32[72,2304]{1,0:T(8,128)} async-done(((f32[2304,2304]{1,0:T(8,128)}), f32[72,2304]{1,0:T(8,128)}) %reduce-scatter.11.cloned.1.call-update) | async-done | bytes 663568 | tf_op jit(solution)/shard_map/reduce_scatter | solution.py:367
  (422 shorter events, 217.7 us)
Async XLA Ops:
  7.2 3.8 copy-start.47
  7.2 30.9 copy-start.48
  7.2 31.0 copy-start.4
  7.2 105.8 %all-gather.10.cloned.1.call-start = ((), (), s32[]{:S(2)}) async-start(), calls=%async_computation.4 | async-start | bytes 11943936 | tf_op jit(solution)/shard_map/all_gather | solution.py:123
  8.0 205.7 %all-gather.12.cloned.1.call-start = ((), (), s32[]{:S(2)}) async-start(), calls=%async_computation.5 | async-start | bytes 11943936 | tf_op jit(solution)/shard_map/all_gather | solution.py:124
  8.7 305.4 %all-gather.14.cloned.1.call-start = ((), (), s32[]{:S(2)}) async-start(), calls=%async_computation.6 | async-start | bytes 11943936 | tf_op jit(solution)/shard_map/all_gather | solution.py:122
  9.5 502.0 %all-reduce.15.cloned.1.call-start = ((), (), s32[]{:S(2)}) async-start(), calls=%async_computation.18 | async-start | bytes 18874368 | tf_op jit(solution)/shard_map/psum | solution.py:22
  38.1 276.1 %copy-start.28 = (f32[2304]{0:T(1024)}, f32[2304]{0:T(1024)S(1)}, u32[]{:S(2)}) copy-start(f32[2304]{0:T(1024)S(1)} %convert_element_type.121) | copy-start | bytes 27652
  38.5 275.7 %copy-start.37 = (f32[256]{0:T(256)}, f32[256]{0:T(256)S(1)}, u32[]{:S(2)}) copy-start(f32[256]{0:T(256)S(1)} %fusion.36) | copy-start | bytes 3076
  39.4 80.8 %copy-start.31 = (f32[256,32]{0,1:T(8,128)}, f32[256,32]{0,1:T(8,128)S(1)}, u32[]{:S(2)}) copy-start(f32[256,32]{0,1:T(8,128)S(1)} %get-tuple-element.485) | copy-start | bytes 98308
  39.4 80.8 %copy-start.34 = (f32[256,32]{0,1:T(8,128)}, f32[256,32]{0,1:T(8,128)S(1)}, u32[]{:S(2)}) copy-start(f32[256,32]{0,1:T(8,128)S(1)} %get-tuple-element.486) | copy-start | bytes 98308
  220.6 4.8 copy-start.16
  225.4 389.4 %all-gather.16.cloned.1.call-start = ((), (), s32[]{:S(2)}) async-start(), calls=%async_computation.7 | async-start | bytes 11943936 | tf_op jit(solution)/shard_map/all_gather | solution.py:193
  226.0 619.2 %all-gather.18.cloned.1.call-start = ((), (), s32[]{:S(2)}) async-start(), calls=%async_computation.8 | async-start | bytes 29859840 | tf_op jit(solution)/shard_map/all_gather | solution.py:200
  226.5 849.6 %all-gather.20.cloned.1.call-start = ((), (), s32[]{:S(2)}) async-start(), calls=%async_computation.9 | async-start | bytes 29859840 | tf_op jit(solution)/shard_map/all_gather | solution.py:201
  227.3 1079.9 %all-gather.22.cloned.1.call-start = ((), (), s32[]{:S(2)}) async-start(), calls=%async_computation.10 | async-start | bytes 29859840 | tf_op jit(solution)/shard_map/all_gather | solution.py:224
  228.1 1352.6 %reduce-scatter.7.cloned.1.call-start = ((), (), s32[]{:S(2)}) async-start(), calls=%async_computation.11 | async-start | bytes 5308416 | tf_op jit(solution)/shard_map/reduce_scatter | solution.py:303
  232.8 88.4 %copy-start.32 = (f32[256,32]{0,1:T(8,128)S(1)}, f32[256,32]{0,1:T(8,128)}, u32[]{:S(2)}) copy-start(f32[256,32]{0,1:T(8,128)} %copy-done.31) | copy-start | bytes 98308
  232.8 88.4 %copy-start.35 = (f32[256,32]{0,1:T(8,128)S(1)}, f32[256,32]{0,1:T(8,128)}, u32[]{:S(2)}) copy-start(f32[256,32]{0,1:T(8,128)} %copy-done.34) | copy-start | bytes 98308
  541.5 9.1 copy-start.8
  541.5 9.1 copy-start.11
  550.6 65.2 %copy-start.5 = (bf16[256,2304]{1,0:T(8,128)(2,1)S(1)}, bf16[256,2304]{1,0:T(8,128)(2,1)}, u32[]{:S(2)}) copy-start(bf16[256,2304]{1,0:T(8,128)(2,1)} %param.16) | copy-start | bytes 3538948
  615.8 7.1 copy-start.40
  622.4 734.8 %copy-start.2 = (f32[256,2304]{1,0:T(8,128)}, f32[256,2304]{1,0:T(8,128)S(1)}, u32[]{:S(2)}) copy-start(f32[256,2304]{1,0:T(8,128)S(1)} %get-tuple-element.490) | copy-start | bytes 7077892
  623.2 453.0 %copy-start.14 = (bf16[256,2304]{1,0:T(8,128)(2,1)}, bf16[256,2304]{1,0:T(8,128)(2,1)S(1)}, u32[]{:S(2)}) copy-start(bf16[256,2304]{1,0:T(8,128)(2,1)S(1)} %multiply_convert_fusion.4) | copy-start | bytes 3538948
  1342.2 14.9 copy-start.43
  1342.2 15.0 copy-start.17
  1357.8 7.9 copy-start
  1372.4 5.0 copy-start.12
  1383.8 4.0 slice-start.1
  1400.0 4.0 slice-start.1
  1416.2 4.0 slice-start.1
  1432.4 4.0 slice-start.1
  1448.7 4.0 slice-start.1
  1464.9 3.7 slice-start
  1464.9 4.0 slice-start.1
  1481.2 4.0 slice-start.1
  1497.4 4.0 slice-start.1
  1513.6 4.0 slice-start.1
  1529.9 106.2 %reduce-scatter.9.cloned.1.call-start = ((), (), s32[]{:S(2)}) async-start(), calls=%async_computation.13 | async-start | bytes 5308416 | tf_op jit(solution)/shard_map/reduce_scatter | solution.py:309
  1536.5 153.9 %all-gather.24.cloned.1.call-start = ((), (), s32[]{:S(2)}) async-start(), calls=%async_computation.12 | async-start | bytes 5308416 | tf_op jit(solution)/shard_map/all_gather | solution.py:317
  1580.7 161.8 %all-gather.26.cloned.1.call-start = ((), (), s32[]{:S(2)}) async-start(), calls=%async_computation.14 | async-start | bytes 5308416 | tf_op jit(solution)/shard_map/all_gather | solution.py:320
  1636.2 1588.7 %all-reduce.13.cloned.1.call-start = ((), (), s32[]{:S(2)}) async-start(), calls=%async_computation.17 | async-start | bytes 127401984
  1636.2 56.4 %copy-start.13 = (f32[256,2304]{0,1:T(8,128)S(1)}, f32[256,2304]{0,1:T(8,128)}, u32[]{:S(2)}) copy-start(f32[256,2304]{0,1:T(8,128)} %get-tuple-element.341) | copy-start | bytes 7077892
  1636.2 56.4 %copy-start.33 = (f32[256,32]{0,1:T(8,128)S(1)}, f32[256,32]{0,1:T(8,128)}, u32[]{:S(2)}) copy-start(f32[256,32]{0,1:T(8,128)} %copy-done.31) | copy-start | bytes 98308
  1636.2 56.4 %copy-start.36 = (f32[256,32]{0,1:T(8,128)S(1)}, f32[256,32]{0,1:T(8,128)}, u32[]{:S(2)}) copy-start(f32[256,32]{0,1:T(8,128)} %copy-done.34) | copy-start | bytes 98308
  1693.6 51.2 %copy-start.21 = (bf16[256,36,64]{0,2,1:T(8,128)(2,1)}, bf16[256,36,64]{0,2,1:T(8,128)(2,1)S(1)}, u32[]{:S(2)}) copy-start(bf16[256,36,64]{0,2,1:T(8,128)(2,1)S(1)} %pad_maximum_fusion.4) | copy-start | bytes 3538948
  1694.8 50.0 %copy-start.6 = (bf16[256,2304]{1,0:T(8,128)(2,1)S(1)}, bf16[256,2304]{1,0:T(8,128)(2,1)}, u32[]{:S(2)}) copy-start(bf16[256,2304]{1,0:T(8,128)(2,1)} %param.16) | copy-start | bytes 3538948
  1694.8 50.0 %copy-start.29 = (f32[2304]{0:T(1024)S(1)}, f32[2304]{0:T(1024)}, u32[]{:S(2)}) copy-start(f32[2304]{0:T(1024)} %copy-done.28) | copy-start | bytes 27652
  1694.8 50.0 %copy-start.38 = (f32[256]{0:T(256)S(1)}, f32[256]{0:T(256)}, u32[]{:S(2)}) copy-start(f32[256]{0:T(256)} %copy-done.37) | copy-start | bytes 3076
  1744.8 24.6 copy-start.19
  1769.4 2322.6 %reduce-scatter.13.cloned.1.call-start = ((), (), s32[]{:S(2)}) async-start(), calls=%async_computation.16 | async-start | bytes 109486080 | tf_op jit(solution)/shard_map/reduce_scatter | solution.py:71
  1810.5 2508.1 %reduce-scatter.11.cloned.1.call-start = ((), (), s32[]{:S(2)}) async-start(), calls=%async_computation.15 | async-start | bytes 21897216 | tf_op jit(solution)/shard_map/reduce_scatter | solution.py:367
  2936.0 7.6 copy-start.3
  2937.8 135.8 %collective-permute-start = (f32[192,2304]{1,0:T(8,128)}, f32[192,2304]{1,0:T(8,128)}, u32[]{:S(2)}, u32[]{:S(2)}) collective-permute-start(f32[192,2304]{1,0:T(8,128)} %fusion), channel_id=1, source_target_pairs={{0,1},{1,2},{2,3},{3,4},{4,5},{5,6},{6,7},{7,8},{8,9},{9,10},{10,1... | collective-permute-start | bytes 5308424
  2942.2 130.2 %collective-permute-start.1 = (f32[180,2304]{1,0:T(8,128)S(1)}, f32[180,2304]{1,0:T(8,128)S(1)}, u32[]{:S(2)}, u32[]{:S(2)}) collective-permute-start(f32[180,2304]{1,0:T(8,128)S(1)} %slice.97), channel_id=1, source_target_pairs={{0,2},{1,3},{2,4},{3,5},{4,6},{5,7},{6,8},{7,9},{8,10},{9,11},{10,... | collective-permute-start | bytes 4976648
  3095.0 9.3 copy-start.23
  3095.0 17.5 slice-start.2
  3095.0 17.5 slice-start.3
  3104.3 8.2 copy-start.7
  3104.3 8.2 copy-start.20
  3104.3 8.2 copy-start.30
  3104.3 8.2 copy-start.39
  3104.4 8.2 slice-start.4
  (25 other events, 61.7 us)
Sparse Core Ops, SparseCore 0:
  9.7 103.3 all-gather.9
  114.7 98.8 all-gather.11
  215.3 98.8 all-gather.13
  317.2 194.1 all-reduce.14
  512.9 101.1 all-gather.15
  615.6 229.5 all-gather.17
  846.8 229.3 all-gather.19
  1077.8 229.3 all-gather.21
  1530.0 50.5 reduce-scatter.6
  1582.8 53.3 reduce-scatter.8
  1637.8 52.5 all-gather.23
  1691.9 50.5 all-gather.25
  1769.5 1455.3 all-reduce.12
  3231.2 860.8 reduce-scatter.12
  4100.0 218.4 reduce-scatter.10
where the time goes:
time: 4340 us; the launch traced here: 4330 us
  waiting for transfers between devices  2550 us (59%)
  blocking collectives  1160 us (27%)
  matrix products  354 us (8%)
  local copies, waits for them, and re-layouts  196 us (5%)
    unnamed x3, blocking collectives  1160 us
    reduce_scatter x1, waiting for transfers between devices, weight_sums(): lax.psum_scatter(contract_rows(left, right), ('grp', 'tok', 'fs'), scatte...  864 us
    reduce_scatter x1, waiting for transfers between devices, local(): lax.psum_scatter(output_full, ('grp', 'tok', 'fs'), scatter_dimension=0,...  223 us
    all_gather x1, waiting for transfers between devices, local(): lax.all_gather(gate_weight, ('tok', 'fs'), axis=0, tiled=True)  222 us
    all_gather x1, waiting for transfers between devices, local(): piece = lax.all_gather(down_weight, ('tok', 'fs'), axis=0, tiled=True)  215 us
    all_gather x1, waiting for transfers between devices, local(): lax.all_gather(up_weight, ('tok', 'fs'), axis=0, tiled=True)  214 us
    psum x1, waiting for transfers between devices, spread(): return lax.psum(block, axis)  189 us
    unnamed x18, waiting for transfers between devices  178 us
  transfers between devices with their start and end apart: 17, of which 15 were waited for; matrix products, arithmetic and copies ran while one was open for 33% of the time, Pallas kernels for 0%

commit v1 on v0

--- a/solution.py
+++ b/solution.py
@@ -1,8 +1,11 @@
+import functools
 import math
 
 import jax
 import jax.numpy as jnp
 from jax import lax
+from jax.experimental import pallas as pl
+from jax.experimental.pallas import tpu as pltpu
 from jax.sharding import PartitionSpec as P
 
 HEAD_DIM = 64
@@ -15,6 +18,638 @@
 RESIDUAL = 1.4 / math.sqrt(40.0)
 NEGATIVE = -1e30
 GROUP_HEADS = 4
+
+ALL = ("grp", "tok", "fs")
+LAYER = ("grp", "fs")
+PIECE = 64
+TILE = 256
+PAIR = 2 * HEAD_DIM
+SLAB = 3 * PAIR
+BF = jnp.bfloat16
+F32 = jnp.float32
+
+
+def turn(field):
+    lane = lax.broadcasted_iota(jnp.int32, field.shape, 1)
+    return jnp.where(
+        lane % HEAD_DIM < HEAD_DIM // 2,
+        pltpu.roll(field, PAIR - HEAD_DIM // 2, 1),
+        pltpu.roll(field, HEAD_DIM // 2, 1),
+    )
+
+
+def table_row(piece):
+    prompt_pieces = PROMPT // PIECE
+    cont_pieces = CONT // PIECE
+    return jnp.where(
+        piece < prompt_pieces,
+        piece,
+        prompt_pieces + lax.rem(jnp.maximum(piece - prompt_pieces, 0), cont_pieces),
+    )
+
+
+def head_tiles(index_ref, total, run_tile):
+    pair = pl.program_id(0)
+    side = index_ref[total // PIECE]
+    own = pair < 2
+    prompt_tiles = PROMPT // TILE
+    for tile in range(prompt_tiles):
+        mine = side == (0 if tile % 4 in (0, 3) else 1)
+        for head in range(2):
+            keep = own if head else jnp.logical_or(own, mine)
+
+            @pl.when(keep)
+            def _(tile=tile, head=head):
+                run_tile(tile * TILE, tile * TILE, head)
+
+    later = (total - PROMPT) // TILE
+
+    def body(step, carry):
+        mine = (step * 2 >= later).astype(jnp.int32) == side
+        for head in range(2):
+            keep = own if head else jnp.logical_or(own, mine)
+
+            @pl.when(keep)
+            def _(head=head):
+                run_tile(pl.multiple_of(PROMPT + step * TILE, TILE), PROMPT, head)
+
+        return carry
+
+    lax.fori_loop(0, later, body, 0)
+
+
+def lanes_of(head, shape):
+    lane = lax.broadcasted_iota(jnp.int32, shape, 1)
+    return lane < HEAD_DIM if head == 0 else lane >= HEAD_DIM
+
+
+def nt_dot(left, right):
+    return lax.dot_general(left, right, (((1,), (1,)), ((), ())), preferred_element_type=F32)
+
+
+def tn_dot(left, right):
+    return lax.dot_general(left, right, (((0,), (0,)), ((), ())), preferred_element_type=F32)
+
+
+def nn_dot(left, right):
+    return lax.dot_general(left, right, (((1,), (0,)), ((), ())), preferred_element_type=F32)
+
+
+def attend_kernel(index_ref, raw_ref, cos_ref, sin_ref, out_ref, kept_ref, mixed):
+    total = out_ref.shape[0]
+    pieces = total // PIECE
+    pair = pl.program_id(0)
+
+    def rope(field, row):
+        cosine = cos_ref[pl.ds(row, PIECE), :]
+        sine = sin_ref[pl.ds(row, PIECE), :]
+        return field * cosine + turn(field) * sine
+
+    @pl.when(pair < 2)
+    def _():
+        def body(piece, carry):
+            source = pl.multiple_of(index_ref[piece], PIECE)
+            row = pl.multiple_of(table_row(piece) * PIECE, PIECE)
+            target = pl.ds(pl.multiple_of(piece * PIECE, PIECE), PIECE)
+            query = rope(raw_ref[pl.ds(source, PIECE), 0:PAIR], row)
+            key = rope(raw_ref[pl.ds(source, PIECE), PAIR : 2 * PAIR], row)
+            value = raw_ref[pl.ds(source, PIECE), 2 * PAIR : 3 * PAIR]
+            kept_ref[0, target, 0:PAIR] = query.astype(BF)
+            kept_ref[0, target, PAIR : 2 * PAIR] = key.astype(BF)
+            kept_ref[0, target, 2 * PAIR : 3 * PAIR] = value.astype(BF)
+            return carry
+
+        lax.fori_loop(0, pieces, body, 0)
+
+    @pl.when(pair == 2)
+    def _():
+        def body(piece, carry):
+            source = pl.multiple_of(index_ref[piece], PIECE)
+            row = pl.multiple_of(table_row(piece) * PIECE, PIECE)
+            target = pl.ds(pl.multiple_of(piece * PIECE, PIECE), PIECE)
+            both = rope(raw_ref[pl.ds(source, PIECE), 0:PAIR], row)
+            value = raw_ref[pl.ds(source, PIECE), PAIR : 2 * PAIR]
+            low = lanes_of(0, both.shape)
+            kept_ref[0, target, 0:PAIR] = jnp.where(low, both, 0.0).astype(BF)
+            kept_ref[0, target, PAIR : 2 * PAIR] = jnp.where(
+                low, pltpu.roll(both, HEAD_DIM, 1), 0.0
+            ).astype(BF)
+            kept_ref[0, target, 2 * PAIR : 3 * PAIR] = jnp.where(low, value, 0.0).astype(BF)
+            return carry
+
+        lax.fori_loop(0, pieces, body, 0)
+
+    mixed[...] = jnp.zeros_like(mixed)
+    scale = 1.0 / math.sqrt(HEAD_DIM)
+
+    def run_tile(start, prefix, head):
+        rows = pl.ds(start, TILE)
+        query = kept_ref[0, rows, 0:PAIR]
+        mask = lanes_of(head, query.shape)
+        query = jnp.where(mask, query.astype(F32) * scale, 0.0).astype(BF)
+        seen = lax.broadcasted_iota(jnp.int32, (TILE, TILE), 1) <= lax.broadcasted_iota(
+            jnp.int32, (TILE, TILE), 0
+        )
+        near = jnp.where(seen, nt_dot(query, kept_ref[0, rows, PAIR : 2 * PAIR]), NEGATIVE)
+        peak = jnp.max(near, axis=1, keepdims=True)
+        if prefix:
+            far = nt_dot(query, kept_ref[0, 0:prefix, PAIR : 2 * PAIR])
+            peak = jnp.maximum(peak, jnp.max(far, axis=1, keepdims=True))
+        near = jnp.exp(near - peak)
+        count = jnp.sum(near, axis=1, keepdims=True)
+        out = nn_dot(near.astype(BF), kept_ref[0, rows, 2 * PAIR : 3 * PAIR])
+        if prefix:
+            far = jnp.exp(far - peak)
+            count = count + jnp.sum(far, axis=1, keepdims=True)
+            out = out + nn_dot(far.astype(BF), kept_ref[0, 0:prefix, 2 * PAIR : 3 * PAIR])
+        mixed[rows, :] = jnp.where(mask, out / count, mixed[rows, :])
+
+    head_tiles(index_ref, total, run_tile)
+
+    def back(piece, carry):
+        source = pl.multiple_of(index_ref[piece], PIECE)
+        target = pl.ds(pl.multiple_of(piece * PIECE, PIECE), PIECE)
+        out_ref[pl.ds(source, PIECE), :] = mixed[target, :].astype(BF)
+        return carry
+
+    lax.fori_loop(0, pieces, back, 0)
+
+
+def attend(index, raw, cosine, sine):
+    total = raw.shape[0]
+    return pl.pallas_call(
+        attend_kernel,
+        grid_spec=pltpu.PrefetchScalarGridSpec(
+            num_scalar_prefetch=1,
+            grid=(3,),
+            in_specs=[
+                pl.BlockSpec((total, SLAB), lambda j, index: (0, j)),
+                pl.BlockSpec(cosine.shape, lambda j, index: (0, 0)),
+                pl.BlockSpec(sine.shape, lambda j, index: (0, 0)),
+            ],
+            out_specs=[
+                pl.BlockSpec((total, PAIR), lambda j, index: (0, j)),
+                pl.BlockSpec((1, total, SLAB), lambda j, index: (j, 0, 0)),
+            ],
+            scratch_shapes=[pltpu.VMEM((total, PAIR), F32)],
+        ),
+        out_shape=[
+            jax.ShapeDtypeStruct((total, 3 * PAIR), BF),
+            jax.ShapeDtypeStruct((3, total, SLAB), BF),
+        ],
+        compiler_params=pltpu.CompilerParams(vmem_limit_bytes=40 << 20),
+        cost_estimate=pl.CostEstimate(
+            flops=10 * 2 * 7680 * 256 * 128, bytes_accessed=20 << 20, transcendentals=9 << 20
+        ),
+        name="attend",
+    )(index, raw, cosine, sine)
+
+
+def attend_back_kernel(
+    index_ref, kept_ref, outer_ref, cos_ref, sin_ref, grad_ref, outer, grad_q, grad_k, grad_v
+):
+    total = outer.shape[0]
+    pieces = total // PIECE
+    pair = pl.program_id(0)
+
+    def sort(piece, carry):
+        source = pl.multiple_of(index_ref[piece], PIECE)
+        target = pl.ds(pl.multiple_of(piece * PIECE, PIECE), PIECE)
+        outer[target, :] = outer_ref[pl.ds(source, PIECE), :]
+        return carry
+
+    lax.fori_loop(0, pieces, sort, 0)
+    grad_q[...] = jnp.zeros_like(grad_q)
+    grad_k[...] = jnp.zeros_like(grad_k)
+    grad_v[...] = jnp.zeros_like(grad_v)
+    scale = 1.0 / math.sqrt(HEAD_DIM)
+
+    def run_tile(start, prefix, head):
+        rows = pl.ds(start, TILE)
+        query = kept_ref[0, rows, 0:PAIR]
+        mask = lanes_of(head, query.shape)
+        query = jnp.where(mask, query.astype(F32) * scale, 0.0).astype(BF)
+        away = jnp.where(mask, outer[rows, :].astype(F32), 0.0).astype(BF)
+        seen = lax.broadcasted_iota(jnp.int32, (TILE, TILE), 0) <= lax.broadcasted_iota(
+            jnp.int32, (TILE, TILE), 1
+        )
+        near_key = kept_ref[0, rows, PAIR : 2 * PAIR]
+        near = jnp.where(seen, nt_dot(near_key, query), NEGATIVE)
+        peak = jnp.max(near, axis=0, keepdims=True)
+        if prefix:
+            far_key = kept_ref[0, 0:prefix, PAIR : 2 * PAIR]
+            far = nt_dot(far_key, query)
+            peak = jnp.maximum(peak, jnp.max(far, axis=0, keepdims=True))
+        near = jnp.exp(near - peak)
+        count = jnp.sum(near, axis=0, keepdims=True)
+        if prefix:
+            far = jnp.exp(far - peak)
+            count = count + jnp.sum(far, axis=0, keepdims=True)
+        inverse = 1.0 / count
+        near = near * inverse
+        near_pull = nt_dot(kept_ref[0, rows, 2 * PAIR : 3 * PAIR], away)
+        delta = jnp.sum(near * near_pull, axis=0, keepdims=True)
+        if prefix:
+            far = far * inverse
+            far_pull = nt_dot(kept_ref[0, 0:prefix, 2 * PAIR : 3 * PAIR], away)
+            delta = delta + jnp.sum(far * far_pull, axis=0, keepdims=True)
+        grad_v[rows, :] += nn_dot(near.astype(BF), away)
+        near = (near * (near_pull - delta)).astype(BF)
+        grad_k[rows, :] += nn_dot(near, query)
+        part = tn_dot(near, near_key)
+        if prefix:
+            grad_v[0:prefix, :] += nn_dot(far.astype(BF), away)
+            far = (far * (far_pull - delta)).astype(BF)
+            grad_k[0:prefix, :] += nn_dot(far, query)
+            part = part + tn_dot(far, far_key)
+        grad_q[rows, :] = jnp.where(mask, part * scale, grad_q[rows, :])
+
+    head_tiles(index_ref, total, run_tile)
+
+    def unrope(field, row):
+        cosine = cos_ref[pl.ds(row, PIECE), :]
+        sine = sin_ref[pl.ds(row, PIECE), :]
+        return field * cosine - turn(field) * sine
+
+    @pl.when(pair < 2)
+    def _():
+        def back(piece, carry):
+            source = pl.ds(pl.multiple_of(index_ref[piece], PIECE), PIECE)
+            row = pl.multiple_of(table_row(piece) * PIECE, PIECE)
+            here = pl.ds(pl.multiple_of(piece * PIECE, PIECE), PIECE)
+            grad_ref[source, 0:PAIR] = unrope(grad_q[here, :], row).astype(BF)
+            grad_ref[source, PAIR : 2 * PAIR] = unrope(grad_k[here, :], row).astype(BF)
+            grad_ref[source, 2 * PAIR : 3 * PAIR] = grad_v[here, :].astype(BF)
+            return carry
+
+        lax.fori_loop(0, pieces, back, 0)
+
+    @pl.when(pair == 2)
+    def _():
+        def back(piece, carry):
+            source = pl.ds(pl.multiple_of(index_ref[piece], PIECE), PIECE)
+            row = pl.multiple_of(table_row(piece) * PIECE, PIECE)
+            here = pl.ds(pl.multiple_of(piece * PIECE, PIECE), PIECE)
+            low = lanes_of(0, (PIECE, PAIR))
+            both = jnp.where(low, grad_q[here, :], pltpu.roll(grad_k[here, :], HEAD_DIM, 1))
+            grad_ref[source, 0:PAIR] = unrope(both, row).astype(BF)
+            grad_ref[source, PAIR : 2 * PAIR] = grad_v[here, :].astype(BF)
+            grad_ref[source, 2 * PAIR : 3 * PAIR] = jnp.zeros((PIECE, PAIR), BF)
+            return carry
+
+        lax.fori_loop(0, pieces, back, 0)
+
+
+def attend_back(index, kept, outer, cosine, sine, columns):
+    total = outer.shape[0]
+    return pl.pallas_call(
+        attend_back_kernel,
+        grid_spec=pltpu.PrefetchScalarGridSpec(
+            num_scalar_prefetch=1,
+            grid=(3,),
+            in_specs=[
+                pl.BlockSpec((1, total, SLAB), lambda j, index: (j, 0, 0)),
+                pl.BlockSpec((total, PAIR), lambda j, index: (0, j)),
+                pl.BlockSpec(cosine.shape, lambda j, index: (0, 0)),
+                pl.BlockSpec(sine.shape, lambda j, index: (0, 0)),
+            ],
+            out_specs=pl.BlockSpec((total, SLAB), lambda j, index: (0, j)),
+            scratch_shapes=[
+                pltpu.VMEM((total, PAIR), BF),
+                pltpu.VMEM((total, PAIR), F32),
+                pltpu.VMEM((total, PAIR), F32),
+                pltpu.VMEM((total, PAIR), F32),
+            ],
+        ),
+        out_shape=jax.ShapeDtypeStruct((total, columns), BF),
+        compiler_params=pltpu.CompilerParams(vmem_limit_bytes=48 << 20),
+        cost_estimate=pl.CostEstimate(
+            flops=25 * 2 * 7680 * 256 * 128, bytes_accessed=20 << 20, transcendentals=9 << 20
+        ),
+        name="attend_back",
+    )(index, kept, outer, cosine, sine)
+
+
+def make_layered(mesh):
+    n_grp, n_tok, n_fs = (mesh.shape[axis] for axis in ALL)
+
+    def device(grp, tok, fs):
+        return (grp * n_tok + tok) * n_fs + fs
+
+    def permutation(move):
+        return [
+            (device(g, t, f), device(*move(g, t, f)))
+            for g in range(n_grp)
+            for t in range(n_tok)
+            for f in range(n_fs)
+        ]
+
+    def send(array, move):
+        return lax.ppermute(array, ALL, permutation(move))
+
+    def cross(step):
+        return lambda g, t, f: (g ^ step, t, f)
+
+    def sibling(g, t, f):
+        return (g, t, 1 - f)
+
+    def local(
+        hidden_in,
+        cotangent,
+        block_start,
+        query_weight,
+        key_weight,
+        value_weight,
+        output_weight,
+        gate_weight,
+        up_weight,
+        down_weight,
+        first_gain,
+        second_gain,
+    ):
+        rows, width = hidden_in.shape
+        ff_width = gate_weight.shape[1]
+        g, t, f = (lax.axis_index(axis) for axis in ALL)
+        even = f == 0
+        ranks = n_grp * n_fs
+        total = rows * ranks
+        quarter = rows // n_grp
+
+
+        def shuffle_in(array):
+            parts = array.reshape(n_grp, quarter, width)
+            result = jnp.zeros_like(parts)
+            for turn_by in range(n_grp):
+                piece = lax.dynamic_index_in_dim(parts, g ^ t ^ turn_by, 0, keepdims=True)
+                piece = send(piece, lambda g, t, f: (g ^ t ^ turn_by, g, f))
+                result = lax.dynamic_update_slice_in_dim(result, piece, g ^ t ^ turn_by, 0)
+            return result.reshape(rows, width)
+
+        def shuffle_out(array):
+            parts = array.reshape(n_tok, quarter, width)
+            result = jnp.zeros_like(parts)
+            for turn_by in range(n_grp):
+                piece = lax.dynamic_index_in_dim(parts, g ^ t ^ turn_by, 0, keepdims=True)
+                piece = send(piece, lambda g, t, f: (t, g ^ t ^ turn_by, f))
+                result = lax.dynamic_update_slice_in_dim(result, piece, g ^ t ^ turn_by, 0)
+            return result.reshape(rows, width)
+
+
+        def layer_gather(array):
+            half = array.shape[0] // 2
+            by_x = send(array, cross(1))
+            by_y = send(array, cross(2))
+            by_xy = jnp.concatenate(
+                [send(by_x[:half], cross(2)), send(by_y[half:], cross(1))], axis=0
+            )
+            mine = [array, by_x, by_y, by_xy]
+            return jnp.concatenate(mine + [send(part, sibling) for part in mine], axis=0)
+
+        def layer_sum(array):
+            half = array.shape[0] // 2
+            both = array[:half].astype(F32) + send(array[half:], sibling).astype(F32)
+            parts = both.astype(BF).reshape(n_grp, rows, array.shape[1])
+            return both[:rows] + sum(
+                send(parts[step], cross(step)).astype(F32) for step in range(1, n_grp)
+            )
+
+        xs = shuffle_in(hidden_in)
+        gain_one = lax.all_gather(first_gain, ("tok", "fs"), axis=0, tiled=True).astype(F32)
+        gain_two = lax.all_gather(second_gain, ("tok", "fs"), axis=0, tiled=True).astype(F32)
+
+
+        head_span = width // n_grp
+        own_span = 4 * HEAD_DIM
+
+        def rank_columns(side):
+            picked = [
+                lax.dynamic_slice_in_dim(weight, g * head_span, head_span, 1)
+                for weight in (query_weight, key_weight, value_weight)
+            ]
+            first = side * (own_span + HEAD_DIM)
+            spans = [(first, PAIR), (first + PAIR, PAIR), (own_span, HEAD_DIM)]
+            return jnp.concatenate(
+                [weight[:, at : at + size] for at, size in spans for weight in picked], axis=1
+            )
+
+        def pair_rows(zero_block, one_block):
+            mine = jnp.where(even, zero_block, one_block)
+            other = send(jnp.where(even, one_block, zero_block), sibling)
+            return jnp.concatenate(
+                [jnp.where(even, mine, other), jnp.where(even, other, mine)], axis=0
+            )
+
+        qkv_weight = lax.all_gather(
+            pair_rows(rank_columns(0), rank_columns(1)), "tok", axis=0, tiled=True
+        )
+        out_rows = output_weight.shape[0] // n_grp
+        out_weight = lax.all_gather(
+            lax.dynamic_slice_in_dim(output_weight, g * out_rows, out_rows, 0),
+            "tok",
+            axis=0,
+            tiled=True,
+        )
+        out_weight = lax.all_to_all(out_weight, "grp", 0, 0, tiled=True)
+        half_head = HEAD_DIM // 2
+        swapped = send(
+            jnp.where(even, out_weight[own_span:], out_weight[:half_head]), sibling
+        )
+        out_weight = jnp.concatenate(
+            [
+                jnp.where(even, out_weight[:own_span], out_weight[half_head:]),
+                jnp.where(even, out_weight[own_span:], swapped),
+                jnp.where(even, swapped, out_weight[:half_head]),
+                jnp.zeros((HEAD_DIM, width), BF),
+            ],
+            axis=0,
+        )
+
+        ff_piece = ff_width // (ranks * n_tok)
+
+        def ff_columns(weight, side):
+            return jnp.concatenate(
+                [
+                    lax.dynamic_slice_in_dim(
+                        weight, (step * n_fs + side) * n_grp * ff_piece + g * ff_piece, ff_piece, 1
+                    )
+                    for step in range(n_tok)
+                ],
+                axis=1,
+            )
+
+        def ff_weight(weight):
+            return lax.all_gather(
+                pair_rows(ff_columns(weight, 0), ff_columns(weight, 1)), "tok", axis=0, tiled=True
+            )
+
+        gate_w = ff_weight(gate_weight)
+        up_w = ff_weight(up_weight)
+        down_w = lax.all_gather(
+            lax.dynamic_slice_in_dim(down_weight, g * ff_piece, ff_piece, 0),
+            "tok",
+            axis=0,
+            tiled=True,
+        )
+
+
+        starts = lax.dynamic_index_in_dim(
+            lax.all_gather(block_start, "grp", axis=0, tiled=True), t, 0, keepdims=False
+        )
+        number = jnp.arange(total // BLOCK, dtype=jnp.int32)
+        prompt_blocks = PROMPT // BLOCK
+        cont_blocks = CONT // BLOCK
+        place = jnp.where(
+            number < prompt_blocks,
+            starts // BLOCK,
+            prompt_blocks
+            + (number - prompt_blocks) // cont_blocks * cont_blocks
+            + (starts - PROMPT) // BLOCK,
+        )
+        order = jnp.sum(
+            jnp.where(place[None, :] == number[:, None], number[None, :], 0), axis=1
+        )
+        pieces = (
+            order[:, None] * (BLOCK // PIECE) + jnp.arange(BLOCK // PIECE, dtype=jnp.int32)
+        ).reshape(-1)
+        from_t = pieces // ranks
+        from_f = pieces // n_grp % n_fs
+        from_g = pieces % n_grp
+        index = jnp.concatenate(
+            [
+                (((from_f ^ f) * n_grp + (from_g ^ g)) * n_tok + from_t) * PIECE,
+                f[None].astype(jnp.int32),
+            ]
+        ).astype(jnp.int32)
+        lane = jnp.arange(PAIR, dtype=jnp.int32)
+        half_head_lane = lane % (HEAD_DIM // 2)
+        freq = 10000.0 ** (-(half_head_lane.astype(F32) * 2.0) / HEAD_DIM)
+        angle = jnp.arange(PROMPT + CONT, dtype=F32)[:, None] * freq[None, :]
+        cosine = jnp.cos(angle)
+        sine = jnp.where(lane[None, :] % HEAD_DIM < HEAD_DIM // 2, -jnp.sin(angle), jnp.sin(angle))
+
+
+        hidden = xs.astype(F32)
+        scale_one = lax.rsqrt(jnp.mean(hidden * hidden, axis=1, keepdims=True) + EPS)
+        normed_one = hidden * scale_one
+        h_one = layer_gather((normed_one * gain_one[None, :]).astype(BF))
+        raw = jnp.dot(h_one, qkv_weight, preferred_element_type=F32)
+        attn_out, kept = attend(index, raw, cosine, sine)
+        branch = layer_sum(jnp.dot(attn_out, out_weight, preferred_element_type=F32).astype(BF))
+        second_in = hidden + RESIDUAL * branch
+        scale_two = lax.rsqrt(jnp.mean(second_in * second_in, axis=1, keepdims=True) + EPS)
+        normed_two = second_in * scale_two
+        h_two = layer_gather((normed_two * gain_two[None, :]).astype(BF))
+        gate = jnp.dot(h_two, gate_w, preferred_element_type=F32)
+        up_val = jnp.dot(h_two, up_w, preferred_element_type=F32)
+        sigma = jax.nn.sigmoid(gate)
+        silu = gate * sigma
+        act = (silu * up_val).astype(BF)
+        feed = layer_sum(jnp.dot(act, down_w, preferred_element_type=F32).astype(BF))
+        layer_output = shuffle_out((second_in + RESIDUAL * feed).astype(BF))
+
+
+        grad_out = shuffle_in(cotangent).astype(F32)
+        grad_m = layer_gather((RESIDUAL * grad_out).astype(BF))
+        grad_act = nt_dot(grad_m, down_w)
+        down_grad = lax.psum_scatter(
+            tn_dot(act, grad_m).astype(BF).reshape(n_tok, ff_piece, width),
+            "tok",
+            scatter_dimension=0,
+            tiled=True,
+        )[0]
+        down_grad = send(
+            down_grad, lambda g, t, f: (t, (n_grp * f + g) // n_fs, (n_grp * f + g) % n_fs)
+        ).astype(F32)
+        grad_gate = (grad_act * up_val * (sigma * (1.0 + gate * (1.0 - sigma)))).astype(BF)
+        grad_up = (grad_act * silu).astype(BF)
+
+        def to_rows(grad):
+            columns = grad.shape[1]
+            grad = grad.astype(BF).reshape(n_grp, n_tok, width // (n_grp * n_tok), columns)
+            grad = grad.transpose(1, 0, 2, 3).reshape(n_tok, width // n_tok, columns)
+            grad = lax.psum_scatter(grad, "tok", scatter_dimension=0, tiled=True)
+            grad = grad.reshape(ranks, width // (ranks * n_tok), columns)
+            return lax.all_to_all(grad, LAYER, 0, 0, tiled=True)
+
+        def ff_grad(grad):
+            got = to_rows(grad).reshape(n_grp, n_fs, -1, n_tok, ff_piece)
+            return got.transpose(2, 3, 1, 0, 4).reshape(-1, ff_width).astype(F32)
+
+        gate_grad = ff_grad(tn_dot(h_two, grad_gate))
+        up_grad = ff_grad(tn_dot(h_two, grad_up))
+        grad_h2 = layer_sum((nt_dot(grad_gate, gate_w) + nt_dot(grad_up, up_w)).astype(BF))
+        gain_two_sum = jnp.sum(grad_h2 * normed_two, axis=0)
+        pulled = grad_h2 * gain_two[None, :]
+        grad_second = (
+            grad_out
+            + scale_two * pulled
+            - scale_two**3 * second_in * jnp.mean(pulled * second_in, axis=1, keepdims=True)
+        )
+        grad_z = layer_gather((RESIDUAL * grad_second).astype(BF))
+        grad_attn = nt_dot(grad_z, out_weight).astype(BF)
+        out_full = tn_dot(attn_out, grad_z)
+        shared = out_full[own_span : own_span + HEAD_DIM]
+        got = send(
+            jnp.where(even, shared[half_head:], shared[:half_head]).astype(BF), sibling
+        ).astype(F32)
+        kept_half = jnp.where(even, shared[:half_head], shared[half_head:]) + got
+        out_full = jnp.where(
+            even,
+            jnp.concatenate([out_full[:own_span], kept_half], axis=0),
+            jnp.concatenate([kept_half, out_full[:own_span]], axis=0),
+        )
+        output_grad = lax.psum_scatter(
+            out_full.astype(BF).reshape(n_tok, -1, width), "tok", scatter_dimension=0, tiled=True
+        )[0]
+        output_grad = send(
+            output_grad, lambda g, t, f: (g, (n_tok * f + t) // n_fs, (n_tok * f + t) % n_fs)
+        ).astype(F32)
+
+        grads = attend_back(index, kept, grad_attn, cosine, sine, qkv_weight.shape[1])
+        grad_h1 = layer_sum(nt_dot(grads, qkv_weight).astype(BF))
+        gain_one_sum = jnp.sum(grad_h1 * normed_one, axis=0)
+        pulled = grad_h1 * gain_one[None, :]
+        input_grad = (
+            grad_second
+            + scale_one * pulled
+            - scale_one**3 * hidden * jnp.mean(pulled * hidden, axis=1, keepdims=True)
+        )
+        input_grad = shuffle_out(input_grad.astype(BF)).astype(F32)
+        got = to_rows(tn_dot(h_one, grads)).astype(F32)
+        own_rows = got.shape[1]
+        got = got.reshape(n_grp, n_fs, own_rows, got.shape[2])
+
+        def projection_grad(which):
+            def own(side):
+                return [
+                    got[:, side, :, SLAB * pair + PAIR * which : SLAB * pair + PAIR * (which + 1)]
+                    for pair in range(2)
+                ]
+
+            at = 2 * SLAB + HEAD_DIM * which
+            shared = got[:, 0, :, at : at + HEAD_DIM] + got[:, 1, :, at : at + HEAD_DIM]
+            whole = jnp.concatenate(own(0) + [shared] + own(1), axis=2)
+            return whole.transpose(1, 0, 2).reshape(own_rows, width)
+
+        gains = jnp.stack([gain_one_sum, gain_two_sum], axis=1).reshape(
+            n_grp * n_tok * n_fs, -1
+        )
+        gains = jnp.sum(lax.all_to_all(gains, ALL, 0, 0, tiled=True), axis=0).reshape(-1, 2)
+        return (
+            layer_output,
+            input_grad,
+            projection_grad(0),
+            projection_grad(1),
+            projection_grad(2),
+            output_grad,
+            gate_grad,
+            up_grad,
+            down_grad,
+            gains[:, 0],
+            gains[:, 1],
+        )
+
+    return local
 
 
 def spread(block, axis, source):
@@ -73,7 +708,7 @@
     )
 
 
-def local(
+def spread_local(
     hidden_in,
     cotangent,
     block_start,
@@ -384,8 +1019,9 @@
 
 
 def solution(mesh):
+    layered = mesh.shape["grp"] == mesh.shape["tok"] == 4 and mesh.shape["fs"] == 2
     return jax.shard_map(
-        local,
+        make_layered(mesh) if layered else spread_local,
         mesh=mesh,
         in_specs=(
             P(("grp", "tok", "fs"), None),

time: 4340 us -> 1250 us (0.29)
  waiting for transfers between devices: 2550 us -> 309 us
  blocking collectives: 1160 us -> 138 us
  starting transfers between devices: 6.56 us -> 188 us
  matrix products: 354 us -> 185 us
  Pallas kernels: 0 us -> 103 us
  other arithmetic: 41.7 us -> 92.3 us
    reduce_scatter x4 -> x5, waiting for transfers between devices: 1190 us -> 0.05 us  [the longest x3 0.02 us: to_rows(): grad = lax.psum_scatter(grad, 'tok', scatter_dimension=0, tiled=True)]
    unnamed x3 -> x1, blocking collectives: 1160 us -> 127 us
    all_gather x9 -> x5, waiting for transfers between devices: 1000 us -> 0.01 us  [the longest x2 0.01 us: ff_weight(): lax.all_gather(pair_rows(ff_columns(weight, 0), ff_columns(weight, 1)), '...]
    ppermute x0 -> x71, waiting for transfers between devices: none -> 287 us  [send(): return lax.ppermute(array, ALL, permutation(move))]
    psum x1 -> x0, waiting for transfers between devices: 189 us -> none  [spread(): return lax.psum(block, axis)]
    unnamed x18 -> x10, waiting for transfers between devices: 178 us -> 0.16 us
    dot_general x81 -> x15, matrix products: 354 us -> 185 us  [the longest x5 60 us: nt_dot(): lax.dot_general(left, right, (((1,), (1,)), ((), ())), preferred_element_...]
    ppermute x0 -> x71, starting transfers between devices: none -> 146 us  [send(): return lax.ppermute(array, ALL, permutation(move))]
  transfers between devices with their start and end apart: 17 -> 86, of which waited for: 15 -> 26; matrix products, arithmetic and copies ran while one was open for 33% -> 32% of each run, Pallas kernels for 0% -> 8%
where the time goes in v1:
time: 1250 us; the launch traced here: 1240 us
  waiting for transfers between devices  309 us (25%)
  local copies, waits for them, and re-layouts  204 us (16%)
  starting transfers between devices  188 us (15%)
  matrix products  185 us (15%)
  blocking collectives  138 us (11%)
  Pallas kernels  103 us (8%)
  other arithmetic  92.3 us (7%)
  between operations  16.5 us (1%)
    ppermute x71, waiting for transfers between devices, send(): return lax.ppermute(array, ALL, permutation(move))  287 us
    ppermute x71, starting transfers between devices, send(): return lax.ppermute(array, ALL, permutation(move))  146 us
    unnamed x1, blocking collectives  127 us
    pallas_call x1, Pallas kernels, attend_back(): pl.pallas_call(attend_back_kernel, grid_spec=pltpu.PrefetchScalarGridSpec...  62.2 us
    unnamed x143, local copies, waits for them, and re-layouts  60.2 us
    dot_general x5, matrix products, nt_dot(): lax.dot_general(left, right, (((1,), (1,)), ((), ())), preferred_element_...  60 us
    dot_general x5, matrix products, tn_dot(): lax.dot_general(left, right, (((0,), (0,)), ((), ())), preferred_element_...  54.5 us
    pallas_call x1, Pallas kernels, attend(): pl.pallas_call(attend_kernel, grid_spec=pltpu.PrefetchScalarGridSpec(num_...  40.4 us
  transfers between devices with their start and end apart: 86, of which 26 were waited for; matrix products, arithmetic and copies ran while one was open for 32% of the time, Pallas kernels for 8%

profile of v1, /device:TPU:1, one launch (start us, length us, event | category | flops | bytes accessed | tf_op | source)
XLA Modules:
  0.0 1235.3 jit_solution(2372184727585307767)
XLA Ops:
  27.2 5.1 collective-permute-start.3
  32.4 4.3 collective-permute-start.2
  48.2 4.2 constant_dynamic-slice_fusion.31
  52.4 11.6 all-gather
  65.7 126.8 %all-reduce.2 = (bf16[2304]{0:T(1024)(128)(2,1)S(1)}, bf16[2304]{0:T(1024)(128)(2,1)S(1)}) all-reduce(bf16[2304]{0:T(1024)(128)(2,1)S(1)} %dynamic-update-slice, bf16[2304]{0:T(1024)(128)(2,1)S(1)} %dynamic-update-slice.1), channel_id=1, replica_groups=mesh['grp'=4,'tok'=4,'fs'=2] {'tok','fs'}, use_global_device_ids=true, to_apply=%add | all-reduce | flops 4608 | bytes 18432
  209.4 4.1 collective-permute-start.4
  213.9 5.9 collective-permute-start.38
  226.4 11.8 collective-permute-done.5
  240.1 6.0 collective-permute-start.7
  246.1 11.0 collective-permute-done.4
  264.0 4.6 all-to-all-start
  272.3 12.3 collective-permute-start.9
  304.3 15.9 %fusion.47.raw_ref = f32[2048,960]{1,0:T(8,128)} fusion(bf16[2048,2304]{1,0:T(8,128)(2,1)} %constant_dynamic-update-slice_fusion, bf16[2304,960]{1,0:T(8,128)(2,1)} %all-gather.8.cloned.1.call-done), kind=kOutput, calls=%fused_computation.273 | convolution fusion | flops 9059696640 | bytes 21725184 | tf_op jit(solution)/shard_map/dot_general | solution.py:535
  320.3 40.4 %attend.1 = (bf16[2048,384]{1,0:T(8,128)(2,1)S(1)}, bf16[3,2048,384]{2,1,0:T(8,128)(2,1)S(1)}) custom-call(s32[33]{0:T(128)S(1)} %pad_add_fusion.index_ref, f32[2048,960]{1,0:T(8,128)} %fusion.47.raw_ref, f32[1280,128]{1,0:T(8,128)S(1)} %get-tuple-element.126.cos_ref, f32[1280,128]{1,0:T(8,128)S(1)} %get-tuple-element.125.sin_ref), custom_call_target="tpu_custom_call" | custom-call | flops 5033164800 | bytes 20971520 | tf_op jit(solution)/shard_map/attend/pallas_call | solution.py:180
  360.7 15.4 %convolution_convert_fusion.2 = bf16[2048,2304]{1,0:T(8,128)(2,1)S(1)} fusion(bf16[2048,384]{1,0:T(8,128)(2,1)S(1)} %get-tuple-element.13, bf16[32,2304]{1,0:T(8,128)(2,1)S(1)} %get-tuple-element.94, bf16[32,2304]{1,0:T(8,128)(2,1)S(1)} %get-tuple-element.93, bf16[256,2304]{1,0:T(8,128)(2,1)S(1)} %copy-done.28, bf16[384]{0:T(512)(128)(2,1)S(1)} %pad.35.clone), kind=kOutput, calls=%fused_computation.3 | convolution fusion | flops 3635675136 | bytes 12485376 | tf_op jit(solution)/shard_map/dot_general | solution.py:537
  392.9 23.8 %collective-permute-done.41 = bf16[256,2304]{1,0:T(8,128)(2,1)} collective-permute-done((bf16[256,2304]{1,0:T(8,128)(2,1)}, bf16[256,2304]{1,0:T(8,128)(2,1)}, u32[]{:S(2)}, u32[]{:S(2)}) %collective-permute-start.41) | collective-permute-done | bytes 1179680 | tf_op jit(solution)/shard_map/ppermute | solution.py:348
  425.3 6.8 collective-permute-done.43
  437.8 8.4 convert_add_fusion.3
  462.7 13.3 %collective-permute-done.15 = bf16[256,2304]{1,0:T(8,128)(2,1)} collective-permute-done((bf16[256,2304]{1,0:T(8,128)(2,1)}, bf16[256,2304]{1,0:T(8,128)(2,1)}, u32[]{:S(2)}, u32[]{:S(2)}) %collective-permute-start.15) | collective-permute-done | bytes 1179680 | tf_op jit(solution)/shard_map/ppermute | solution.py:348
  476.0 25.2 %collective-permute-done.17 = bf16[256,2304]{1,0:T(8,128)(2,1)} collective-permute-done((bf16[256,2304]{1,0:T(8,128)(2,1)}, bf16[256,2304]{1,0:T(8,128)(2,1)}, u32[]{:S(2)}, u32[]{:S(2)}) %collective-permute-start.17) | collective-permute-done | bytes 1179680 | tf_op jit(solution)/shard_map/ppermute | solution.py:348
  510.4 9.0 fusion.49
  521.3 12.8 %collective-permute-done.19 = bf16[256,2304]{1,0:T(8,128)(2,1)S(1)} collective-permute-done((bf16[256,2304]{1,0:T(8,128)(2,1)S(1)}, bf16[256,2304]{1,0:T(8,128)(2,1)S(1)}, u32[]{:S(2)}, u32[]{:S(2)}) %collective-permute-start.19) | collective-permute-done | bytes 1179680 | tf_op jit(solution)/shard_map/ppermute | solution.py:348
  541.7 5.1 collective-permute-done.21
  557.4 12.4 %fusion.48 = f32[2048,720]{0,1:T(8,128)} fusion(bf16[2048,2304]{1,0:T(8,128)(2,1)} %constant_dynamic-update-slice_fusion.9, bf16[2304,720]{1,0:T(8,128)(2,1)} %all-gather.14.cloned.1.call-done), kind=kOutput, calls=%fused_computation.274 | convolution fusion | flops 6794772480 | bytes 18653184 | tf_op jit(solution)/shard_map/dot_general | solution.py:543
  569.8 18.1 %multiply_convert_fusion.1 = (bf16[2048,720]{0,1:T(8,128)(2,1)}, bf16[2048,720]{0,1:T(8,128)(2,1)}, bf16[2048,720]{0,1:T(8,128)(2,1)}) fusion(f32[2048,720]{0,1:T(8,128)} %fusion.49, f32[2048,720]{0,1:T(8,128)} %fusion.48, bf16[2048,2304]{1,0:T(8,128)(2,1)} %constant_dynamic-update-slice_fusion.9, bf16[2304,720]{1,0:T(8,128)(2,1)} %all-gather.12.cloned.1.call-done), kind=kOutput, calls=%fused_computation.9 | convolution fusion | flops 6816890880 | bytes 33398784 | tf_op jit(solution)/shard_map/dot_general | solution.py:542
  588.0 13.9 %fusion.50 = f32[2048,2304]{1,0:T(8,128)} fusion(bf16[2048,720]{0,1:T(8,128)(2,1)} %get-tuple-element.40, bf16[2304,720]{1,0:T(8,128)(2,1)} %all-gather.14.cloned.1.call-done), kind=kOutput, calls=%fused_computation.276 | convolution fusion | flops 6794772480 | bytes 25141248 | tf_op jit(solution)/shard_map/dot_general | solution.py:87
  601.9 15.6 %add_convert_fusion = bf16[2048,2304]{1,0:T(8,128)(2,1)} fusion(f32[2048,2304]{1,0:T(8,128)} %fusion.50, bf16[2048,720]{0,1:T(8,128)(2,1)} %get-tuple-element.39, bf16[2304,720]{1,0:T(8,128)(2,1)} %all-gather.12.cloned.1.call-done), kind=kOutput, calls=%fused_computation | convolution fusion | flops 6804209664 | bytes 34578432 | tf_op jit(solution)/shard_map/dot_general | solution.py:87
  617.5 4.9 slice.342
  622.9 8.3 convolution_convert_fusion.1
  636.9 12.1 convolution_convert_fusion.4
  649.0 5.7 copy.128
  659.0 8.7 convert_add_fusion.1
  672.2 8.5 fusion.39
  683.6 13.4 %collective-permute-done.49 = bf16[256,2304]{1,0:T(8,128)(2,1)S(1)} collective-permute-done((bf16[256,2304]{1,0:T(8,128)(2,1)}, bf16[256,2304]{1,0:T(8,128)(2,1)S(1)}, u32[]{:S(2)}, u32[]{:S(2)}) %collective-permute-start.49) | collective-permute-done | bytes 1179680 | tf_op jit(solution)/shard_map/ppermute | solution.py:348
  698.3 25.0 %collective-permute-done.51 = bf16[256,2304]{1,0:T(8,128)(2,1)S(1)} collective-permute-done((bf16[256,2304]{1,0:T(8,128)(2,1)}, bf16[256,2304]{1,0:T(8,128)(2,1)S(1)}, u32[]{:S(2)}, u32[]{:S(2)}) %collective-permute-start.51) | collective-permute-done | bytes 1179680 | tf_op jit(solution)/shard_map/ppermute | solution.py:348
  726.8 20.7 %collective-permute-done.29 = bf16[256,2304]{1,0:T(8,128)(2,1)S(1)} collective-permute-done((bf16[256,2304]{1,0:T(8,128)(2,1)S(1)}, bf16[256,2304]{1,0:T(8,128)(2,1)S(1)}, u32[]{:S(2)}, u32[]{:S(2)}) %collective-permute-start.29) | collective-permute-done | bytes 1179680 | tf_op jit(solution)/shard_map/ppermute | solution.py:348
  747.5 26.3 %collective-permute-done.31 = bf16[256,2304]{1,0:T(8,128)(2,1)S(1)} collective-permute-done((bf16[256,2304]{1,0:T(8,128)(2,1)S(1)}, bf16[256,2304]{1,0:T(8,128)(2,1)S(1)}, u32[]{:S(2)}, u32[]{:S(2)}) %collective-permute-start.31) | collective-permute-done | bytes 1179680 | tf_op jit(solution)/shard_map/ppermute | solution.py:348
  781.9 8.4 convolution_convert_fusion.6
  796.4 8.5 collective-permute-done.53
  831.4 6.9 fusion.51
  841.2 12.5 %convolution_convert_fusion.5 = bf16[2304,720]{0,1:T(8,128)(2,1)} fusion(bf16[2048,720]{0,1:T(8,128)(2,1)} %get-tuple-element.39, bf16[2048,2304]{1,0:T(8,128)(2,1)} %constant_dynamic-update-slice_fusion.9), kind=kOutput, calls=%fused_computation.15 | convolution fusion | flops 6796431360 | bytes 15704064 | tf_op jit(solution)/shard_map/dot_general | solution.py:91
  853.8 5.7 copy.125
  859.5 4.1 copy.126
  864.5 8.1 convolution_convert_fusion.7.outer_ref
  872.6 62.2 %attend_back.1 = bf16[2048,960]{1,0:T(8,128)(2,1)} custom-call(s32[33]{0:T(128)S(1)} %pad_add_fusion.index_ref, bf16[3,2048,384]{2,1,0:T(8,128)(2,1)} %copy-done.4, bf16[2048,384]{1,0:T(8,128)(2,1)S(1)} %convolution_convert_fusion.7.outer_ref, f32[1280,128]{1,0:T(8,128)S(1)} %get-tuple-element.126.cos_ref, f32[1280,128]{1,0:T(8,128)S(1)} %get-tuple-element.125.sin_ref), custom_call_target="tpu_custom_call" | custom-call | flops 12582912000 | bytes 20971520 | tf_op jit(solution)/shard_map/attend_back/pallas_call | solution.py:305
  934.9 13.4 %convolution_convert_fusion = bf16[2048,2304]{1,0:T(8,128)(2,1)S(1)} fusion(bf16[2048,960]{1,0:T(8,128)(2,1)} %attend_back.1, bf16[2304,960]{1,0:T(8,128)(2,1)} %all-gather.8.cloned.1.call-done), kind=kOutput, calls=%fused_computation.1 | convolution fusion | flops 9064415232 | bytes 17793024 | tf_op jit(solution)/shard_map/dot_general | solution.py:87
  954.7 14.6 %convolution_convert_fusion.3 = bf16[2304,960]{0,1:T(8,128)(2,1)} fusion(bf16[2048,2304]{1,0:T(8,128)(2,1)} %constant_dynamic-update-slice_fusion, bf16[2048,960]{1,0:T(8,128)(2,1)S(1)} %copy-done.50), kind=kOutput, calls=%fused_computation.13 | convolution fusion | flops 9061908480 | bytes 17793024 | tf_op jit(solution)/shard_map/dot_general | solution.py:91
  969.3 6.6 copy.105
  975.9 5.2 copy.106
  982.9 8.6 convert_add_fusion
  993.4 4.8 collective-permute-start.61
  1010.2 52.1 %collective-permute-done.33 = bf16[1,64,2304]{2,1,0:T(8,128)(2,1)S(1)} collective-permute-done((bf16[1,64,2304]{2,1,0:T(8,128)(2,1)S(1)}, bf16[1,64,2304]{2,1,0:T(8,128)(2,1)S(1)}, u32[]{:S(2)}, u32[]{:S(2)}) %collective-permute-start.33) | collective-permute-done | bytes 294944 | tf_op jit(solution)/shard_map/ppermute | solution.py:348
  1065.0 5.0 all-to-all-start.3
  1070.1 7.5 collective-permute-done.34
  1079.3 10.1 collective-permute-start.70
  1089.4 6.2 collective-permute-start.69
  1096.6 5.9 fusion.12
  1103.1 5.9 all-to-all-start.2
  1115.7 9.8 all-to-all-done.2
  1125.5 11.9 all-to-all-start.4
  1163.4 5.1 collective-permute-start.67
  1176.5 10.8 collective-permute-done.65
  1187.3 13.1 %all-to-all-start.1 = ((bf16[8,72,960]{2,1,0:T(8,128)(2,1)}), bf16[8,72,960]{2,1,0:T(8,128)(2,1)S(1)}, u32[]{:S(2)}, u32[]{:S(2)}) async-start(bf16[8,72,960]{2,1,0:T(8,128)(2,1)} %bitcast.194), calls=%async_computation.2 | async-start | bytes 2359296 | tf_op jit(solution)/shard_map/all_to_all | solution.py:572
  1202.2 11.7 all-to-all-done.1
  (423 shorter events, 316.5 us)
Async XLA Ops:
  7.2 256.8 %all-gather.10.cloned.1.call-start = ((), (), s32[]{:S(2)}) async-start(), calls=%async_computation.11 | async-start | bytes 1658880 | tf_op jit(solution)/shard_map/all_gather | solution.py:446
  9.1 295.2 %all-gather.8.cloned.1.call-start = ((), (), s32[]{:S(2)}) async-start(), calls=%async_computation.10 | async-start | bytes 5898240 | tf_op jit(solution)/shard_map/all_gather | solution.py:442
  24.8 434.2 %all-gather.16.cloned.1.call-start = ((), (), s32[]{:S(2)}) async-start(), calls=%async_computation.19 | async-start | bytes 4239360 | tf_op jit(solution)/shard_map/all_gather | solution.py:487
  27.2 179.0 %collective-permute-start.3 = (bf16[1,64,2304]{2,1,0:T(8,128)(2,1)}, bf16[1,64,2304]{2,1,0:T(8,128)(2,1)}, u32[]{:S(2)}, u32[]{:S(2)}) collective-permute-start(bf16[1,64,2304]{2,1,0:T(8,128)(2,1)} %get-tuple-element.119), channel_id=1, source_target_pairs={{0,24},{1,25},{2,16},{3,17},{4,8},{5,9},{6,0},{7,1},{8,18},{9,19},... | collective-permute-start | bytes 884744 | tf_op jit(solution)/shard_map/ppermute | solution.py:348
  32.4 172.8 %collective-permute-start.2 = (bf16[1,64,2304]{2,1,0:T(8,128)(2,1)}, bf16[1,64,2304]{2,1,0:T(8,128)(2,1)}, u32[]{:S(2)}, u32[]{:S(2)}) collective-permute-start(bf16[1,64,2304]{2,1,0:T(8,128)(2,1)} %get-tuple-element.120), channel_id=1, source_target_pairs={{0,16},{1,17},{2,24},{3,25},{4,0},{5,1},{6,8},{7,9},{8,26},{9,27},... | collective-permute-start | bytes 884744 | tf_op jit(solution)/shard_map/ppermute | solution.py:348
  36.7 164.5 %collective-permute-start.1 = (bf16[1,64,2304]{2,1,0:T(8,128)(2,1)}, bf16[1,64,2304]{2,1,0:T(8,128)(2,1)}, u32[]{:S(2)}, u32[]{:S(2)}) collective-permute-start(bf16[1,64,2304]{2,1,0:T(8,128)(2,1)} %get-tuple-element.121), channel_id=1, source_target_pairs={{0,8},{1,9},{2,0},{3,1},{4,24},{5,25},{6,16},{7,17},{8,2},{9,3},{1... | collective-permute-start | bytes 884744 | tf_op jit(solution)/shard_map/ppermute | solution.py:348
  39.9 156.5 %collective-permute-start = (bf16[1,64,2304]{2,1,0:T(8,128)(2,1)}, bf16[1,64,2304]{2,1,0:T(8,128)(2,1)}, u32[]{:S(2)}, u32[]{:S(2)}) collective-permute-start(bf16[1,64,2304]{2,1,0:T(8,128)(2,1)} %get-tuple-element.122), channel_id=1, source_target_pairs={{0,0},{1,1},{2,8},{3,9},{4,16},{5,17},{6,24},{7,25},{8,10},{9,11},... | collective-permute-start | bytes 884744 | tf_op jit(solution)/shard_map/ppermute | solution.py:348
  44.7 339.6 %collective-permute-start.39 = (bf16[1,64,2304]{2,1,0:T(8,128)(2,1)}, bf16[1,64,2304]{2,1,0:T(8,128)(2,1)}, u32[]{:S(2)}, u32[]{:S(2)}) collective-permute-start(bf16[1,64,2304]{2,1,0:T(8,128)(2,1)} %get-tuple-element.111), channel_id=1, source_target_pairs={{0,24},{1,25},{2,16},{3,17},{4,8},{5,9},{6,0},{7,1},{8,18},{9,19},... | collective-permute-start | bytes 884744 | tf_op jit(solution)/shard_map/ppermute | solution.py:348
  48.0 509.4 %all-gather.14.cloned.1.call-start = ((), (), s32[]{:S(2)}) async-start(), calls=%async_computation.13 | async-start | bytes 4423680 | tf_op jit(solution)/shard_map/all_gather | solution.py:481
  201.2 21.5 %collective-permute-start.27 = (bf16[288,720]{1,0:T(8,128)(2,1)}, bf16[288,720]{1,0:T(8,128)(2,1)}, u32[]{:S(2)}, u32[]{:S(2)}) collective-permute-start(bf16[288,720]{1,0:T(8,128)(2,1)} %broadcast_select_fusion.6), channel_id=1, source_target_pairs={{0,1},{1,0},{2,3},{3,2},{4,5},{5,4},{6,7},{7,6},{8,9},{9,8},{10,11... | collective-permute-start | bytes 1244168 | tf_op jit(solution)/shard_map/ppermute | solution.py:348
  209.4 28.8 %collective-permute-start.5 = (bf16[256,2304]{1,0:T(8,128)(2,1)}, bf16[256,2304]{1,0:T(8,128)(2,1)}, u32[]{:S(2)}, u32[]{:S(2)}) collective-permute-start(bf16[256,2304]{1,0:T(8,128)(2,1)} %get-tuple-element.128), channel_id=1, source_target_pairs={{0,16},{1,17},{2,18},{3,19},{4,20},{5,21},{6,22},{7,23},{8,24},{9,... | collective-permute-start | bytes 3538952 | tf_op jit(solution)/shard_map/ppermute | solution.py:348
  209.4 47.7 %collective-permute-start.4 = (bf16[256,2304]{1,0:T(8,128)(2,1)}, bf16[256,2304]{1,0:T(8,128)(2,1)}, u32[]{:S(2)}, u32[]{:S(2)}) collective-permute-start(bf16[256,2304]{1,0:T(8,128)(2,1)} %get-tuple-element.128), channel_id=1, source_target_pairs={{0,8},{1,9},{2,10},{3,11},{4,12},{5,13},{6,14},{7,15},{8,0},{9,1},... | collective-permute-start | bytes 3538952 | tf_op jit(solution)/shard_map/ppermute | solution.py:348
  213.9 168.6 %collective-permute-start.38 = (bf16[1,64,2304]{2,1,0:T(8,128)(2,1)}, bf16[1,64,2304]{2,1,0:T(8,128)(2,1)}, u32[]{:S(2)}, u32[]{:S(2)}) collective-permute-start(bf16[1,64,2304]{2,1,0:T(8,128)(2,1)} %get-tuple-element.112), channel_id=1, source_target_pairs={{0,16},{1,17},{2,24},{3,25},{4,0},{5,1},{6,8},{7,9},{8,26},{9,27},... | collective-permute-start | bytes 884744 | tf_op jit(solution)/shard_map/ppermute | solution.py:348
  222.7 67.0 %collective-permute-start.8 = (bf16[256,2304]{1,0:T(8,128)(2,1)}, bf16[256,2304]{1,0:T(8,128)(2,1)}, u32[]{:S(2)}, u32[]{:S(2)}) collective-permute-start(bf16[256,2304]{1,0:T(8,128)(2,1)} %get-tuple-element.128), channel_id=1, source_target_pairs={{0,1},{1,0},{2,3},{3,2},{4,5},{5,4},{6,7},{7,6},{8,9},{9,8},{10,11... | collective-permute-start | bytes 3538952 | tf_op jit(solution)/shard_map/ppermute | solution.py:348
  240.1 46.4 %collective-permute-start.7 = (bf16[128,2304]{1,0:T(8,128)(2,1)}, bf16[128,2304]{1,0:T(8,128)(2,1)S(1)}, u32[]{:S(2)}, u32[]{:S(2)}) collective-permute-start(bf16[128,2304]{1,0:T(8,128)(2,1)} %slice.320), channel_id=1, source_target_pairs={{0,8},{1,9},{2,10},{3,11},{4,12},{5,13},{6,14},{7,15},{8,0},{9,1},... | collective-permute-start | bytes 1769480 | tf_op jit(solution)/shard_map/ppermute | solution.py:348
  264.0 32.9 %all-to-all-start = ((bf16[4,72,2304]{2,1,0:T(8,128)(2,1)}), bf16[4,72,2304]{2,1,0:T(8,128)(2,1)}, u32[]{:S(2)}, u32[]{:S(2)}) async-start(bf16[4,72,2304]{2,1,0:T(8,128)(2,1)} %bitcast.193), calls=%async_computation | async-start | bytes 2654208 | tf_op jit(solution)/shard_map/all_to_all | solution.py:452
  268.6 301.3 %all-gather.12.cloned.1.call-start = ((), (), s32[]{:S(2)}) async-start(), calls=%async_computation.12 | async-start | bytes 4423680 | tf_op jit(solution)/shard_map/all_gather | solution.py:481
  272.3 21.9 %collective-permute-start.9 = (bf16[256,2304]{1,0:T(8,128)(2,1)}, bf16[256,2304]{1,0:T(8,128)(2,1)S(1)}, u32[]{:S(2)}, u32[]{:S(2)}) collective-permute-start(bf16[256,2304]{1,0:T(8,128)(2,1)} %collective-permute-done.4), channel_id=1, source_target_pairs={{0,1},{1,0},{2,3},{3,2},{4,5},{5,4},{6,7},{7,6},{8,9},{9,8},{10,11... | collective-permute-start | bytes 3538952 | tf_op jit(solution)/shard_map/ppermute | solution.py:348
  289.7 92.1 %collective-permute-start.37 = (bf16[1,64,2304]{2,1,0:T(8,128)(2,1)}, bf16[1,64,2304]{2,1,0:T(8,128)(2,1)S(1)}, u32[]{:S(2)}, u32[]{:S(2)}) collective-permute-start(bf16[1,64,2304]{2,1,0:T(8,128)(2,1)} %get-tuple-element.113), channel_id=1, source_target_pairs={{0,8},{1,9},{2,0},{3,1},{4,24},{5,25},{6,16},{7,17},{8,2},{9,3},{1... | collective-permute-start | bytes 884744 | tf_op jit(solution)/shard_map/ppermute | solution.py:348
  381.3 56.5 %collective-permute-start.14 = (bf16[1024,2304]{1,0:T(8,128)(2,1)}, bf16[1024,2304]{1,0:T(8,128)(2,1)}, u32[]{:S(2)}, u32[]{:S(2)}) collective-permute-start(bf16[1024,2304]{1,0:T(8,128)(2,1)} %slice.326), channel_id=1, source_target_pairs={{0,1},{1,0},{2,3},{3,2},{4,5},{5,4},{6,7},{7,6},{8,9},{9,8},{10,11... | collective-permute-start | bytes 14155784 | tf_op jit(solution)/shard_map/ppermute | solution.py:348
  388.9 27.9 %collective-permute-start.41 = (bf16[256,2304]{1,0:T(8,128)(2,1)}, bf16[256,2304]{1,0:T(8,128)(2,1)}, u32[]{:S(2)}, u32[]{:S(2)}) collective-permute-start(bf16[256,2304]{1,0:T(8,128)(2,1)} %get-tuple-element.130), channel_id=1, source_target_pairs={{0,16},{1,17},{2,18},{3,19},{4,20},{5,21},{6,22},{7,23},{8,24},{9,... | collective-permute-start | bytes 3538952 | tf_op jit(solution)/shard_map/ppermute | solution.py:348
  388.9 29.1 %collective-permute-start.40 = (bf16[256,2304]{1,0:T(8,128)(2,1)}, bf16[256,2304]{1,0:T(8,128)(2,1)}, u32[]{:S(2)}, u32[]{:S(2)}) collective-permute-start(bf16[256,2304]{1,0:T(8,128)(2,1)} %get-tuple-element.130), channel_id=1, source_target_pairs={{0,8},{1,9},{2,10},{3,11},{4,12},{5,13},{6,14},{7,15},{8,0},{9,1},... | collective-permute-start | bytes 3538952 | tf_op jit(solution)/shard_map/ppermute | solution.py:348
  389.6 60.0 %collective-permute-start.44 = (bf16[256,2304]{1,0:T(8,128)(2,1)}, bf16[256,2304]{1,0:T(8,128)(2,1)}, u32[]{:S(2)}, u32[]{:S(2)}) collective-permute-start(bf16[256,2304]{1,0:T(8,128)(2,1)} %get-tuple-element.130), channel_id=1, source_target_pairs={{0,1},{1,0},{2,3},{3,2},{4,5},{5,4},{6,7},{7,6},{8,9},{9,8},{10,11... | collective-permute-start | bytes 3538952 | tf_op jit(solution)/shard_map/ppermute | solution.py:348
  392.9 672.1 %reduce-scatter.12.cloned.1.call-start = ((), (), s32[]{:S(2)}) async-start(), calls=%async_computation.17 | async-start | bytes 4423680 | tf_op jit(solution)/shard_map/reduce_scatter | solution.py:570
  419.4 36.1 %collective-permute-start.46 = (bf16[256,2304]{1,0:T(8,128)(2,1)}, bf16[256,2304]{1,0:T(8,128)(2,1)S(1)}, u32[]{:S(2)}, u32[]{:S(2)}) collective-permute-start(bf16[256,2304]{1,0:T(8,128)(2,1)} %collective-permute-done.41), channel_id=1, source_target_pairs={{0,1},{1,0},{2,3},{3,2},{4,5},{5,4},{6,7},{7,6},{8,9},{9,8},{10,11... | collective-permute-start | bytes 3538952 | tf_op jit(solution)/shard_map/ppermute | solution.py:348
  434.8 21.8 %collective-permute-start.47 = (bf16[256,2304]{1,0:T(8,128)(2,1)}, bf16[256,2304]{1,0:T(8,128)(2,1)}, u32[]{:S(2)}, u32[]{:S(2)}) collective-permute-start(bf16[256,2304]{1,0:T(8,128)(2,1)} %pad_maximum_fusion.3), channel_id=1, source_target_pairs={{0,1},{1,0},{2,3},{3,2},{4,5},{5,4},{6,7},{7,6},{8,9},{9,8},{10,11... | collective-permute-start | bytes 3538952 | tf_op jit(solution)/shard_map/ppermute | solution.py:348
  448.1 27.9 %collective-permute-start.15 = (bf16[256,2304]{1,0:T(8,128)(2,1)}, bf16[256,2304]{1,0:T(8,128)(2,1)}, u32[]{:S(2)}, u32[]{:S(2)}) collective-permute-start(bf16[256,2304]{1,0:T(8,128)(2,1)} %get-tuple-element.51), channel_id=1, source_target_pairs={{0,8},{1,9},{2,10},{3,11},{4,12},{5,13},{6,14},{7,15},{8,0},{9,1},... | collective-permute-start | bytes 3538952 | tf_op jit(solution)/shard_map/ppermute | solution.py:348
  449.5 51.7 %collective-permute-start.17 = (bf16[256,2304]{1,0:T(8,128)(2,1)}, bf16[256,2304]{1,0:T(8,128)(2,1)}, u32[]{:S(2)}, u32[]{:S(2)}) collective-permute-start(bf16[256,2304]{1,0:T(8,128)(2,1)} %get-tuple-element.52), channel_id=1, source_target_pairs={{0,24},{1,25},{2,26},{3,27},{4,28},{5,29},{6,30},{7,31},{8,16},{9,... | collective-permute-start | bytes 3538952 | tf_op jit(solution)/shard_map/ppermute | solution.py:348
  449.6 52.8 %collective-permute-start.16 = (bf16[256,2304]{1,0:T(8,128)(2,1)}, bf16[256,2304]{1,0:T(8,128)(2,1)}, u32[]{:S(2)}, u32[]{:S(2)}) collective-permute-start(bf16[256,2304]{1,0:T(8,128)(2,1)} %get-tuple-element.53), channel_id=1, source_target_pairs={{0,16},{1,17},{2,18},{3,19},{4,20},{5,21},{6,22},{7,23},{8,24},{9,... | collective-permute-start | bytes 3538952 | tf_op jit(solution)/shard_map/ppermute | solution.py:348
  507.9 26.2 %collective-permute-start.19 = (bf16[256,2304]{1,0:T(8,128)(2,1)S(1)}, bf16[256,2304]{1,0:T(8,128)(2,1)S(1)}, u32[]{:S(2)}, u32[]{:S(2)}) collective-permute-start(bf16[256,2304]{1,0:T(8,128)(2,1)S(1)} %get-tuple-element.28), channel_id=1, source_target_pairs={{0,16},{1,17},{2,18},{3,19},{4,20},{5,21},{6,22},{7,23},{8,24},{9,... | collective-permute-start | bytes 3538952 | tf_op jit(solution)/shard_map/ppermute | solution.py:348
  508.9 26.3 %collective-permute-start.18 = (bf16[256,2304]{1,0:T(8,128)(2,1)S(1)}, bf16[256,2304]{1,0:T(8,128)(2,1)S(1)}, u32[]{:S(2)}, u32[]{:S(2)}) collective-permute-start(bf16[256,2304]{1,0:T(8,128)(2,1)S(1)} %get-tuple-element.28), channel_id=1, source_target_pairs={{0,8},{1,9},{2,10},{3,11},{4,12},{5,13},{6,14},{7,15},{8,0},{9,1},... | collective-permute-start | bytes 3538952 | tf_op jit(solution)/shard_map/ppermute | solution.py:348
  519.3 33.6 %collective-permute-start.22 = (bf16[256,2304]{1,0:T(8,128)(2,1)S(1)}, bf16[256,2304]{1,0:T(8,128)(2,1)S(1)}, u32[]{:S(2)}, u32[]{:S(2)}) collective-permute-start(bf16[256,2304]{1,0:T(8,128)(2,1)S(1)} %get-tuple-element.28), channel_id=1, source_target_pairs={{0,1},{1,0},{2,3},{3,2},{4,5},{5,4},{6,7},{7,6},{8,9},{9,8},{10,11... | collective-permute-start | bytes 3538952 | tf_op jit(solution)/shard_map/ppermute | solution.py:348
  622.4 36.5 %collective-permute-start.48 = (bf16[1024,2304]{1,0:T(8,128)(2,1)}, bf16[1024,2304]{1,0:T(8,128)(2,1)}, u32[]{:S(2)}, u32[]{:S(2)}) collective-permute-start(bf16[1024,2304]{1,0:T(8,128)(2,1)} %slice.342), channel_id=1, source_target_pairs={{0,1},{1,0},{2,3},{3,2},{4,5},{5,4},{6,7},{7,6},{8,9},{9,8},{10,11... | collective-permute-start | bytes 14155784 | tf_op jit(solution)/shard_map/ppermute | solution.py:348
  636.8 35.4 %collective-permute-start.28 = (bf16[1024,2304]{1,0:T(8,128)(2,1)}, bf16[1024,2304]{1,0:T(8,128)(2,1)}, u32[]{:S(2)}, u32[]{:S(2)}) collective-permute-start(bf16[1024,2304]{1,0:T(8,128)(2,1)} %slice.334), channel_id=1, source_target_pairs={{0,1},{1,0},{2,3},{3,2},{4,5},{5,4},{6,7},{7,6},{8,9},{9,8},{10,11... | collective-permute-start | bytes 14155784 | tf_op jit(solution)/shard_map/ppermute | solution.py:348
  658.7 420.5 %reduce-scatter.14.cloned.1.call-start = ((), (), s32[]{:S(2)}) async-start(), calls=%async_computation.18 | async-start | bytes 4239360 | tf_op jit(solution)/shard_map/reduce_scatter | solution.py:554
  669.6 27.4 %collective-permute-start.49 = (bf16[256,2304]{1,0:T(8,128)(2,1)}, bf16[256,2304]{1,0:T(8,128)(2,1)S(1)}, u32[]{:S(2)}, u32[]{:S(2)}) collective-permute-start(bf16[256,2304]{1,0:T(8,128)(2,1)} %get-tuple-element.45), channel_id=1, source_target_pairs={{0,8},{1,9},{2,10},{3,11},{4,12},{5,13},{6,14},{7,15},{8,0},{9,1},... | collective-permute-start | bytes 3538952 | tf_op jit(solution)/shard_map/ppermute | solution.py:348
  670.5 52.8 %collective-permute-start.51 = (bf16[256,2304]{1,0:T(8,128)(2,1)}, bf16[256,2304]{1,0:T(8,128)(2,1)S(1)}, u32[]{:S(2)}, u32[]{:S(2)}) collective-permute-start(bf16[256,2304]{1,0:T(8,128)(2,1)} %get-tuple-element.46), channel_id=1, source_target_pairs={{0,24},{1,25},{2,26},{3,27},{4,28},{5,29},{6,30},{7,31},{8,16},{9,... | collective-permute-start | bytes 3538952 | tf_op jit(solution)/shard_map/ppermute | solution.py:348
  672.1 51.2 %collective-permute-start.50 = (bf16[256,2304]{1,0:T(8,128)(2,1)}, bf16[256,2304]{1,0:T(8,128)(2,1)}, u32[]{:S(2)}, u32[]{:S(2)}) collective-permute-start(bf16[256,2304]{1,0:T(8,128)(2,1)} %get-tuple-element.47), channel_id=1, source_target_pairs={{0,16},{1,17},{2,18},{3,19},{4,20},{5,21},{6,22},{7,23},{8,24},{9,... | collective-permute-start | bytes 3538952 | tf_op jit(solution)/shard_map/ppermute | solution.py:348
  681.0 66.5 %collective-permute-start.29 = (bf16[256,2304]{1,0:T(8,128)(2,1)S(1)}, bf16[256,2304]{1,0:T(8,128)(2,1)S(1)}, u32[]{:S(2)}, u32[]{:S(2)}) collective-permute-start(bf16[256,2304]{1,0:T(8,128)(2,1)S(1)} %get-tuple-element.48), channel_id=1, source_target_pairs={{0,8},{1,9},{2,10},{3,11},{4,12},{5,13},{6,14},{7,15},{8,0},{9,1},... | collective-permute-start | bytes 3538952 | tf_op jit(solution)/shard_map/ppermute | solution.py:348
  682.1 91.8 %collective-permute-start.31 = (bf16[256,2304]{1,0:T(8,128)(2,1)S(1)}, bf16[256,2304]{1,0:T(8,128)(2,1)S(1)}, u32[]{:S(2)}, u32[]{:S(2)}) collective-permute-start(bf16[256,2304]{1,0:T(8,128)(2,1)S(1)} %get-tuple-element.49), channel_id=1, source_target_pairs={{0,24},{1,25},{2,26},{3,27},{4,28},{5,29},{6,30},{7,31},{8,16},{9,... | collective-permute-start | bytes 3538952 | tf_op jit(solution)/shard_map/ppermute | solution.py:348
  697.0 76.8 %collective-permute-start.30 = (bf16[256,2304]{1,0:T(8,128)(2,1)S(1)}, bf16[256,2304]{1,0:T(8,128)(2,1)S(1)}, u32[]{:S(2)}, u32[]{:S(2)}) collective-permute-start(bf16[256,2304]{1,0:T(8,128)(2,1)S(1)} %get-tuple-element.50), channel_id=1, source_target_pairs={{0,16},{1,17},{2,18},{3,19},{4,20},{5,21},{6,22},{7,23},{8,24},{9,... | collective-permute-start | bytes 3538952 | tf_op jit(solution)/shard_map/ppermute | solution.py:348
  779.9 25.1 %collective-permute-start.53 = (bf16[256,2304]{1,0:T(8,128)(2,1)}, bf16[256,2304]{1,0:T(8,128)(2,1)}, u32[]{:S(2)}, u32[]{:S(2)}) collective-permute-start(bf16[256,2304]{1,0:T(8,128)(2,1)} %get-tuple-element.25), channel_id=1, source_target_pairs={{0,16},{1,17},{2,18},{3,19},{4,20},{5,21},{6,22},{7,23},{8,24},{9,... | collective-permute-start | bytes 3538952 | tf_op jit(solution)/shard_map/ppermute | solution.py:348
  781.0 27.1 %collective-permute-start.52 = (bf16[256,2304]{1,0:T(8,128)(2,1)}, bf16[256,2304]{1,0:T(8,128)(2,1)}, u32[]{:S(2)}, u32[]{:S(2)}) collective-permute-start(bf16[256,2304]{1,0:T(8,128)(2,1)} %get-tuple-element.25), channel_id=1, source_target_pairs={{0,8},{1,9},{2,10},{3,11},{4,12},{5,13},{6,14},{7,15},{8,0},{9,1},... | collective-permute-start | bytes 3538952 | tf_op jit(solution)/shard_map/ppermute | solution.py:348
  793.9 295.5 %reduce-scatter.8.cloned.1.call-start = ((), (), s32[]{:S(2)}) async-start(), calls=%async_computation.15 | async-start | bytes 1658880 | tf_op jit(solution)/shard_map/reduce_scatter | solution.py:601
  794.1 32.8 %collective-permute-start.56 = (bf16[256,2304]{1,0:T(8,128)(2,1)}, bf16[256,2304]{1,0:T(8,128)(2,1)S(1)}, u32[]{:S(2)}, u32[]{:S(2)}) collective-permute-start(bf16[256,2304]{1,0:T(8,128)(2,1)} %get-tuple-element.25), channel_id=1, source_target_pairs={{0,1},{1,0},{2,3},{3,2},{4,5},{5,4},{6,7},{7,6},{8,9},{9,8},{10,11... | collective-permute-start | bytes 3538952 | tf_op jit(solution)/shard_map/ppermute | solution.py:348
  810.3 18.9 %collective-permute-start.58 = (bf16[256,2304]{1,0:T(8,128)(2,1)}, bf16[256,2304]{1,0:T(8,128)(2,1)S(1)}, u32[]{:S(2)}, u32[]{:S(2)}) collective-permute-start(bf16[256,2304]{1,0:T(8,128)(2,1)} %collective-permute-done.53), channel_id=1, source_target_pairs={{0,1},{1,0},{2,3},{3,2},{4,5},{5,4},{6,7},{7,6},{8,9},{9,8},{10,11... | collective-permute-start | bytes 3538952 | tf_op jit(solution)/shard_map/ppermute | solution.py:348
  841.2 261.9 %reduce-scatter.10.cloned.1.call-start = ((), (), s32[]{:S(2)}) async-start(), calls=%async_computation.16 | async-start | bytes 4423680 | tf_op jit(solution)/shard_map/reduce_scatter | solution.py:570
  863.6 323.7 %reduce-scatter.6.cloned.1.call-start = ((), (), s32[]{:S(2)}) async-start(), calls=%async_computation.14 | async-start | bytes 5898240 | tf_op jit(solution)/shard_map/reduce_scatter | solution.py:570
  954.3 28.5 %collective-permute-start.60 = (bf16[1024,2304]{1,0:T(8,128)(2,1)}, bf16[1024,2304]{1,0:T(8,128)(2,1)}, u32[]{:S(2)}, u32[]{:S(2)}) collective-permute-start(bf16[1024,2304]{1,0:T(8,128)(2,1)} %slice.350), channel_id=1, source_target_pairs={{0,1},{1,0},{2,3},{3,2},{4,5},{5,4},{6,7},{7,6},{8,9},{9,8},{10,11... | collective-permute-start | bytes 14155784 | tf_op jit(solution)/shard_map/ppermute | solution.py:348
  982.0 23.5 %collective-permute-start.32 = (bf16[1,64,2304]{2,1,0:T(8,128)(2,1)S(1)}, bf16[1,64,2304]{2,1,0:T(8,128)(2,1)S(1)}, u32[]{:S(2)}, u32[]{:S(2)}) collective-permute-start(bf16[1,64,2304]{2,1,0:T(8,128)(2,1)S(1)} %get-tuple-element.118), channel_id=1, source_target_pairs={{0,0},{1,1},{2,10},{3,11},{4,20},{5,21},{6,30},{7,31},{8,2},{9,3},... | collective-permute-start | bytes 884744 | tf_op jit(solution)/shard_map/ppermute | solution.py:348
  993.4 96.0 %collective-permute-start.61 = (bf16[256,2304]{1,0:T(8,128)(2,1)}, bf16[256,2304]{1,0:T(8,128)(2,1)S(1)}, u32[]{:S(2)}, u32[]{:S(2)}) collective-permute-start(bf16[256,2304]{1,0:T(8,128)(2,1)} %get-tuple-element.42), channel_id=1, source_target_pairs={{0,8},{1,9},{2,10},{3,11},{4,12},{5,13},{6,14},{7,15},{8,0},{9,1},... | collective-permute-start | bytes 3538952 | tf_op jit(solution)/shard_map/ppermute | solution.py:348
  998.2 97.4 %collective-permute-start.63 = (bf16[256,2304]{1,0:T(8,128)(2,1)}, bf16[256,2304]{1,0:T(8,128)(2,1)S(1)}, u32[]{:S(2)}, u32[]{:S(2)}) collective-permute-start(bf16[256,2304]{1,0:T(8,128)(2,1)} %get-tuple-element.43), channel_id=1, source_target_pairs={{0,24},{1,25},{2,26},{3,27},{4,28},{5,29},{6,30},{7,31},{8,16},{9,... | collective-permute-start | bytes 3538952 | tf_op jit(solution)/shard_map/ppermute | solution.py:348
  1000.2 95.5 %collective-permute-start.62 = (bf16[256,2304]{1,0:T(8,128)(2,1)}, bf16[256,2304]{1,0:T(8,128)(2,1)}, u32[]{:S(2)}, u32[]{:S(2)}) collective-permute-start(bf16[256,2304]{1,0:T(8,128)(2,1)} %get-tuple-element.44), channel_id=1, source_target_pairs={{0,16},{1,17},{2,18},{3,19},{4,20},{5,21},{6,22},{7,23},{8,24},{9,... | collective-permute-start | bytes 3538952 | tf_op jit(solution)/shard_map/ppermute | solution.py:348
  1001.6 135.8 %collective-permute-start.35 = (bf16[1,64,2304]{2,1,0:T(8,128)(2,1)}, bf16[1,64,2304]{2,1,0:T(8,128)(2,1)}, u32[]{:S(2)}, u32[]{:S(2)}) collective-permute-start(bf16[1,64,2304]{2,1,0:T(8,128)(2,1)} %get-tuple-element.115), channel_id=1, source_target_pairs={{0,6},{1,7},{2,12},{3,13},{4,18},{5,19},{6,24},{7,25},{8,4},{9,5},... | collective-permute-start | bytes 884744 | tf_op jit(solution)/shard_map/ppermute | solution.py:348
  1005.5 56.9 %collective-permute-start.33 = (bf16[1,64,2304]{2,1,0:T(8,128)(2,1)S(1)}, bf16[1,64,2304]{2,1,0:T(8,128)(2,1)S(1)}, u32[]{:S(2)}, u32[]{:S(2)}) collective-permute-start(bf16[1,64,2304]{2,1,0:T(8,128)(2,1)S(1)} %get-tuple-element.117), channel_id=1, source_target_pairs={{0,2},{1,3},{2,8},{3,9},{4,22},{5,23},{6,28},{7,29},{8,0},{9,1},{1... | collective-permute-start | bytes 884744 | tf_op jit(solution)/shard_map/ppermute | solution.py:348
  1065.0 38.1 %all-to-all-start.3 = ((bf16[8,72,720]{2,1,0:T(8,128)(2,1)}), bf16[8,72,720]{2,1,0:T(8,128)(2,1)}, u32[]{:S(2)}, u32[]{:S(2)}) async-start(bf16[8,72,720]{2,1,0:T(8,128)(2,1)} %bitcast.197), calls=%async_computation.7 | async-start | bytes 1769472 | tf_op jit(solution)/shard_map/all_to_all | solution.py:572
  1079.3 79.8 %collective-permute-start.70 = (bf16[180,2304]{1,0:T(8,128)(2,1)}, bf16[180,2304]{1,0:T(8,128)(2,1)}, u32[]{:S(2)}, u32[]{:S(2)}) collective-permute-start(bf16[180,2304]{1,0:T(8,128)(2,1)} %bitcast.202), channel_id=1, source_target_pairs={{0,0},{1,4},{2,8},{3,12},{4,16},{5,20},{6,24},{7,28},{8,1},{9,5},{... | collective-permute-start | bytes 2488328 | tf_op jit(solution)/shard_map/ppermute | solution.py:348
  1089.4 72.1 %collective-permute-start.69 = (bf16[72,2304]{1,0:T(8,128)(2,1)}, bf16[72,2304]{1,0:T(8,128)(2,1)}, u32[]{:S(2)}, u32[]{:S(2)}) collective-permute-start(bf16[72,2304]{1,0:T(8,128)(2,1)} %bitcast.203), channel_id=1, source_target_pairs={{0,0},{1,4},{2,1},{3,5},{4,2},{5,6},{6,3},{7,7},{8,8},{9,12},{10,9... | collective-permute-start | bytes 995336 | tf_op jit(solution)/shard_map/ppermute | solution.py:348
  1103.1 22.4 %all-to-all-start.2 = ((bf16[8,72,720]{2,1,0:T(8,128)(2,1)}), bf16[8,72,720]{2,1,0:T(8,128)(2,1)}, u32[]{:S(2)}, u32[]{:S(2)}) async-start(bf16[8,72,720]{2,1,0:T(8,128)(2,1)} %bitcast.198), calls=%async_computation.5 | async-start | bytes 1769472 | tf_op jit(solution)/shard_map/all_to_all | solution.py:572
  1112.3 64.0 %collective-permute-start.64 = (bf16[1,64,2304]{2,1,0:T(8,128)(2,1)}, bf16[1,64,2304]{2,1,0:T(8,128)(2,1)S(1)}, u32[]{:S(2)}, u32[]{:S(2)}) collective-permute-start(bf16[1,64,2304]{2,1,0:T(8,128)(2,1)} %get-tuple-element.110), channel_id=1, source_target_pairs={{0,0},{1,1},{2,10},{3,11},{4,20},{5,21},{6,30},{7,31},{8,2},{9,3},... | collective-permute-start | bytes 884744 | tf_op jit(solution)/shard_map/ppermute | solution.py:348
  1125.5 49.2 %all-to-all-start.4 = ((f32[32,1,144]{2,1,0:T(1,128)}), f32[32,1,144]{2,1,0:T(1,128)}, u32[]{:S(2)}, u32[]{:S(2)}) async-start(f32[32,1,144]{2,1,0:T(1,128)} %all_to_all.31), calls=%async_computation.9 | async-start | bytes 65536 | tf_op jit(solution)/shard_map/all_to_all | solution.py:637
  1163.4 37.1 %collective-permute-start.67 = (bf16[1,64,2304]{2,1,0:T(8,128)(2,1)S(1)}, bf16[1,64,2304]{2,1,0:T(8,128)(2,1)S(1)}, u32[]{:S(2)}, u32[]{:S(2)}) collective-permute-start(bf16[1,64,2304]{2,1,0:T(8,128)(2,1)S(1)} %get-tuple-element.107), channel_id=1, source_target_pairs={{0,6},{1,7},{2,12},{3,13},{4,18},{5,19},{6,24},{7,25},{8,4},{9,5},... | collective-permute-start | bytes 884744 | tf_op jit(solution)/shard_map/ppermute | solution.py:348
  1168.5 18.7 %collective-permute-start.66 = (bf16[1,64,2304]{2,1,0:T(8,128)(2,1)S(1)}, bf16[1,64,2304]{2,1,0:T(8,128)(2,1)S(1)}, u32[]{:S(2)}, u32[]{:S(2)}) collective-permute-start(bf16[1,64,2304]{2,1,0:T(8,128)(2,1)S(1)} %get-tuple-element.108), channel_id=1, source_target_pairs={{0,4},{1,5},{2,14},{3,15},{4,16},{5,17},{6,26},{7,27},{8,6},{9,7},... | collective-permute-start | bytes 884744 | tf_op jit(solution)/shard_map/ppermute | solution.py:348
  1187.3 26.5 %all-to-all-start.1 = ((bf16[8,72,960]{2,1,0:T(8,128)(2,1)}), bf16[8,72,960]{2,1,0:T(8,128)(2,1)S(1)}, u32[]{:S(2)}, u32[]{:S(2)}) async-start(bf16[8,72,960]{2,1,0:T(8,128)(2,1)} %bitcast.194), calls=%async_computation.2 | async-start | bytes 2359296 | tf_op jit(solution)/shard_map/all_to_all | solution.py:572
  (76 other events, 2075.0 us)
Sparse Core Ops, SparseCore 0:
  10.2 101.6 all-gather.9
  114.0 137.6 all-gather.7
  253.2 83.8 all-gather.15
  338.5 69.9 all-gather.13
  409.9 68.5 all-gather.11
  658.9 66.0 reduce-scatter.11
  794.0 65.9 reduce-scatter.13
  862.8 31.8 reduce-scatter.7
  897.1 65.1 reduce-scatter.9
  981.2 102.9 reduce-scatter.5

commit v2 on v1

--- a/solution.py
+++ b/solution.py
@@ -48,8 +48,7 @@
     )
 
 
-def head_tiles(index_ref, total, run_tile):
-    pair = pl.program_id(0)
+def head_tiles(pair, index_ref, total, run_tile):
     side = index_ref[total // PIECE]
     own = pair < 2
     prompt_tiles = PROMPT // TILE
@@ -164,7 +163,7 @@
             out = out + nn_dot(far.astype(BF), kept_ref[0, 0:prefix, 2 * PAIR : 3 * PAIR])
         mixed[rows, :] = jnp.where(mask, out / count, mixed[rows, :])
 
-    head_tiles(index_ref, total, run_tile)
+    head_tiles(pair, index_ref, total, run_tile)
 
     def back(piece, carry):
         source = pl.multiple_of(index_ref[piece], PIECE)
@@ -199,18 +198,18 @@
         ],
         compiler_params=pltpu.CompilerParams(vmem_limit_bytes=40 << 20),
         cost_estimate=pl.CostEstimate(
-            flops=10 * 2 * 7680 * 256 * 128, bytes_accessed=20 << 20, transcendentals=9 << 20
+            flops=0, bytes_accessed=1 << 20, transcendentals=0
         ),
         name="attend",
     )(index, raw, cosine, sine)
 
 
 def attend_back_kernel(
-    index_ref, kept_ref, outer_ref, cos_ref, sin_ref, grad_ref, outer, grad_q, grad_k, grad_v
+    first, index_ref, kept_ref, outer_ref, cos_ref, sin_ref, grad_ref, outer, grad_q, grad_k, grad_v
 ):
     total = outer.shape[0]
     pieces = total // PIECE
-    pair = pl.program_id(0)
+    pair = pl.program_id(0) + first
 
     def sort(piece, carry):
         source = pl.multiple_of(index_ref[piece], PIECE)
@@ -264,7 +263,7 @@
             part = part + tn_dot(far, far_key)
         grad_q[rows, :] = jnp.where(mask, part * scale, grad_q[rows, :])
 
-    head_tiles(index_ref, total, run_tile)
+    head_tiles(pair, index_ref, total, run_tile)
 
     def unrope(field, row):
         cosine = cos_ref[pl.ds(row, PIECE), :]
@@ -300,16 +299,16 @@
         lax.fori_loop(0, pieces, back, 0)
 
 
-def attend_back(index, kept, outer, cosine, sine, columns):
+def attend_back(first, count, index, kept, outer, cosine, sine, columns):
     total = outer.shape[0]
     return pl.pallas_call(
-        attend_back_kernel,
+        functools.partial(attend_back_kernel, first),
         grid_spec=pltpu.PrefetchScalarGridSpec(
             num_scalar_prefetch=1,
-            grid=(3,),
+            grid=(count,),
             in_specs=[
-                pl.BlockSpec((1, total, SLAB), lambda j, index: (j, 0, 0)),
-                pl.BlockSpec((total, PAIR), lambda j, index: (0, j)),
+                pl.BlockSpec((1, total, SLAB), lambda j, index: (j + first, 0, 0)),
+                pl.BlockSpec((total, PAIR), lambda j, index: (0, j + first)),
                 pl.BlockSpec(cosine.shape, lambda j, index: (0, 0)),
                 pl.BlockSpec(sine.shape, lambda j, index: (0, 0)),
             ],
@@ -324,10 +323,23 @@
         out_shape=jax.ShapeDtypeStruct((total, columns), BF),
         compiler_params=pltpu.CompilerParams(vmem_limit_bytes=48 << 20),
         cost_estimate=pl.CostEstimate(
-            flops=25 * 2 * 7680 * 256 * 128, bytes_accessed=20 << 20, transcendentals=9 << 20
+            flops=0, bytes_accessed=1 << 20, transcendentals=0
         ),
         name="attend_back",
     )(index, kept, outer, cosine, sine)
+
+
+def after(array, *earlier):
+    leaves = [array] + jax.tree.leaves(earlier)
+    place = pl.BlockSpec(memory_space=pl.ANY)
+    return pl.pallas_call(
+        lambda *refs: None,
+        in_specs=[place] * len(leaves),
+        out_specs=place,
+        out_shape=jax.ShapeDtypeStruct(array.shape, array.dtype),
+        input_output_aliases={0: 0},
+        name="after",
+    )(*leaves)
 
 
 def make_layered(mesh):
@@ -376,46 +388,95 @@
         quarter = rows // n_grp
 
 
-        def shuffle_in(array):
-            parts = array.reshape(n_grp, quarter, width)
-            result = jnp.zeros_like(parts)
+        def spread_in(array):
+            return lax.all_to_all(array.reshape(n_grp, quarter, width), "grp", 0, 0, tiled=True)
+
+        def shuffle_in(parts):
+            return lax.all_to_all(parts, "tok", 0, 0, tiled=True).reshape(rows, width)
+
+        def shuffle_out(*arrays):
+            parts = [array.reshape(n_tok, quarter, width) for array in arrays]
+            results = [jnp.zeros_like(part) for part in parts]
             for turn_by in range(n_grp):
-                piece = lax.dynamic_index_in_dim(parts, g ^ t ^ turn_by, 0, keepdims=True)
-                piece = send(piece, lambda g, t, f: (g ^ t ^ turn_by, g, f))
-                result = lax.dynamic_update_slice_in_dim(result, piece, g ^ t ^ turn_by, 0)
-            return result.reshape(rows, width)
-
-        def shuffle_out(array):
-            parts = array.reshape(n_tok, quarter, width)
-            result = jnp.zeros_like(parts)
-            for turn_by in range(n_grp):
-                piece = lax.dynamic_index_in_dim(parts, g ^ t ^ turn_by, 0, keepdims=True)
-                piece = send(piece, lambda g, t, f: (t, g ^ t ^ turn_by, f))
-                result = lax.dynamic_update_slice_in_dim(result, piece, g ^ t ^ turn_by, 0)
-            return result.reshape(rows, width)
-
-
-        def layer_gather(array):
+                away = g ^ t ^ turn_by
+                pieces = [lax.dynamic_index_in_dim(part, away, 0, keepdims=True) for part in parts]
+                piece = send(
+                    jnp.concatenate(pieces, axis=1),
+                    lambda g, t, f, turn_by=turn_by: (t, g ^ t ^ turn_by, f),
+                )
+                for i, result in enumerate(results):
+                    results[i] = lax.dynamic_update_slice_in_dim(
+                        result, piece[:, i * quarter : (i + 1) * quarter], away, 0
+                    )
+            return [result.reshape(rows, width) for result in results]
+
+
+        def layer_pieces(array):
             half = array.shape[0] // 2
             by_x = send(array, cross(1))
             by_y = send(array, cross(2))
-            by_xy = jnp.concatenate(
-                [send(by_x[:half], cross(2)), send(by_y[half:], cross(1))], axis=0
-            )
-            mine = [array, by_x, by_y, by_xy]
+            return array, by_x, by_y, send(by_x[:half], cross(2)), send(by_y[half:], cross(1))
+
+        def layer_join(array, by_x, by_y, *by_xy):
+            mine = [array, by_x, by_y, jnp.concatenate(by_xy, axis=0)]
             return jnp.concatenate(mine + [send(part, sibling) for part in mine], axis=0)
 
-        def layer_sum(array):
-            half = array.shape[0] // 2
-            both = array[:half].astype(F32) + send(array[half:], sibling).astype(F32)
-            parts = both.astype(BF).reshape(n_grp, rows, array.shape[1])
-            return both[:rows] + sum(
-                send(parts[step], cross(step)).astype(F32) for step in range(1, n_grp)
-            )
-
-        xs = shuffle_in(hidden_in)
-        gain_one = lax.all_gather(first_gain, ("tok", "fs"), axis=0, tiled=True).astype(F32)
-        gain_two = lax.all_gather(second_gain, ("tok", "fs"), axis=0, tiled=True).astype(F32)
+        def layer_gather(array):
+            return layer_join(*layer_pieces(array))
+
+        def pair_sum(rows_of):
+            away = send(rows_of(1).astype(BF), sibling)
+            here = rows_of(0)
+            away = away.reshape(n_grp, rows, -1)
+            here = here.reshape(n_grp, rows, -1)
+            parts = [(here[step] + away[step].astype(F32)).astype(BF) for step in (3, 1, 2)]
+            return here[0], away[0], parts
+
+        def layer_send(sums, *earlier):
+            here, away, parts = sums
+            if earlier:
+                parts = [after(part, *earlier) for part in parts]
+            return here, away, [send(part, cross(step)) for part, step in zip(parts, (3, 1, 2))]
+
+        def layer_add(parts, beside=None):
+            here, away, got = parts
+            if beside is not None:
+                got = [after(part, beside) for part in got]
+            return here + away.astype(F32) + sum(part.astype(F32) for part in got)
+
+        def layer_sum(rows_of, beside=None):
+            return layer_add(layer_send(pair_sum(rows_of)), beside)
+
+        def halves(*arrays):
+            half = arrays[0].shape[0] // 2
+            return lambda which: [array[which * half : (which + 1) * half] for array in arrays]
+
+        extra = 8
+        gains_here = jnp.concatenate([first_gain, second_gain])
+        span = gains_here.shape[0]
+        gains_here = jnp.pad(gains_here[None, :], ((0, extra - 1), (0, width - span)))
+        hidden_parts = spread_in(hidden_in)
+        cotangent_parts = spread_in(after(cotangent, hidden_parts))
+        arrived = lax.all_to_all(
+            jnp.concatenate(
+                [hidden_parts, jnp.broadcast_to(gains_here[None], (n_tok, extra, width))], axis=1
+            ),
+            "tok",
+            0,
+            0,
+            tiled=True,
+        )
+        gains_mine = arrived[:, quarter, :span]
+        gains_other = send(gains_mine, sibling)
+        gains_all = jnp.stack(
+            [jnp.where(even, gains_mine, gains_other), jnp.where(even, gains_other, gains_mine)],
+            axis=1,
+        ).astype(F32).reshape(n_tok * n_fs, 2, -1)
+        gain_one = gains_all[:, 0].reshape(width)
+        gain_two = gains_all[:, 1].reshape(width)
+        starts = send(block_start, lambda g, t, f: (t, g, f))[0]
+        xs = arrived[:, :quarter].reshape(rows, width)
+        cotangent_here = shuffle_in(after(cotangent_parts, xs))
 
 
         head_span = width // n_grp
@@ -439,17 +500,49 @@
                 [jnp.where(even, mine, other), jnp.where(even, other, mine)], axis=0
             )
 
-        qkv_weight = lax.all_gather(
-            pair_rows(rank_columns(0), rank_columns(1)), "tok", axis=0, tiled=True
-        )
+        def gather_rows(array, *earlier):
+            array = after(array, *earlier)
+            return array, lax.all_gather(array, "tok", axis=0, tiled=True)
+
+        turn_one, qkv_weight = gather_rows(
+            pair_rows(rank_columns(0), rank_columns(1)), xs
+        )
+        ff_piece = ff_width // (ranks * n_tok)
+        ff_tall = -(-ff_piece // 64) * 64
+        ff_wide = ff_tall * n_tok
+
+        def ff_columns(side):
+            parts = [
+                lax.dynamic_slice_in_dim(
+                    weight, (step * n_fs + side) * n_grp * ff_piece + g * ff_piece, ff_piece, 1
+                )
+                for weight in (gate_weight, up_weight)
+                for step in range(n_tok)
+            ]
+            zeros = jnp.zeros((gate_weight.shape[0], ff_tall - ff_piece), BF)
+            return jnp.concatenate([item for part in parts for item in (part, zeros)], axis=1)
+
+        ff_inputs = (
+            pair_rows(ff_columns(0), ff_columns(1)),
+            jnp.pad(
+                lax.dynamic_slice_in_dim(down_weight, g * ff_piece, ff_piece, 0),
+                ((0, ff_tall - ff_piece), (0, 0)),
+            ),
+        )
+
+        hidden = after(xs, *ff_inputs).astype(F32)
+        scale_one = lax.rsqrt(jnp.mean(hidden * hidden, axis=1, keepdims=True) + EPS)
+        normed_one = hidden * scale_one
+        h_one = layer_gather((normed_one * gain_one[None, :]).astype(BF))
         out_rows = output_weight.shape[0] // n_grp
-        out_weight = lax.all_gather(
-            lax.dynamic_slice_in_dim(output_weight, g * out_rows, out_rows, 0),
-            "tok",
-            axis=0,
-            tiled=True,
-        )
-        out_weight = lax.all_to_all(out_weight, "grp", 0, 0, tiled=True)
+        turn_two, out_weight = gather_rows(
+            lax.dynamic_slice_in_dim(output_weight, g * out_rows, out_rows, 0), turn_one, h_one
+        )
+        grad_out = cotangent_here.astype(F32)
+        grad_m_pieces = layer_pieces(after((RESIDUAL * grad_out).astype(BF), h_one))
+        grad_m = layer_join(*grad_m_pieces)
+        raw = nn_dot(after(h_one, *grad_m_pieces[1:3]), qkv_weight)
+        out_weight = lax.all_to_all(after(out_weight, raw), "grp", 0, 0, tiled=True)
         half_head = HEAD_DIM // 2
         swapped = send(
             jnp.where(even, out_weight[own_span:], out_weight[:half_head]), sibling
@@ -464,37 +557,10 @@
             axis=0,
         )
 
-        ff_piece = ff_width // (ranks * n_tok)
-
-        def ff_columns(weight, side):
-            return jnp.concatenate(
-                [
-                    lax.dynamic_slice_in_dim(
-                        weight, (step * n_fs + side) * n_grp * ff_piece + g * ff_piece, ff_piece, 1
-                    )
-                    for step in range(n_tok)
-                ],
-                axis=1,
-            )
-
-        def ff_weight(weight):
-            return lax.all_gather(
-                pair_rows(ff_columns(weight, 0), ff_columns(weight, 1)), "tok", axis=0, tiled=True
-            )
-
-        gate_w = ff_weight(gate_weight)
-        up_w = ff_weight(up_weight)
-        down_w = lax.all_gather(
-            lax.dynamic_slice_in_dim(down_weight, g * ff_piece, ff_piece, 0),
-            "tok",
-            axis=0,
-            tiled=True,
-        )
-
-
-        starts = lax.dynamic_index_in_dim(
-            lax.all_gather(block_start, "grp", axis=0, tiled=True), t, 0, keepdims=False
-        )
+        _, ff_weight = gather_rows(ff_inputs[0], turn_two)
+        _, down_w = gather_rows(ff_inputs[1], ff_inputs[0], turn_two)
+
+
         number = jnp.arange(total // BLOCK, dtype=jnp.int32)
         prompt_blocks = PROMPT // BLOCK
         cont_blocks = CONT // BLOCK
@@ -528,56 +594,49 @@
         sine = jnp.where(lane[None, :] % HEAD_DIM < HEAD_DIM // 2, -jnp.sin(angle), jnp.sin(angle))
 
 
-        hidden = xs.astype(F32)
-        scale_one = lax.rsqrt(jnp.mean(hidden * hidden, axis=1, keepdims=True) + EPS)
-        normed_one = hidden * scale_one
-        h_one = layer_gather((normed_one * gain_one[None, :]).astype(BF))
-        raw = jnp.dot(h_one, qkv_weight, preferred_element_type=F32)
         attn_out, kept = attend(index, raw, cosine, sine)
-        branch = layer_sum(jnp.dot(attn_out, out_weight, preferred_element_type=F32).astype(BF))
+        pick = halves(attn_out)
+        branch = layer_sum(lambda side, pick=pick: nn_dot(pick(side)[0], out_weight), grad_m)
         second_in = hidden + RESIDUAL * branch
         scale_two = lax.rsqrt(jnp.mean(second_in * second_in, axis=1, keepdims=True) + EPS)
         normed_two = second_in * scale_two
         h_two = layer_gather((normed_two * gain_two[None, :]).astype(BF))
-        gate = jnp.dot(h_two, gate_w, preferred_element_type=F32)
-        up_val = jnp.dot(h_two, up_w, preferred_element_type=F32)
+        both = nn_dot(h_two, ff_weight)
+        gate = both[:, :ff_wide]
+        up_val = both[:, ff_wide:]
         sigma = jax.nn.sigmoid(gate)
         silu = gate * sigma
         act = (silu * up_val).astype(BF)
-        feed = layer_sum(jnp.dot(act, down_w, preferred_element_type=F32).astype(BF))
-        layer_output = shuffle_out((second_in + RESIDUAL * feed).astype(BF))
-
-
-        grad_out = shuffle_in(cotangent).astype(F32)
-        grad_m = layer_gather((RESIDUAL * grad_out).astype(BF))
-        grad_act = nt_dot(grad_m, down_w)
-        down_grad = lax.psum_scatter(
-            tn_dot(act, grad_m).astype(BF).reshape(n_tok, ff_piece, width),
-            "tok",
-            scatter_dimension=0,
-            tiled=True,
-        )[0]
-        down_grad = send(
-            down_grad, lambda g, t, f: (t, (n_grp * f + g) // n_fs, (n_grp * f + g) % n_fs)
-        ).astype(F32)
-        grad_gate = (grad_act * up_val * (sigma * (1.0 + gate * (1.0 - sigma)))).astype(BF)
-        grad_up = (grad_act * silu).astype(BF)
-
-        def to_rows(grad):
+
+
+        down_local = tn_dot(act, grad_m).astype(BF).reshape(n_tok, ff_tall, width)
+        grad_act = nt_dot(after(grad_m, down_local), down_w)
+        grad_both = jnp.concatenate(
+            [
+                (grad_act * up_val * (sigma * (1.0 + gate * (1.0 - sigma)))).astype(BF),
+                (grad_act * silu).astype(BF),
+            ],
+            axis=1,
+        )
+        def spread_rows(grad):
             columns = grad.shape[1]
             grad = grad.astype(BF).reshape(n_grp, n_tok, width // (n_grp * n_tok), columns)
-            grad = grad.transpose(1, 0, 2, 3).reshape(n_tok, width // n_tok, columns)
+            return grad.transpose(1, 0, 2, 3).reshape(n_tok, width // n_tok, columns)
+
+        def sum_rows(grad):
             grad = lax.psum_scatter(grad, "tok", scatter_dimension=0, tiled=True)
-            grad = grad.reshape(ranks, width // (ranks * n_tok), columns)
+            return grad.reshape(ranks, width // (ranks * n_tok), grad.shape[2])
+
+        def to_owners(grad):
             return lax.all_to_all(grad, LAYER, 0, 0, tiled=True)
 
-        def ff_grad(grad):
-            got = to_rows(grad).reshape(n_grp, n_fs, -1, n_tok, ff_piece)
-            return got.transpose(2, 3, 1, 0, 4).reshape(-1, ff_width).astype(F32)
-
-        gate_grad = ff_grad(tn_dot(h_two, grad_gate))
-        up_grad = ff_grad(tn_dot(h_two, grad_up))
-        grad_h2 = layer_sum((nt_dot(grad_gate, gate_w) + nt_dot(grad_up, up_w)).astype(BF))
+        pick = halves(grad_both)
+        parts = layer_send(pair_sum(lambda side, pick=pick: nt_dot(pick(side)[0], ff_weight)))
+        ff_local = spread_rows(tn_dot(h_two, after(grad_both, parts[0])))
+        grad_h2 = layer_add(parts, ff_local)
+        down_rows = lax.psum_scatter(down_local, "tok", scatter_dimension=0, tiled=True)
+        down_rows = down_rows[0, :ff_piece]
+        ff_rows = sum_rows(ff_local)
         gain_two_sum = jnp.sum(grad_h2 * normed_two, axis=0)
         pulled = grad_h2 * gain_two[None, :]
         grad_second = (
@@ -585,28 +644,49 @@
             + scale_two * pulled
             - scale_two**3 * second_in * jnp.mean(pulled * second_in, axis=1, keepdims=True)
         )
-        grad_z = layer_gather((RESIDUAL * grad_second).astype(BF))
+        grad_z_here = (RESIDUAL * grad_second).astype(BF)
+        grad_z = layer_gather(grad_z_here)
+        pick = halves(after(act, grad_z_here))
+        feed_sums = pair_sum(lambda side, pick=pick: nn_dot(pick(side)[0], down_w))
         grad_attn = nt_dot(grad_z, out_weight).astype(BF)
+        feed_parts = layer_send(feed_sums, grad_z)
         out_full = tn_dot(attn_out, grad_z)
         shared = out_full[own_span : own_span + HEAD_DIM]
-        got = send(
+        swapped = send(
             jnp.where(even, shared[half_head:], shared[:half_head]).astype(BF), sibling
         ).astype(F32)
-        kept_half = jnp.where(even, shared[:half_head], shared[half_head:]) + got
+        kept_half = jnp.where(even, shared[:half_head], shared[half_head:]) + swapped
         out_full = jnp.where(
             even,
             jnp.concatenate([out_full[:own_span], kept_half], axis=0),
             jnp.concatenate([kept_half, out_full[:own_span]], axis=0),
         )
-        output_grad = lax.psum_scatter(
-            out_full.astype(BF).reshape(n_tok, -1, width), "tok", scatter_dimension=0, tiled=True
-        )[0]
-        output_grad = send(
-            output_grad, lambda g, t, f: (g, (n_tok * f + t) // n_fs, (n_tok * f + t) % n_fs)
-        ).astype(F32)
-
-        grads = attend_back(index, kept, grad_attn, cosine, sine, qkv_weight.shape[1])
-        grad_h1 = layer_sum(nt_dot(grads, qkv_weight).astype(BF))
+        out_full = out_full.astype(BF).reshape(n_tok, -1, width)
+        output_grad = lax.psum_scatter(out_full, "tok", scatter_dimension=0, tiled=True)
+
+        grad_attn = after(grad_attn, out_full, down_rows)
+        grads = attend_back(0, 3, index, kept, grad_attn, cosine, sine, qkv_weight.shape[1])
+        grads = after(grads, ff_rows)
+        qkv_local = spread_rows(tn_dot(h_one, grads))
+        qkv_rows = sum_rows(qkv_local)
+        got = to_owners(after(ff_rows, grads))
+        down_grad = send(
+            after(down_rows, grads),
+            lambda g, t, f: (t, (n_grp * f + g) // n_fs, (n_grp * f + g) % n_fs),
+        )
+        pick = halves(after(grads, qkv_local, got, output_grad, down_grad))
+        parts = layer_send(pair_sum(lambda side, pick=pick: nt_dot(pick(side)[0], qkv_weight)))
+        feed = layer_add(feed_parts, parts[0])
+        layer_output = (second_in + RESIDUAL * feed).astype(BF)
+        got = after(got, layer_output).reshape(n_grp, n_fs, -1, 2, n_tok, ff_tall)
+        gate_grad, up_grad = (
+            got[:, :, :, which, :, :ff_piece]
+            .transpose(2, 3, 1, 0, 4)
+            .reshape(-1, ff_width)
+            .astype(F32)
+            for which in range(2)
+        )
+        grad_h1 = layer_add(parts, (gate_grad, up_grad))
         gain_one_sum = jnp.sum(grad_h1 * normed_one, axis=0)
         pulled = grad_h1 * gain_one[None, :]
         input_grad = (
@@ -614,8 +694,13 @@
             + scale_one * pulled
             - scale_one**3 * hidden * jnp.mean(pulled * hidden, axis=1, keepdims=True)
         )
-        input_grad = shuffle_out(input_grad.astype(BF)).astype(F32)
-        got = to_rows(tn_dot(h_one, grads)).astype(F32)
+        input_grad = after(input_grad.astype(BF), qkv_rows)
+        layer_output, input_grad = shuffle_out(layer_output, input_grad)
+        input_grad = input_grad.astype(F32)
+        output_grad = send(
+            output_grad[0], lambda g, t, f: (g, (n_tok * f + t) // n_fs, (n_tok * f + t) % n_fs)
+        ).astype(F32)
+        got = to_owners(qkv_rows).astype(F32)
         own_rows = got.shape[1]
         got = got.reshape(n_grp, n_fs, own_rows, got.shape[2])
 
@@ -644,7 +729,7 @@
             output_grad,
             gate_grad,
             up_grad,
-            down_grad,
+            down_grad.astype(F32),
             gains[:, 0],
             gains[:, 1],
         )

time: 1250 us -> 1060 us (0.85)
  the two profiles are of different devices: /device:TPU:1 before, /device:TPU:5 now
where the time goes in v2:
time: 1060 us; the launch traced here: 1050 us
  waiting for transfers between devices  349 us (33%)
  matrix products  176 us (17%)
  local copies, waits for them, and re-layouts  161 us (15%)
  starting transfers between devices  134 us (13%)
  other arithmetic  107 us (10%)
  Pallas kernels  103 us (10%)
  between operations  15.6 us (1%)
    ppermute x60, waiting for transfers between devices, send(): return lax.ppermute(array, ALL, permutation(move))  286 us
    ppermute x60, starting transfers between devices, send(): return lax.ppermute(array, ALL, permutation(move))  99.3 us
    unnamed x162, local copies, waits for them, and re-layouts  68.6 us
    dot_general x6, matrix products, nt_dot(): lax.dot_general(left, right, (((1,), (1,)), ((), ())), preferred_element_...  65.6 us
    pallas_call x1, Pallas kernels, attend_back(): pl.pallas_call(functools.partial(attend_back_kernel, first), grid_spec=pl...  62.4 us
    dot_general x6, matrix products, nn_dot(): lax.dot_general(left, right, (((1,), (0,)), ((), ())), preferred_element_...  57.4 us
    dot_general x4, matrix products, tn_dot(): lax.dot_general(left, right, (((0,), (0,)), ((), ())), preferred_element_...  53 us
    pallas_call x1, Pallas kernels, attend(): pl.pallas_call(attend_kernel, grid_spec=pltpu.PrefetchScalarGridSpec(num_...  41 us
  transfers between devices with their start and end apart: 76, of which 29 were waited for; matrix products, arithmetic and copies ran while one was open for 35% of the time, Pallas kernels for 10%

profile of v2, /device:TPU:5, one launch (start us, length us, event | category | flops | bytes accessed | tf_op | source)
XLA Modules:
  0.0 1045.7 jit_solution(9251160672133686371)
XLA Ops:
  9.7 4.3 all-to-all-start
  20.1 8.5 all-to-all-done.refs_1_
  31.0 4.5 all-to-all-start.1
  66.8 4.7 all-to-all-start.2
  77.8 7.2 all-to-all-done.2.refs_0_
  100.1 21.5 %collective-permute-done.3 = bf16[256,2304]{1,0:T(8,128)(2,1)} collective-permute-done((bf16[256,2304]{1,0:T(8,128)(2,1)}, bf16[256,2304]{1,0:T(8,128)(2,1)}, u32[]{:S(2)}, u32[]{:S(2)}) %collective-permute-start.3) | collective-permute-done | bytes 1179680 | tf_op jit(solution)/shard_map/ppermute | solution.py:360
  131.0 28.5 %all-to-all-done.3 = bf16[4,64,2304]{2,1,0:T(8,128)(2,1)S(1)} async-done(((bf16[4,64,2304]{2,1,0:T(8,128)(2,1)}), bf16[4,64,2304]{2,1,0:T(8,128)(2,1)S(1)}, u32[]{:S(2)}, u32[]{:S(2)}) %all-to-all-start.3) | async-done | bytes 1179680 | tf_op jit(solution)/shard_map/all_to_all | solution.py:395
  182.7 8.0 copy.255.refs_0_
  190.7 11.9 %collective-permute-done.11.refs_1_ = bf16[256,2304]{1,0:T(8,128)(2,1)} collective-permute-done((bf16[256,2304]{1,0:T(8,128)(2,1)}, bf16[256,2304]{1,0:T(8,128)(2,1)}, u32[]{:S(2)}, u32[]{:S(2)}) %collective-permute-start.11) | collective-permute-done | bytes 1179680 | tf_op jit(solution)/shard_map/ppermute | solution.py:360
  203.6 15.9 %fusion.68.raw_ref.refs_1_ = f32[2048,960]{1,0:T(8,128)} fusion(bf16[2048,2304]{1,0:T(8,128)(2,1)} %after.39, bf16[2304,960]{1,0:T(8,128)(2,1)} %all-gather.5.cloned.1.call-done), kind=kOutput, calls=%fused_computation.296 | convolution fusion | flops 9059696640 | bytes 21725184 | tf_op jit(solution)/shard_map/dot_general | solution.py:94
  219.5 6.2 all-gather.7.cloned.1.call-done.refs_0_
  225.7 4.5 all-to-all-start.4
  231.4 41.0 %attend.1 = (bf16[2048,384]{1,0:T(8,128)(2,1)S(1)}, bf16[3,2048,384]{2,1,0:T(8,128)(2,1)S(1)}) custom-call(s32[33]{0:T(128)S(1)} %pad_add_fusion.index_ref, f32[2048,960]{1,0:T(8,128)} %fusion.68.raw_ref.refs_1_, f32[1280,128]{1,0:T(8,128)S(1)} %get-tuple-element.121.cos_ref, f32[1280,128]{1,0:T(8,128)S(1)} %get-tuple-element.120.sin_ref), custom_call_target="tpu_custom_call" | custom-call | bytes 1048576 | tf_op jit(solution)/shard_map/attend/pallas_call | solution.py:179
  280.8 4.8 convolution_convert_fusion.3
  295.6 9.3 collective-permute-done.17
  310.4 7.2 fusion.33
  324.8 21.1 %collective-permute-done.16.refs_0_ = bf16[256,2304]{1,0:T(8,128)(2,1)S(1)} collective-permute-done((bf16[256,2304]{1,0:T(8,128)(2,1)S(1)}, bf16[256,2304]{1,0:T(8,128)(2,1)S(1)}, u32[]{:S(2)}, u32[]{:S(2)}) %collective-permute-start.16) | collective-permute-done | bytes 1179680 | tf_op jit(solution)/shard_map/ppermute | solution.py:360
  346.9 25.0 %collective-permute-done.23.refs_0_ = bf16[256,2304]{1,0:T(8,128)(2,1)} collective-permute-done((bf16[256,2304]{1,0:T(8,128)(2,1)}, bf16[256,2304]{1,0:T(8,128)(2,1)}, u32[]{:S(2)}, u32[]{:S(2)}) %collective-permute-start.23) | collective-permute-done | bytes 1179680 | tf_op jit(solution)/shard_map/ppermute | solution.py:360
  373.1 4.2 multiply_reduce_fusion.2
  382.6 24.1 %collective-permute-done.25 = bf16[256,2304]{1,0:T(8,128)(2,1)} collective-permute-done((bf16[256,2304]{1,0:T(8,128)(2,1)}, bf16[256,2304]{1,0:T(8,128)(2,1)}, u32[]{:S(2)}, u32[]{:S(2)}) %collective-permute-start.25) | collective-permute-done | bytes 1179680 | tf_op jit(solution)/shard_map/ppermute | solution.py:360
  415.1 6.0 collective-permute-done.27
  430.5 19.5 %fusion.69 = f32[2048,1536]{1,0:T(8,128)S(1)} fusion(bf16[2048,2304]{1,0:T(8,128)(2,1)} %constant_dynamic-update-slice_fusion.18, bf16[2304,1536]{1,0:T(8,128)(2,1)} %all-gather.9.cloned.1.call-done), kind=kOutput, calls=%fused_computation.297 | convolution fusion | flops 14495514624 | bytes 29097984 | tf_op jit(solution)/shard_map/dot_general | solution.py:94
  450.0 4.6 copy-done.17
  456.7 14.0 %convolution_convert_fusion.6 = bf16[768,2304]{1,0:T(8,128)(2,1)} fusion(bf16[2048,768]{1,0:T(8,128)(2,1)S(1)} %multiply_convert_fusion.2.refs_0_, bf16[2048,2304]{1,0:T(8,128)(2,1)} %constant_dynamic-update-slice_fusion.9.refs_1_.refs_0_), kind=kOutput, calls=%fused_computation.16 | convolution fusion | flops 7249526784 | bytes 16121856 | tf_op jit(solution)/shard_map/dot_general | solution.py:90
  470.7 15.3 %multiply_convert_fusion = (bf16[2048,768]{1,0:T(8,128)(2,1)S(1)}, bf16[2048,768]{1,0:T(8,128)(2,1)S(1)}) fusion(f32[2048,1536]{1,0:T(8,128)} %copy-done.17, bf16[2048,2304]{1,0:T(8,128)(2,1)} %after.47, bf16[768,2304]{1,0:T(8,128)(2,1)} %all-gather.11.cloned.1.call-done), kind=kOutput, calls=%fused_computation.6 | convolution fusion | flops 7268204544 | bytes 31850496 | tf_op jit(solution)/shard_map/dot_general | solution.py:86
  486.0 14.4 %convolution_convert_fusion.2 = bf16[1024,2304]{1,0:T(8,128)(2,1)} fusion(bf16[2304,1536]{1,0:T(8,128)(2,1)} %all-gather.9.cloned.1.call-done, bf16[2048,768]{1,0:T(8,128)(2,1)S(1)} %get-tuple-element.34, bf16[2048,768]{1,0:T(8,128)(2,1)S(1)} %get-tuple-element.33), kind=kOutput, calls=%fused_computation.12 | convolution fusion | flops 7256408064 | bytes 18087936 | tf_op jit(solution)/shard_map/dot_general | solution.py:86
  500.7 6.5 pad_maximum_fusion.refs_0_
  507.2 9.6 fusion.2
  516.8 7.6 fusion.30
  524.5 19.1 %convolution_convert_fusion = bf16[2304,1536]{1,0:T(8,128)(2,1)S(1)} fusion(bf16[2048,2304]{1,0:T(8,128)(2,1)} %constant_dynamic-update-slice_fusion.18, bf16[2048,1536]{1,0:T(8,128)(2,1)} %after.49), kind=kOutput, calls=%fused_computation | convolution fusion | flops 14499053568 | bytes 22806528 | tf_op jit(solution)/shard_map/dot_general | solution.py:90
  550.3 25.7 %collective-permute-done.34.refs_0_ = bf16[256,2304]{1,0:T(8,128)(2,1)} collective-permute-done((bf16[256,2304]{1,0:T(8,128)(2,1)}, bf16[256,2304]{1,0:T(8,128)(2,1)}, u32[]{:S(2)}, u32[]{:S(2)}) %collective-permute-start.34) | collective-permute-done | bytes 1179680 | tf_op jit(solution)/shard_map/ppermute | solution.py:360
  576.0 24.7 %collective-permute-done.35.refs_0_ = bf16[256,2304]{1,0:T(8,128)(2,1)} collective-permute-done((bf16[256,2304]{1,0:T(8,128)(2,1)}, bf16[256,2304]{1,0:T(8,128)(2,1)}, u32[]{:S(2)}, u32[]{:S(2)}) %collective-permute-start.35) | collective-permute-done | bytes 1179680 | tf_op jit(solution)/shard_map/ppermute | solution.py:360
  603.1 5.2 multiply_reduce_fusion
  614.2 8.6 convolution_convert_fusion.1
  622.8 16.0 %collective-permute-done.38 = bf16[256,2304]{1,0:T(8,128)(2,1)S(1)} collective-permute-done((bf16[256,2304]{1,0:T(8,128)(2,1)}, bf16[256,2304]{1,0:T(8,128)(2,1)S(1)}, u32[]{:S(2)}, u32[]{:S(2)}) %collective-permute-start.38) | collective-permute-done | bytes 1179680 | tf_op jit(solution)/shard_map/ppermute | solution.py:360
  645.2 7.7 collective-permute-done.40
  659.4 4.1 fusion.70
  672.1 8.8 convolution_convert_fusion.7.refs_0_
  682.5 62.4 %attend_back.1.refs_0_ = bf16[2048,960]{1,0:T(8,128)(2,1)} custom-call(s32[33]{0:T(128)S(1)} %pad_add_fusion.index_ref, bf16[3,2048,384]{2,1,0:T(8,128)(2,1)} %copy-done.5, bf16[2048,384]{1,0:T(8,128)(2,1)S(1)} %copy-done.2, f32[1280,128]{1,0:T(8,128)S(1)} %get-tuple-element.121.cos_ref, f32[1280,128]{1,0:T(8,128)S(1)} %get-tuple-element.120.sin_ref), custom_call_target="tpu_custom_call" | custom-call | bytes 1048576 | tf_op jit(solution)/shard_map/attend_back/pallas_call | solution.py:304
  746.0 3.9 collective-permute-start.48
  749.9 3.8 all-to-all-start.5
  753.7 15.9 %convolution_convert_fusion.5 = bf16[2304,960]{0,1:T(8,128)(2,1)} fusion(bf16[2048,2304]{1,0:T(8,128)(2,1)} %constant_dynamic-update-slice_fusion.refs_1_.refs_2_, bf16[2048,960]{1,0:T(8,128)(2,1)} %after.56.refs_1_.refs_0_), kind=kOutput, calls=%fused_computation.15 | convolution fusion | flops 9061908480 | bytes 17793024 | tf_op jit(solution)/shard_map/dot_general | solution.py:90
  769.6 6.6 copy.188
  776.2 5.2 copy.189
  781.4 6.6 all-to-all-done.5.refs_2_.refs_0_
  789.2 9.3 convolution_convert_fusion.4
  798.5 3.7 collective-permute-start.51
  802.3 5.8 fusion.40
  811.0 4.6 fusion.23
  815.6 9.1 collective-permute-start.46
  828.8 8.1 fusion.37
  837.0 7.6 fusion.20
  844.6 17.5 %collective-permute-start.52 = (bf16[256,2304]{1,0:T(8,128)(2,1)}, bf16[256,2304]{1,0:T(8,128)(2,1)}, u32[]{:S(2)}, u32[]{:S(2)}) collective-permute-start(bf16[256,2304]{1,0:T(8,128)(2,1)} %get-tuple-element.35), channel_id=1, source_target_pairs={{0,24},{1,25},{2,26},{3,27},{4,28},{5,29},{6,30},{7,31},{8,16},{9,... | collective-permute-start | bytes 3538952 | tf_op jit(solution)/shard_map/ppermute | solution.py:360
  863.1 13.5 %collective-permute-done.49.refs_0_ = bf16[256,2304]{1,0:T(8,128)(2,1)S(1)} collective-permute-done((bf16[256,2304]{1,0:T(8,128)(2,1)}, bf16[256,2304]{1,0:T(8,128)(2,1)S(1)}, u32[]{:S(2)}, u32[]{:S(2)}) %collective-permute-start.49) | collective-permute-done | bytes 1179680 | tf_op jit(solution)/shard_map/ppermute | solution.py:360
  879.3 5.0 fusion.27.refs_1_
  884.2 5.2 reshape.341
  902.0 25.3 %collective-permute-done.53.refs_0_ = bf16[256,2304]{1,0:T(8,128)(2,1)} collective-permute-done((bf16[256,2304]{1,0:T(8,128)(2,1)}, bf16[256,2304]{1,0:T(8,128)(2,1)}, u32[]{:S(2)}, u32[]{:S(2)}) %collective-permute-start.53) | collective-permute-done | bytes 1179680 | tf_op jit(solution)/shard_map/ppermute | solution.py:360
  928.5 5.5 fusion.10
  939.4 4.1 fusion.16.refs_0_
  946.3 5.0 all-to-all-start.6
  956.0 4.2 collective-permute-start.55
  962.3 7.0 collective-permute-start.56
  969.3 29.5 %collective-permute-done.55 = bf16[1,128,2304]{2,1,0:T(8,128)(2,1)S(1)} collective-permute-done((bf16[1,128,2304]{2,1,0:T(8,128)(2,1)S(1)}, bf16[1,128,2304]{2,1,0:T(8,128)(2,1)S(1)}, u32[]{:S(2)}, u32[]{:S(2)}) %collective-permute-start.55) | collective-permute-done | bytes 589856 | tf_op jit(solution)/shard_map/ppermute | solution.py:360
  999.0 19.1 %collective-permute-done.56 = bf16[1,128,2304]{2,1,0:T(8,128)(2,1)S(1)} collective-permute-done((bf16[1,128,2304]{2,1,0:T(8,128)(2,1)S(1)}, bf16[1,128,2304]{2,1,0:T(8,128)(2,1)S(1)}, u32[]{:S(2)}, u32[]{:S(2)}) %collective-permute-start.56) | collective-permute-done | bytes 589856 | tf_op jit(solution)/shard_map/ppermute | solution.py:360
  (447 shorter events, 257.1 us)
Async XLA Ops:
  9.7 18.9 %all-to-all-start = ((bf16[4,64,2304]{2,1,0:T(8,128)(2,1)}), bf16[4,64,2304]{2,1,0:T(8,128)(2,1)}, u32[]{:S(2)}, u32[]{:S(2)}) async-start(bf16[4,64,2304]{2,1,0:T(8,128)(2,1)} %bitcast.187), calls=%async_computation | async-start | bytes 2359296 | tf_op jit(solution)/shard_map/all_to_all | solution.py:392
  31.0 35.8 %all-to-all-start.1 = ((bf16[4,72,2304]{2,1,0:T(8,128)(2,1)}), bf16[4,72,2304]{2,1,0:T(8,128)(2,1)}, u32[]{:S(2)}, u32[]{:S(2)}) async-start(bf16[4,72,2304]{2,1,0:T(8,128)(2,1)} %pad_maximum_fusion.2), calls=%async_computation.1 | async-start | bytes 2654208 | tf_op jit(solution)/shard_map/all_to_all | solution.py:460
  44.1 17.9 %collective-permute-start.13 = (bf16[288,960]{1,0:T(8,128)(2,1)}, bf16[288,960]{1,0:T(8,128)(2,1)}, u32[]{:S(2)}, u32[]{:S(2)}) collective-permute-start(bf16[288,960]{1,0:T(8,128)(2,1)} %broadcast_select_fusion.6), channel_id=1, source_target_pairs={{0,1},{1,0},{2,3},{3,2},{4,5},{5,4},{6,7},{7,6},{8,9},{9,8},{10,11... | collective-permute-start | bytes 1658888 | tf_op jit(solution)/shard_map/ppermute | solution.py:360
  66.8 18.2 %all-to-all-start.2 = ((bf16[4,64,2304]{2,1,0:T(8,128)(2,1)}), bf16[4,64,2304]{2,1,0:T(8,128)(2,1)}, u32[]{:S(2)}, u32[]{:S(2)}) async-start(bf16[4,64,2304]{2,1,0:T(8,128)(2,1)} %bitcast.176), calls=%async_computation.2 | async-start | bytes 2359296 | tf_op jit(solution)/shard_map/all_to_all | solution.py:392
  71.5 132.1 %all-gather.5.cloned.1.call-start = ((), (), s32[]{:S(2)}) async-start(), calls=%async_computation.12 | async-start | bytes 5898240 | tf_op jit(solution)/shard_map/all_gather | solution.py:505
  94.1 27.5 %collective-permute-start.3 = (bf16[256,2304]{1,0:T(8,128)(2,1)}, bf16[256,2304]{1,0:T(8,128)(2,1)}, u32[]{:S(2)}, u32[]{:S(2)}) collective-permute-start(bf16[256,2304]{1,0:T(8,128)(2,1)} %get-tuple-element.32), channel_id=1, source_target_pairs={{0,8},{1,9},{2,10},{3,11},{4,12},{5,13},{6,14},{7,15},{8,0},{9,1},... | collective-permute-start | bytes 3538952 | tf_op jit(solution)/shard_map/ppermute | solution.py:360
  94.4 29.4 %collective-permute-start.4 = (bf16[256,2304]{1,0:T(8,128)(2,1)}, bf16[256,2304]{1,0:T(8,128)(2,1)S(1)}, u32[]{:S(2)}, u32[]{:S(2)}) collective-permute-start(bf16[256,2304]{1,0:T(8,128)(2,1)} %get-tuple-element.32), channel_id=1, source_target_pairs={{0,16},{1,17},{2,18},{3,19},{4,20},{5,21},{6,22},{7,23},{8,24},{9,... | collective-permute-start | bytes 3538952 | tf_op jit(solution)/shard_map/ppermute | solution.py:360
  95.5 64.0 %all-to-all-start.3 = ((bf16[4,64,2304]{2,1,0:T(8,128)(2,1)}), bf16[4,64,2304]{2,1,0:T(8,128)(2,1)S(1)}, u32[]{:S(2)}, u32[]{:S(2)}) async-start(bf16[4,64,2304]{2,1,0:T(8,128)(2,1)} %after.37), calls=%async_computation.3 | async-start | bytes 2359296 | tf_op jit(solution)/shard_map/all_to_all | solution.py:395
  99.1 126.6 %all-gather.7.cloned.1.call-start = ((), (), s32[]{:S(2)}) async-start(), calls=%async_computation.13 | async-start | bytes 1658880 | tf_op jit(solution)/shard_map/all_gather | solution.py:505
  99.1 67.3 %collective-permute-start.7 = (bf16[256,2304]{1,0:T(8,128)(2,1)}, bf16[256,2304]{1,0:T(8,128)(2,1)}, u32[]{:S(2)}, u32[]{:S(2)}) collective-permute-start(bf16[256,2304]{1,0:T(8,128)(2,1)} %get-tuple-element.32), channel_id=1, source_target_pairs={{0,1},{1,0},{2,3},{3,2},{4,5},{5,4},{6,7},{7,6},{8,9},{9,8},{10,11... | collective-permute-start | bytes 3538952 | tf_op jit(solution)/shard_map/ppermute | solution.py:360
  123.5 37.4 %collective-permute-start.5 = (bf16[128,2304]{1,0:T(8,128)(2,1)}, bf16[128,2304]{1,0:T(8,128)(2,1)S(1)}, u32[]{:S(2)}, u32[]{:S(2)}) collective-permute-start(bf16[128,2304]{1,0:T(8,128)(2,1)} %slice.474), channel_id=1, source_target_pairs={{0,16},{1,17},{2,18},{3,19},{4,20},{5,21},{6,22},{7,23},{8,24},{9,... | collective-permute-start | bytes 1769480 | tf_op jit(solution)/shard_map/ppermute | solution.py:360
  124.6 36.4 %collective-permute-start.6 = (bf16[128,2304]{1,0:T(8,128)(2,1)}, bf16[128,2304]{1,0:T(8,128)(2,1)}, u32[]{:S(2)}, u32[]{:S(2)}) collective-permute-start(bf16[128,2304]{1,0:T(8,128)(2,1)} %slice.475), channel_id=1, source_target_pairs={{0,8},{1,9},{2,10},{3,11},{4,12},{5,13},{6,14},{7,15},{8,0},{9,1},... | collective-permute-start | bytes 1769480 | tf_op jit(solution)/shard_map/ppermute | solution.py:360
  125.8 43.0 %collective-permute-start.8 = (bf16[256,2304]{1,0:T(8,128)(2,1)}, bf16[256,2304]{1,0:T(8,128)(2,1)}, u32[]{:S(2)}, u32[]{:S(2)}) collective-permute-start(bf16[256,2304]{1,0:T(8,128)(2,1)} %collective-permute-done.3), channel_id=1, source_target_pairs={{0,1},{1,0},{2,3},{3,2},{4,5},{5,4},{6,7},{7,6},{8,9},{9,8},{10,11... | collective-permute-start | bytes 3538952 | tf_op jit(solution)/shard_map/ppermute | solution.py:360
  127.5 43.6 %collective-permute-start.9 = (bf16[256,2304]{1,0:T(8,128)(2,1)S(1)}, bf16[256,2304]{1,0:T(8,128)(2,1)}, u32[]{:S(2)}, u32[]{:S(2)}) collective-permute-start(bf16[256,2304]{1,0:T(8,128)(2,1)S(1)} %collective-permute-done.4), channel_id=1, source_target_pairs={{0,1},{1,0},{2,3},{3,2},{4,5},{5,4},{6,7},{7,6},{8,9},{9,8},{10,11... | collective-permute-start | bytes 3538952 | tf_op jit(solution)/shard_map/ppermute | solution.py:360
  174.7 27.9 %collective-permute-start.11 = (bf16[256,2304]{1,0:T(8,128)(2,1)}, bf16[256,2304]{1,0:T(8,128)(2,1)}, u32[]{:S(2)}, u32[]{:S(2)}) collective-permute-start(bf16[256,2304]{1,0:T(8,128)(2,1)} %after.38), channel_id=1, source_target_pairs={{0,8},{1,9},{2,10},{3,11},{4,12},{5,13},{6,14},{7,15},{8,0},{9,1},... | collective-permute-start | bytes 3538952 | tf_op jit(solution)/shard_map/ppermute | solution.py:360
  175.0 27.6 %collective-permute-start.12 = (bf16[256,2304]{1,0:T(8,128)(2,1)}, bf16[256,2304]{1,0:T(8,128)(2,1)S(1)}, u32[]{:S(2)}, u32[]{:S(2)}) collective-permute-start(bf16[256,2304]{1,0:T(8,128)(2,1)} %after.38), channel_id=1, source_target_pairs={{0,16},{1,17},{2,18},{3,19},{4,20},{5,21},{6,22},{7,23},{8,24},{9,... | collective-permute-start | bytes 3538952 | tf_op jit(solution)/shard_map/ppermute | solution.py:360
  176.1 54.0 %collective-permute-start.1 = (s32[1,16]{1,0:T(1,128)S(1)}, s32[1,16]{1,0:T(1,128)S(1)}, u32[]{:S(2)}, u32[]{:S(2)}) collective-permute-start(s32[1,16]{1,0:T(1,128)S(1)} %copy-done.64), channel_id=1, source_target_pairs={{0,0},{1,1},{2,8},{3,9},{4,16},{5,17},{6,24},{7,25},{8,2},{9,3},{1... | collective-permute-start | bytes 200 | tf_op jit(solution)/shard_map/ppermute | solution.py:360
  225.7 48.8 %all-to-all-start.4 = ((bf16[4,72,2304]{2,1,0:T(8,128)(2,1)}), bf16[4,72,2304]{2,1,0:T(8,128)(2,1)}, u32[]{:S(2)}, u32[]{:S(2)}) async-start(bf16[4,72,2304]{2,1,0:T(8,128)(2,1)} %bitcast.180), calls=%async_computation.4 | async-start | bytes 2654208 | tf_op jit(solution)/shard_map/all_to_all | solution.py:545
  230.6 199.8 %all-gather.9.cloned.1.call-start = ((), (), s32[]{:S(2)}) async-start(), calls=%async_computation.14 | async-start | bytes 8847360 | tf_op jit(solution)/shard_map/all_gather | solution.py:505
  231.3 239.3 %all-gather.11.cloned.1.call-start = ((), (), s32[]{:S(2)}) async-start(), calls=%async_computation.15 | async-start | bytes 4423680 | tf_op jit(solution)/shard_map/all_gather | solution.py:505
  285.7 24.7 %collective-permute-start.15 = (bf16[1024,2304]{1,0:T(8,128)(2,1)}, bf16[1024,2304]{1,0:T(8,128)(2,1)}, u32[]{:S(2)}, u32[]{:S(2)}) collective-permute-start(bf16[1024,2304]{1,0:T(8,128)(2,1)} %convolution_convert_fusion.3), channel_id=1, source_target_pairs={{0,1},{1,0},{2,3},{3,2},{4,5},{5,4},{6,7},{7,6},{8,9},{9,8},{10,11... | collective-permute-start | bytes 14155784 | tf_op jit(solution)/shard_map/ppermute | solution.py:360
  285.8 34.3 %collective-permute-start.19 = (bf16[256,2304]{1,0:T(8,128)(2,1)}, bf16[256,2304]{1,0:T(8,128)(2,1)S(1)}, u32[]{:S(2)}, u32[]{:S(2)}) collective-permute-start(bf16[256,2304]{1,0:T(8,128)(2,1)} %after.38), channel_id=1, source_target_pairs={{0,1},{1,0},{2,3},{3,2},{4,5},{5,4},{6,7},{7,6},{8,9},{9,8},{10,11... | collective-permute-start | bytes 3538952 | tf_op jit(solution)/shard_map/ppermute | solution.py:360
  289.8 15.1 %collective-permute-start.17 = (bf16[128,2304]{1,0:T(8,128)(2,1)S(1)}, bf16[128,2304]{1,0:T(8,128)(2,1)S(1)}, u32[]{:S(2)}, u32[]{:S(2)}) collective-permute-start(bf16[128,2304]{1,0:T(8,128)(2,1)S(1)} %slice.484), channel_id=1, source_target_pairs={{0,16},{1,17},{2,18},{3,19},{4,20},{5,21},{6,22},{7,23},{8,24},{9,... | collective-permute-start | bytes 1769480 | tf_op jit(solution)/shard_map/ppermute | solution.py:360
  289.9 15.7 %collective-permute-start.18 = (bf16[128,2304]{1,0:T(8,128)(2,1)S(1)}, bf16[128,2304]{1,0:T(8,128)(2,1)S(1)}, u32[]{:S(2)}, u32[]{:S(2)}) collective-permute-start(bf16[128,2304]{1,0:T(8,128)(2,1)S(1)} %slice.485), channel_id=1, source_target_pairs={{0,8},{1,9},{2,10},{3,11},{4,12},{5,13},{6,14},{7,15},{8,0},{9,1},... | collective-permute-start | bytes 1769480 | tf_op jit(solution)/shard_map/ppermute | solution.py:360
  291.4 28.9 %collective-permute-start.20 = (bf16[256,2304]{1,0:T(8,128)(2,1)}, bf16[256,2304]{1,0:T(8,128)(2,1)S(1)}, u32[]{:S(2)}, u32[]{:S(2)}) collective-permute-start(bf16[256,2304]{1,0:T(8,128)(2,1)} %collective-permute-done.11.refs_1_), channel_id=1, source_target_pairs={{0,1},{1,0},{2,3},{3,2},{4,5},{5,4},{6,7},{7,6},{8,9},{9,8},{10,11... | collective-permute-start | bytes 3538952 | tf_op jit(solution)/shard_map/ppermute | solution.py:360
  304.9 17.7 %collective-permute-start.21 = (bf16[256,2304]{1,0:T(8,128)(2,1)S(1)}, bf16[256,2304]{1,0:T(8,128)(2,1)S(1)}, u32[]{:S(2)}, u32[]{:S(2)}) collective-permute-start(bf16[256,2304]{1,0:T(8,128)(2,1)S(1)} %copy-done.29), channel_id=1, source_target_pairs={{0,1},{1,0},{2,3},{3,2},{4,5},{5,4},{6,7},{7,6},{8,9},{9,8},{10,11... | collective-permute-start | bytes 3538952 | tf_op jit(solution)/shard_map/ppermute | solution.py:360
  305.7 18.0 %collective-permute-start.22 = (bf16[256,2304]{1,0:T(8,128)(2,1)S(1)}, bf16[256,2304]{1,0:T(8,128)(2,1)S(1)}, u32[]{:S(2)}, u32[]{:S(2)}) collective-permute-start(bf16[256,2304]{1,0:T(8,128)(2,1)S(1)} %pad_maximum_fusion.5), channel_id=1, source_target_pairs={{0,1},{1,0},{2,3},{3,2},{4,5},{5,4},{6,7},{7,6},{8,9},{9,8},{10,11... | collective-permute-start | bytes 3538952 | tf_op jit(solution)/shard_map/ppermute | solution.py:360
  317.6 28.2 %collective-permute-start.16 = (bf16[256,2304]{1,0:T(8,128)(2,1)S(1)}, bf16[256,2304]{1,0:T(8,128)(2,1)S(1)}, u32[]{:S(2)}, u32[]{:S(2)}) collective-permute-start(bf16[256,2304]{1,0:T(8,128)(2,1)S(1)} %get-tuple-element.44), channel_id=1, source_target_pairs={{0,24},{1,25},{2,26},{3,27},{4,28},{5,29},{6,30},{7,31},{8,16},{9,... | collective-permute-start | bytes 3538952 | tf_op jit(solution)/shard_map/ppermute | solution.py:360
  320.0 51.8 %collective-permute-start.23 = (bf16[256,2304]{1,0:T(8,128)(2,1)}, bf16[256,2304]{1,0:T(8,128)(2,1)}, u32[]{:S(2)}, u32[]{:S(2)}) collective-permute-start(bf16[256,2304]{1,0:T(8,128)(2,1)} %get-tuple-element.46), channel_id=1, source_target_pairs={{0,8},{1,9},{2,10},{3,11},{4,12},{5,13},{6,14},{7,15},{8,0},{9,1},... | collective-permute-start | bytes 3538952 | tf_op jit(solution)/shard_map/ppermute | solution.py:360
  320.3 51.6 %collective-permute-start.24 = (bf16[256,2304]{1,0:T(8,128)(2,1)}, bf16[256,2304]{1,0:T(8,128)(2,1)}, u32[]{:S(2)}, u32[]{:S(2)}) collective-permute-start(bf16[256,2304]{1,0:T(8,128)(2,1)} %get-tuple-element.45), channel_id=1, source_target_pairs={{0,16},{1,17},{2,18},{3,19},{4,20},{5,21},{6,22},{7,23},{8,24},{9,... | collective-permute-start | bytes 3538952 | tf_op jit(solution)/shard_map/ppermute | solution.py:360
  379.7 27.0 %collective-permute-start.25 = (bf16[256,2304]{1,0:T(8,128)(2,1)}, bf16[256,2304]{1,0:T(8,128)(2,1)}, u32[]{:S(2)}, u32[]{:S(2)}) collective-permute-start(bf16[256,2304]{1,0:T(8,128)(2,1)} %get-tuple-element.28), channel_id=1, source_target_pairs={{0,8},{1,9},{2,10},{3,11},{4,12},{5,13},{6,14},{7,15},{8,0},{9,1},... | collective-permute-start | bytes 3538952 | tf_op jit(solution)/shard_map/ppermute | solution.py:360
  380.9 27.3 %collective-permute-start.26 = (bf16[256,2304]{1,0:T(8,128)(2,1)}, bf16[256,2304]{1,0:T(8,128)(2,1)S(1)}, u32[]{:S(2)}, u32[]{:S(2)}) collective-permute-start(bf16[256,2304]{1,0:T(8,128)(2,1)} %get-tuple-element.28), channel_id=1, source_target_pairs={{0,16},{1,17},{2,18},{3,19},{4,20},{5,21},{6,22},{7,23},{8,24},{9,... | collective-permute-start | bytes 3538952 | tf_op jit(solution)/shard_map/ppermute | solution.py:360
  381.1 284.5 %reduce-scatter.5.cloned.1.call-start = ((), (), s32[]{:S(2)}) async-start(), calls=%async_computation.16 | async-start | bytes 4423680 | tf_op jit(solution)/shard_map/reduce_scatter | solution.py:637
  381.1 44.8 %collective-permute-start.29 = (bf16[256,2304]{1,0:T(8,128)(2,1)}, bf16[256,2304]{1,0:T(8,128)(2,1)S(1)}, u32[]{:S(2)}, u32[]{:S(2)}) collective-permute-start(bf16[256,2304]{1,0:T(8,128)(2,1)} %get-tuple-element.28), channel_id=1, source_target_pairs={{0,1},{1,0},{2,3},{3,2},{4,5},{5,4},{6,7},{7,6},{8,9},{9,8},{10,11... | collective-permute-start | bytes 3538952 | tf_op jit(solution)/shard_map/ppermute | solution.py:360
  409.3 17.8 %collective-permute-start.30 = (bf16[256,2304]{1,0:T(8,128)(2,1)}, bf16[256,2304]{1,0:T(8,128)(2,1)S(1)}, u32[]{:S(2)}, u32[]{:S(2)}) collective-permute-start(bf16[256,2304]{1,0:T(8,128)(2,1)} %collective-permute-done.25), channel_id=1, source_target_pairs={{0,1},{1,0},{2,3},{3,2},{4,5},{5,4},{6,7},{7,6},{8,9},{9,8},{10,11... | collective-permute-start | bytes 3538952 | tf_op jit(solution)/shard_map/ppermute | solution.py:360
  411.6 16.6 %collective-permute-start.31 = (bf16[256,2304]{1,0:T(8,128)(2,1)S(1)}, bf16[256,2304]{1,0:T(8,128)(2,1)S(1)}, u32[]{:S(2)}, u32[]{:S(2)}) collective-permute-start(bf16[256,2304]{1,0:T(8,128)(2,1)S(1)} %collective-permute-done.26), channel_id=1, source_target_pairs={{0,1},{1,0},{2,3},{3,2},{4,5},{5,4},{6,7},{7,6},{8,9},{9,8},{10,11... | collective-permute-start | bytes 3538952 | tf_op jit(solution)/shard_map/ppermute | solution.py:360
  500.4 16.5 %collective-permute-start.33 = (bf16[1024,2304]{1,0:T(8,128)(2,1)}, bf16[1024,2304]{1,0:T(8,128)(2,1)}, u32[]{:S(2)}, u32[]{:S(2)}) collective-permute-start(bf16[1024,2304]{1,0:T(8,128)(2,1)} %convolution_convert_fusion.2), channel_id=1, source_target_pairs={{0,1},{1,0},{2,3},{3,2},{4,5},{5,4},{6,7},{7,6},{8,9},{9,8},{10,11... | collective-permute-start | bytes 14155784 | tf_op jit(solution)/shard_map/ppermute | solution.py:360
  500.4 244.4 %reduce-scatter.7.cloned.1.call-start = ((), (), s32[]{:S(2)}) async-start(), calls=%async_computation.17 | async-start | bytes 8847360 | tf_op jit(solution)/shard_map/reduce_scatter | solution.py:627
  547.1 234.3 %reduce-scatter.9.cloned.1.call-start = ((), (), s32[]{:S(2)}) async-start(), calls=%async_computation.18 | async-start | bytes 1658880 | tf_op jit(solution)/shard_map/reduce_scatter | solution.py:665
  547.6 28.4 %collective-permute-start.34 = (bf16[256,2304]{1,0:T(8,128)(2,1)}, bf16[256,2304]{1,0:T(8,128)(2,1)}, u32[]{:S(2)}, u32[]{:S(2)}) collective-permute-start(bf16[256,2304]{1,0:T(8,128)(2,1)} %get-tuple-element.41), channel_id=1, source_target_pairs={{0,24},{1,25},{2,26},{3,27},{4,28},{5,29},{6,30},{7,31},{8,16},{9,... | collective-permute-start | bytes 3538952 | tf_op jit(solution)/shard_map/ppermute | solution.py:360
  549.3 51.4 %collective-permute-start.35 = (bf16[256,2304]{1,0:T(8,128)(2,1)}, bf16[256,2304]{1,0:T(8,128)(2,1)}, u32[]{:S(2)}, u32[]{:S(2)}) collective-permute-start(bf16[256,2304]{1,0:T(8,128)(2,1)} %get-tuple-element.43), channel_id=1, source_target_pairs={{0,8},{1,9},{2,10},{3,11},{4,12},{5,13},{6,14},{7,15},{8,0},{9,1},... | collective-permute-start | bytes 3538952 | tf_op jit(solution)/shard_map/ppermute | solution.py:360
  549.5 52.5 %collective-permute-start.36 = (bf16[256,2304]{1,0:T(8,128)(2,1)}, bf16[256,2304]{1,0:T(8,128)(2,1)S(1)}, u32[]{:S(2)}, u32[]{:S(2)}) collective-permute-start(bf16[256,2304]{1,0:T(8,128)(2,1)} %get-tuple-element.42), channel_id=1, source_target_pairs={{0,16},{1,17},{2,18},{3,19},{4,20},{5,21},{6,22},{7,23},{8,24},{9,... | collective-permute-start | bytes 3538952 | tf_op jit(solution)/shard_map/ppermute | solution.py:360
  611.3 27.6 %collective-permute-start.38 = (bf16[256,2304]{1,0:T(8,128)(2,1)}, bf16[256,2304]{1,0:T(8,128)(2,1)S(1)}, u32[]{:S(2)}, u32[]{:S(2)}) collective-permute-start(bf16[256,2304]{1,0:T(8,128)(2,1)} %get-tuple-element.25.refs_1_), channel_id=1, source_target_pairs={{0,8},{1,9},{2,10},{3,11},{4,12},{5,13},{6,14},{7,15},{8,0},{9,1},... | collective-permute-start | bytes 3538952 | tf_op jit(solution)/shard_map/ppermute | solution.py:360
  612.2 27.5 %collective-permute-start.39 = (bf16[256,2304]{1,0:T(8,128)(2,1)}, bf16[256,2304]{1,0:T(8,128)(2,1)}, u32[]{:S(2)}, u32[]{:S(2)}) collective-permute-start(bf16[256,2304]{1,0:T(8,128)(2,1)} %get-tuple-element.25.refs_1_), channel_id=1, source_target_pairs={{0,16},{1,17},{2,18},{3,19},{4,20},{5,21},{6,22},{7,23},{8,24},{9,... | collective-permute-start | bytes 3538952 | tf_op jit(solution)/shard_map/ppermute | solution.py:360
  613.3 43.5 %collective-permute-start.42 = (bf16[256,2304]{1,0:T(8,128)(2,1)}, bf16[256,2304]{1,0:T(8,128)(2,1)S(1)}, u32[]{:S(2)}, u32[]{:S(2)}) collective-permute-start(bf16[256,2304]{1,0:T(8,128)(2,1)} %get-tuple-element.25.refs_1_), channel_id=1, source_target_pairs={{0,1},{1,0},{2,3},{3,2},{4,5},{5,4},{6,7},{7,6},{8,9},{9,8},{10,11... | collective-permute-start | bytes 3538952 | tf_op jit(solution)/shard_map/ppermute | solution.py:360
  622.8 188.2 %collective-permute-start.37 = (bf16[1024,2304]{1,0:T(8,128)(2,1)}, bf16[1024,2304]{1,0:T(8,128)(2,1)}, u32[]{:S(2)}, u32[]{:S(2)}) collective-permute-start(bf16[1024,2304]{1,0:T(8,128)(2,1)} %convolution_convert_fusion.1), channel_id=1, source_target_pairs={{0,1},{1,0},{2,3},{3,2},{4,5},{5,4},{6,7},{7,6},{8,9},{9,8},{10,11... | collective-permute-start | bytes 14155784 | tf_op jit(solution)/shard_map/ppermute | solution.py:360
  638.9 14.0 %collective-permute-start.40 = (bf16[128,2304]{1,0:T(8,128)(2,1)S(1)}, bf16[128,2304]{1,0:T(8,128)(2,1)S(1)}, u32[]{:S(2)}, u32[]{:S(2)}) collective-permute-start(bf16[128,2304]{1,0:T(8,128)(2,1)S(1)} %slice.513), channel_id=1, source_target_pairs={{0,16},{1,17},{2,18},{3,19},{4,20},{5,21},{6,22},{7,23},{8,24},{9,... | collective-permute-start | bytes 1769480 | tf_op jit(solution)/shard_map/ppermute | solution.py:360
  642.2 14.8 %collective-permute-start.43 = (bf16[256,2304]{1,0:T(8,128)(2,1)S(1)}, bf16[256,2304]{1,0:T(8,128)(2,1)S(1)}, u32[]{:S(2)}, u32[]{:S(2)}) collective-permute-start(bf16[256,2304]{1,0:T(8,128)(2,1)S(1)} %collective-permute-done.38), channel_id=1, source_target_pairs={{0,1},{1,0},{2,3},{3,2},{4,5},{5,4},{6,7},{7,6},{8,9},{9,8},{10,11... | collective-permute-start | bytes 3538952 | tf_op jit(solution)/shard_map/ppermute | solution.py:360
  746.0 35.4 %collective-permute-start.48 = (bf16[180,2304]{1,0:T(8,128)(2,1)S(1)}, bf16[180,2304]{1,0:T(8,128)(2,1)}, u32[]{:S(2)}, u32[]{:S(2)}) collective-permute-start(bf16[180,2304]{1,0:T(8,128)(2,1)S(1)} %copy-done.27), channel_id=1, source_target_pairs={{0,0},{1,4},{2,8},{3,12},{4,16},{5,20},{6,24},{7,28},{8,1},{9,5},{... | collective-permute-start | bytes 2488328 | tf_op jit(solution)/shard_map/ppermute | solution.py:360
  749.9 38.1 %all-to-all-start.5 = ((bf16[8,72,1536]{2,1,0:T(8,128)(2,1)}), bf16[8,72,1536]{2,1,0:T(8,128)(2,1)S(1)}, u32[]{:S(2)}, u32[]{:S(2)}) async-start(bf16[8,72,1536]{2,1,0:T(8,128)(2,1)} %after.57), calls=%async_computation.7 | async-start | bytes 3538944 | tf_op jit(solution)/shard_map/all_to_all | solution.py:631
  753.7 192.6 %reduce-scatter.11.cloned.1.call-start = ((), (), s32[]{:S(2)}) async-start(), calls=%async_computation.19 | async-start | bytes 5898240 | tf_op jit(solution)/shard_map/reduce_scatter | solution.py:627
  798.5 38.4 %collective-permute-start.51 = (bf16[1024,2304]{1,0:T(8,128)(2,1)}, bf16[1024,2304]{1,0:T(8,128)(2,1)}, u32[]{:S(2)}, u32[]{:S(2)}) collective-permute-start(bf16[1024,2304]{1,0:T(8,128)(2,1)} %convolution_convert_fusion.4), channel_id=1, source_target_pairs={{0,1},{1,0},{2,3},{3,2},{4,5},{5,4},{6,7},{7,6},{8,9},{9,8},{10,11... | collective-permute-start | bytes 14155784 | tf_op jit(solution)/shard_map/ppermute | solution.py:360
  808.1 17.3 %collective-permute-start.59 = (bf16[72,2304]{1,0:T(8,128)(2,1)}, bf16[72,2304]{1,0:T(8,128)(2,1)S(1)}, u32[]{:S(2)}, u32[]{:S(2)}) collective-permute-start(bf16[72,2304]{1,0:T(8,128)(2,1)} %bitcast.51), channel_id=1, source_target_pairs={{0,0},{1,4},{2,1},{3,5},{4,2},{5,6},{6,3},{7,7},{8,8},{9,12},{10,9... | collective-permute-start | bytes 995336 | tf_op jit(solution)/shard_map/ppermute | solution.py:360
  815.6 46.5 %collective-permute-start.46 = (bf16[256,2304]{1,0:T(8,128)(2,1)}, bf16[256,2304]{1,0:T(8,128)(2,1)S(1)}, u32[]{:S(2)}, u32[]{:S(2)}) collective-permute-start(bf16[256,2304]{1,0:T(8,128)(2,1)} %after.54), channel_id=1, source_target_pairs={{0,24},{1,25},{2,26},{3,27},{4,28},{5,29},{6,30},{7,31},{8,16},{9,... | collective-permute-start | bytes 3538952 | tf_op jit(solution)/shard_map/ppermute | solution.py:360
  824.7 51.9 %collective-permute-start.49 = (bf16[256,2304]{1,0:T(8,128)(2,1)}, bf16[256,2304]{1,0:T(8,128)(2,1)S(1)}, u32[]{:S(2)}, u32[]{:S(2)}) collective-permute-start(bf16[256,2304]{1,0:T(8,128)(2,1)} %after.61), channel_id=1, source_target_pairs={{0,8},{1,9},{2,10},{3,11},{4,12},{5,13},{6,14},{7,15},{8,0},{9,1},... | collective-permute-start | bytes 3538952 | tf_op jit(solution)/shard_map/ppermute | solution.py:360
  825.5 53.4 %collective-permute-start.50 = (bf16[256,2304]{1,0:T(8,128)(2,1)}, bf16[256,2304]{1,0:T(8,128)(2,1)}, u32[]{:S(2)}, u32[]{:S(2)}) collective-permute-start(bf16[256,2304]{1,0:T(8,128)(2,1)} %after.63), channel_id=1, source_target_pairs={{0,16},{1,17},{2,18},{3,19},{4,20},{5,21},{6,22},{7,23},{8,24},{9,... | collective-permute-start | bytes 3538952 | tf_op jit(solution)/shard_map/ppermute | solution.py:360
  844.6 57.4 %collective-permute-start.52 = (bf16[256,2304]{1,0:T(8,128)(2,1)}, bf16[256,2304]{1,0:T(8,128)(2,1)}, u32[]{:S(2)}, u32[]{:S(2)}) collective-permute-start(bf16[256,2304]{1,0:T(8,128)(2,1)} %get-tuple-element.35), channel_id=1, source_target_pairs={{0,24},{1,25},{2,26},{3,27},{4,28},{5,29},{6,30},{7,31},{8,16},{9,... | collective-permute-start | bytes 3538952 | tf_op jit(solution)/shard_map/ppermute | solution.py:360
  862.1 65.1 %collective-permute-start.53 = (bf16[256,2304]{1,0:T(8,128)(2,1)}, bf16[256,2304]{1,0:T(8,128)(2,1)}, u32[]{:S(2)}, u32[]{:S(2)}) collective-permute-start(bf16[256,2304]{1,0:T(8,128)(2,1)} %get-tuple-element.37), channel_id=1, source_target_pairs={{0,8},{1,9},{2,10},{3,11},{4,12},{5,13},{6,14},{7,15},{8,0},{9,1},... | collective-permute-start | bytes 3538952 | tf_op jit(solution)/shard_map/ppermute | solution.py:360
  862.1 65.2 %collective-permute-start.54 = (bf16[256,2304]{1,0:T(8,128)(2,1)}, bf16[256,2304]{1,0:T(8,128)(2,1)}, u32[]{:S(2)}, u32[]{:S(2)}) collective-permute-start(bf16[256,2304]{1,0:T(8,128)(2,1)} %get-tuple-element.36), channel_id=1, source_target_pairs={{0,16},{1,17},{2,18},{3,19},{4,20},{5,21},{6,22},{7,23},{8,24},{9,... | collective-permute-start | bytes 3538952 | tf_op jit(solution)/shard_map/ppermute | solution.py:360
  946.3 74.6 %all-to-all-start.6 = ((bf16[8,72,960]{2,1,0:T(8,128)(2,1)}), bf16[8,72,960]{2,1,0:T(8,128)(2,1)S(1)}, u32[]{:S(2)}, u32[]{:S(2)}) async-start(bf16[8,72,960]{2,1,0:T(8,128)(2,1)} %bitcast.181), calls=%async_computation.10 | async-start | bytes 2359296 | tf_op jit(solution)/shard_map/all_to_all | solution.py:631
  954.0 64.2 %collective-permute-start.58 = (bf16[1,128,2304]{2,1,0:T(8,128)(2,1)S(1)}, bf16[1,128,2304]{2,1,0:T(8,128)(2,1)S(1)}, u32[]{:S(2)}, u32[]{:S(2)}) collective-permute-start(bf16[1,128,2304]{2,1,0:T(8,128)(2,1)S(1)} %pad_maximum_fusion.11), channel_id=1, source_target_pairs={{0,6},{1,7},{2,12},{3,13},{4,18},{5,19},{6,24},{7,25},{8,4},{9,5},... | collective-permute-start | bytes 1769480 | tf_op jit(solution)/shard_map/ppermute | solution.py:360
  956.0 42.8 %collective-permute-start.55 = (bf16[1,128,2304]{2,1,0:T(8,128)(2,1)S(1)}, bf16[1,128,2304]{2,1,0:T(8,128)(2,1)S(1)}, u32[]{:S(2)}, u32[]{:S(2)}) collective-permute-start(bf16[1,128,2304]{2,1,0:T(8,128)(2,1)S(1)} %pad_maximum_fusion.8), channel_id=1, source_target_pairs={{0,0},{1,1},{2,10},{3,11},{4,20},{5,21},{6,30},{7,31},{8,2},{9,3},... | collective-permute-start | bytes 1769480 | tf_op jit(solution)/shard_map/ppermute | solution.py:360
  960.3 57.9 %collective-permute-start.57 = (bf16[1,128,2304]{2,1,0:T(8,128)(2,1)S(1)}, bf16[1,128,2304]{2,1,0:T(8,128)(2,1)S(1)}, u32[]{:S(2)}, u32[]{:S(2)}) collective-permute-start(bf16[1,128,2304]{2,1,0:T(8,128)(2,1)S(1)} %pad_maximum_fusion.10), channel_id=1, source_target_pairs={{0,4},{1,5},{2,14},{3,15},{4,16},{5,17},{6,26},{7,27},{8,6},{9,7},... | collective-permute-start | bytes 1769480 | tf_op jit(solution)/shard_map/ppermute | solution.py:360
  962.3 55.8 %collective-permute-start.56 = (bf16[1,128,2304]{2,1,0:T(8,128)(2,1)S(1)}, bf16[1,128,2304]{2,1,0:T(8,128)(2,1)S(1)}, u32[]{:S(2)}, u32[]{:S(2)}) collective-permute-start(bf16[1,128,2304]{2,1,0:T(8,128)(2,1)S(1)} %pad_maximum_fusion.9), channel_id=1, source_target_pairs={{0,2},{1,3},{2,8},{3,9},{4,22},{5,23},{6,28},{7,29},{8,0},{9,1},{1... | collective-permute-start | bytes 1769480 | tf_op jit(solution)/shard_map/ppermute | solution.py:360
  (77 other events, 732.3 us)
Sparse Core Ops, SparseCore 0:
  77.9 114.6 all-gather.4
  194.8 30.8 all-gather.6
  233.0 128.3 all-gather.8
  381.2 68.8 all-gather.10
  500.6 65.0 reduce-scatter.4
  567.8 124.0 reduce-scatter.6
  694.7 31.8 reduce-scatter.8
  802.4 91.9 reduce-scatter.10

commit v3 on v2

--- a/solution.py
+++ b/solution.py
@@ -51,26 +51,30 @@
 def head_tiles(pair, index_ref, total, run_tile):
     side = index_ref[total // PIECE]
     own = pair < 2
-    prompt_tiles = PROMPT // TILE
-    for tile in range(prompt_tiles):
+    for tile in range(PROMPT // TILE):
         mine = side == (0 if tile % 4 in (0, 3) else 1)
-        for head in range(2):
-            keep = own if head else jnp.logical_or(own, mine)
-
-            @pl.when(keep)
-            def _(tile=tile, head=head):
-                run_tile(tile * TILE, tile * TILE, head)
+
+        @pl.when(own)
+        def _(tile=tile):
+            run_tile(tile * TILE, tile * TILE, (0, 1))
+
+        @pl.when(jnp.logical_and(jnp.logical_not(own), mine))
+        def _(tile=tile):
+            run_tile(tile * TILE, tile * TILE, (0,))
 
     later = (total - PROMPT) // TILE
 
     def body(step, carry):
         mine = (step * 2 >= later).astype(jnp.int32) == side
-        for head in range(2):
-            keep = own if head else jnp.logical_or(own, mine)
-
-            @pl.when(keep)
-            def _(head=head):
-                run_tile(pl.multiple_of(PROMPT + step * TILE, TILE), PROMPT, head)
+        start = pl.multiple_of(PROMPT + step * TILE, TILE)
+
+        @pl.when(own)
+        def _():
+            run_tile(start, PROMPT, (0, 1))
+
+        @pl.when(jnp.logical_and(jnp.logical_not(own), mine))
+        def _():
+            run_tile(start, PROMPT, (0,))
 
         return carry
 
@@ -141,27 +145,31 @@
     mixed[...] = jnp.zeros_like(mixed)
     scale = 1.0 / math.sqrt(HEAD_DIM)
 
-    def run_tile(start, prefix, head):
+    def run_tile(start, prefix, heads):
         rows = pl.ds(start, TILE)
-        query = kept_ref[0, rows, 0:PAIR]
-        mask = lanes_of(head, query.shape)
-        query = jnp.where(mask, query.astype(F32) * scale, 0.0).astype(BF)
+        query = kept_ref[0, rows, 0:PAIR].astype(F32) * scale
+        masks = [lanes_of(head, query.shape) for head in heads]
+        queries = [jnp.where(mask, query, 0.0).astype(BF) for mask in masks]
         seen = lax.broadcasted_iota(jnp.int32, (TILE, TILE), 1) <= lax.broadcasted_iota(
             jnp.int32, (TILE, TILE), 0
         )
-        near = jnp.where(seen, nt_dot(query, kept_ref[0, rows, PAIR : 2 * PAIR]), NEGATIVE)
-        peak = jnp.max(near, axis=1, keepdims=True)
+        keys = [kept_ref[0, rows, PAIR : 2 * PAIR]]
+        values = [kept_ref[0, rows, 2 * PAIR : 3 * PAIR]]
         if prefix:
-            far = nt_dot(query, kept_ref[0, 0:prefix, PAIR : 2 * PAIR])
-            peak = jnp.maximum(peak, jnp.max(far, axis=1, keepdims=True))
-        near = jnp.exp(near - peak)
-        count = jnp.sum(near, axis=1, keepdims=True)
-        out = nn_dot(near.astype(BF), kept_ref[0, rows, 2 * PAIR : 3 * PAIR])
-        if prefix:
-            far = jnp.exp(far - peak)
-            count = count + jnp.sum(far, axis=1, keepdims=True)
-            out = out + nn_dot(far.astype(BF), kept_ref[0, 0:prefix, 2 * PAIR : 3 * PAIR])
-        mixed[rows, :] = jnp.where(mask, out / count, mixed[rows, :])
+            keys.append(kept_ref[0, 0:prefix, PAIR : 2 * PAIR])
+            values.append(kept_ref[0, 0:prefix, 2 * PAIR : 3 * PAIR])
+        scores = [[nt_dot(query, key) for key in keys] for query in queries]
+        total_out = mixed[rows, :]
+        for mask, parts in zip(masks, scores):
+            parts[0] = jnp.where(seen, parts[0], NEGATIVE)
+            peak = functools.reduce(
+                jnp.maximum, [jnp.max(part, axis=1, keepdims=True) for part in parts]
+            )
+            parts = [jnp.exp(part - peak) for part in parts]
+            count = sum(jnp.sum(part, axis=1, keepdims=True) for part in parts)
+            out = sum(nn_dot(part.astype(BF), value) for part, value in zip(parts, values))
+            total_out = jnp.where(mask, out / count, total_out)
+        mixed[rows, :] = total_out
 
     head_tiles(pair, index_ref, total, run_tile)
 
@@ -198,7 +206,7 @@
         ],
         compiler_params=pltpu.CompilerParams(vmem_limit_bytes=40 << 20),
         cost_estimate=pl.CostEstimate(
-            flops=0, bytes_accessed=1 << 20, transcendentals=0
+            flops=36 * 10**9, bytes_accessed=1 << 20, transcendentals=0
         ),
         name="attend",
     )(index, raw, cosine, sine)
@@ -223,45 +231,41 @@
     grad_v[...] = jnp.zeros_like(grad_v)
     scale = 1.0 / math.sqrt(HEAD_DIM)
 
-    def run_tile(start, prefix, head):
+    def run_tile(start, prefix, heads):
         rows = pl.ds(start, TILE)
-        query = kept_ref[0, rows, 0:PAIR]
-        mask = lanes_of(head, query.shape)
-        query = jnp.where(mask, query.astype(F32) * scale, 0.0).astype(BF)
-        away = jnp.where(mask, outer[rows, :].astype(F32), 0.0).astype(BF)
+        query = kept_ref[0, rows, 0:PAIR].astype(F32) * scale
+        away = outer[rows, :].astype(F32)
+        masks = [lanes_of(head, query.shape) for head in heads]
+        queries = [jnp.where(mask, query, 0.0).astype(BF) for mask in masks]
+        aways = [jnp.where(mask, away, 0.0).astype(BF) for mask in masks]
         seen = lax.broadcasted_iota(jnp.int32, (TILE, TILE), 0) <= lax.broadcasted_iota(
             jnp.int32, (TILE, TILE), 1
         )
-        near_key = kept_ref[0, rows, PAIR : 2 * PAIR]
-        near = jnp.where(seen, nt_dot(near_key, query), NEGATIVE)
-        peak = jnp.max(near, axis=0, keepdims=True)
-        if prefix:
-            far_key = kept_ref[0, 0:prefix, PAIR : 2 * PAIR]
-            far = nt_dot(far_key, query)
-            peak = jnp.maximum(peak, jnp.max(far, axis=0, keepdims=True))
-        near = jnp.exp(near - peak)
-        count = jnp.sum(near, axis=0, keepdims=True)
-        if prefix:
-            far = jnp.exp(far - peak)
-            count = count + jnp.sum(far, axis=0, keepdims=True)
-        inverse = 1.0 / count
-        near = near * inverse
-        near_pull = nt_dot(kept_ref[0, rows, 2 * PAIR : 3 * PAIR], away)
-        delta = jnp.sum(near * near_pull, axis=0, keepdims=True)
-        if prefix:
-            far = far * inverse
-            far_pull = nt_dot(kept_ref[0, 0:prefix, 2 * PAIR : 3 * PAIR], away)
-            delta = delta + jnp.sum(far * far_pull, axis=0, keepdims=True)
-        grad_v[rows, :] += nn_dot(near.astype(BF), away)
-        near = (near * (near_pull - delta)).astype(BF)
-        grad_k[rows, :] += nn_dot(near, query)
-        part = tn_dot(near, near_key)
-        if prefix:
-            grad_v[0:prefix, :] += nn_dot(far.astype(BF), away)
-            far = (far * (far_pull - delta)).astype(BF)
-            grad_k[0:prefix, :] += nn_dot(far, query)
-            part = part + tn_dot(far, far_key)
-        grad_q[rows, :] = jnp.where(mask, part * scale, grad_q[rows, :])
+        spans = [rows] + ([pl.ds(0, prefix)] if prefix else [])
+        keys = [kept_ref[0, span, PAIR : 2 * PAIR] for span in spans]
+        values = [kept_ref[0, span, 2 * PAIR : 3 * PAIR] for span in spans]
+        scores = [[nt_dot(key, query) for key in keys] for query in queries]
+        pulls = [[nt_dot(value, away) for value in values] for away in aways]
+        probs, slopes = [], []
+        for parts, pull in zip(scores, pulls):
+            parts[0] = jnp.where(seen, parts[0], NEGATIVE)
+            peak = functools.reduce(
+                jnp.maximum, [jnp.max(part, axis=0, keepdims=True) for part in parts]
+            )
+            parts = [jnp.exp(part - peak) for part in parts]
+            inverse = 1.0 / sum(jnp.sum(part, axis=0, keepdims=True) for part in parts)
+            parts = [part * inverse for part in parts]
+            delta = sum(jnp.sum(p * q, axis=0, keepdims=True) for p, q in zip(parts, pull))
+            probs.append([part.astype(BF) for part in parts])
+            slopes.append([(p * (q - delta)).astype(BF) for p, q in zip(parts, pull)])
+        for i, span in enumerate(spans):
+            grad_v[span, :] += sum(nn_dot(prob[i], away) for prob, away in zip(probs, aways))
+            grad_k[span, :] += sum(nn_dot(slope[i], query) for slope, query in zip(slopes, queries))
+        part_q = grad_q[rows, :]
+        for mask, slope in zip(masks, slopes):
+            part = sum(tn_dot(piece, key) for piece, key in zip(slope, keys))
+            part_q = jnp.where(mask, part * scale, part_q)
+        grad_q[rows, :] = part_q
 
     head_tiles(pair, index_ref, total, run_tile)
 
@@ -394,7 +398,7 @@
         def shuffle_in(parts):
             return lax.all_to_all(parts, "tok", 0, 0, tiled=True).reshape(rows, width)
 
-        def shuffle_out(*arrays):
+        def shuffle_out(arrays, beside):
             parts = [array.reshape(n_tok, quarter, width) for array in arrays]
             results = [jnp.zeros_like(part) for part in parts]
             for turn_by in range(n_grp):
@@ -404,6 +408,7 @@
                     jnp.concatenate(pieces, axis=1),
                     lambda g, t, f, turn_by=turn_by: (t, g ^ t ^ turn_by, f),
                 )
+                piece = after(piece, beside)
                 for i, result in enumerate(results):
                     results[i] = lax.dynamic_update_slice_in_dim(
                         result, piece[:, i * quarter : (i + 1) * quarter], away, 0
@@ -425,10 +430,9 @@
             return layer_join(*layer_pieces(array))
 
         def pair_sum(rows_of):
-            away = send(rows_of(1).astype(BF), sibling)
-            here = rows_of(0)
-            away = away.reshape(n_grp, rows, -1)
-            here = here.reshape(n_grp, rows, -1)
+            away = rows_of(1).astype(BF).reshape(n_grp, rows, -1)
+            away = {step: send(away[step], sibling) for step in (3, 1, 2, 0)}
+            here = rows_of(0).reshape(n_grp, rows, -1)
             parts = [(here[step] + away[step].astype(F32)).astype(BF) for step in (3, 1, 2)]
             return here[0], away[0], parts
 
@@ -489,9 +493,10 @@
             ]
             first = side * (own_span + HEAD_DIM)
             spans = [(first, PAIR), (first + PAIR, PAIR), (own_span, HEAD_DIM)]
-            return jnp.concatenate(
-                [weight[:, at : at + size] for at, size in spans for weight in picked], axis=1
-            )
+            columns = [weight[:, at : at + size] for at, size in spans for weight in picked]
+            wide = sum(part.shape[1] for part in columns)
+            columns.append(jnp.zeros((query_weight.shape[0], -wide % PAIR), BF))
+            return jnp.concatenate(columns, axis=1)
 
         def pair_rows(zero_block, one_block):
             mine = jnp.where(even, zero_block, one_block)
@@ -634,8 +639,6 @@
         parts = layer_send(pair_sum(lambda side, pick=pick: nt_dot(pick(side)[0], ff_weight)))
         ff_local = spread_rows(tn_dot(h_two, after(grad_both, parts[0])))
         grad_h2 = layer_add(parts, ff_local)
-        down_rows = lax.psum_scatter(down_local, "tok", scatter_dimension=0, tiled=True)
-        down_rows = down_rows[0, :ff_piece]
         ff_rows = sum_rows(ff_local)
         gain_two_sum = jnp.sum(grad_h2 * normed_two, axis=0)
         pulled = grad_h2 * gain_two[None, :]
@@ -645,6 +648,8 @@
             - scale_two**3 * second_in * jnp.mean(pulled * second_in, axis=1, keepdims=True)
         )
         grad_z_here = (RESIDUAL * grad_second).astype(BF)
+        down_rows = lax.psum_scatter(down_local, "tok", scatter_dimension=0, tiled=True)
+        down_rows = down_rows[0, :ff_piece]
         grad_z = layer_gather(grad_z_here)
         pick = halves(after(act, grad_z_here))
         feed_sums = pair_sum(lambda side, pick=pick: nn_dot(pick(side)[0], down_w))
@@ -664,19 +669,19 @@
         out_full = out_full.astype(BF).reshape(n_tok, -1, width)
         output_grad = lax.psum_scatter(out_full, "tok", scatter_dimension=0, tiled=True)
 
-        grad_attn = after(grad_attn, out_full, down_rows)
+        grad_attn = after(grad_attn, out_full, down_rows, feed_parts[0])
         grads = attend_back(0, 3, index, kept, grad_attn, cosine, sine, qkv_weight.shape[1])
-        grads = after(grads, ff_rows)
+        grads = after(grads, ff_rows, *feed_parts[2])
         qkv_local = spread_rows(tn_dot(h_one, grads))
         qkv_rows = sum_rows(qkv_local)
         got = to_owners(after(ff_rows, grads))
         down_grad = send(
-            after(down_rows, grads),
+            after(down_rows, qkv_rows),
             lambda g, t, f: (t, (n_grp * f + g) // n_fs, (n_grp * f + g) % n_fs),
         )
-        pick = halves(after(grads, qkv_local, got, output_grad, down_grad))
+        pick = halves(after(grads, qkv_local, output_grad, got))
         parts = layer_send(pair_sum(lambda side, pick=pick: nt_dot(pick(side)[0], qkv_weight)))
-        feed = layer_add(feed_parts, parts[0])
+        feed = layer_add(feed_parts, parts[2][1])
         layer_output = (second_in + RESIDUAL * feed).astype(BF)
         got = after(got, layer_output).reshape(n_grp, n_fs, -1, 2, n_tok, ff_tall)
         gate_grad, up_grad = (
@@ -695,37 +700,37 @@
             - scale_one**3 * hidden * jnp.mean(pulled * hidden, axis=1, keepdims=True)
         )
         input_grad = after(input_grad.astype(BF), qkv_rows)
-        layer_output, input_grad = shuffle_out(layer_output, input_grad)
-        input_grad = input_grad.astype(F32)
         output_grad = send(
             output_grad[0], lambda g, t, f: (g, (n_tok * f + t) // n_fs, (n_tok * f + t) % n_fs)
         ).astype(F32)
-        got = to_owners(qkv_rows).astype(F32)
+        got = to_owners(qkv_rows)
         own_rows = got.shape[1]
-        got = got.reshape(n_grp, n_fs, own_rows, got.shape[2])
+        here = got.astype(F32).reshape(n_grp, n_fs, own_rows, got.shape[2])
 
         def projection_grad(which):
             def own(side):
                 return [
-                    got[:, side, :, SLAB * pair + PAIR * which : SLAB * pair + PAIR * (which + 1)]
+                    here[:, side, :, SLAB * pair + PAIR * which : SLAB * pair + PAIR * (which + 1)]
                     for pair in range(2)
                 ]
 
             at = 2 * SLAB + HEAD_DIM * which
-            shared = got[:, 0, :, at : at + HEAD_DIM] + got[:, 1, :, at : at + HEAD_DIM]
+            shared = here[:, 0, :, at : at + HEAD_DIM] + here[:, 1, :, at : at + HEAD_DIM]
             whole = jnp.concatenate(own(0) + [shared] + own(1), axis=2)
             return whole.transpose(1, 0, 2).reshape(own_rows, width)
 
+        qkv_grads = [projection_grad(which) for which in range(3)]
+        layer_output, input_grad = shuffle_out((layer_output, input_grad), qkv_grads)
+        input_grad = input_grad.astype(F32)
         gains = jnp.stack([gain_one_sum, gain_two_sum], axis=1).reshape(
             n_grp * n_tok * n_fs, -1
         )
+        gains = after(gains, got)
         gains = jnp.sum(lax.all_to_all(gains, ALL, 0, 0, tiled=True), axis=0).reshape(-1, 2)
         return (
             layer_output,
             input_grad,
-            projection_grad(0),
-            projection_grad(1),
-            projection_grad(2),
+            *qkv_grads,
             output_grad,
             gate_grad,
             up_grad,

time: 1060 us -> 969 us (0.914)
  the two profiles are of different devices: /device:TPU:5 before, /device:TPU:1 now
where the time goes in v3:
time: 969 us; the launch traced here: 956 us
  waiting for transfers between devices  262 us (27%)
  matrix products  167 us (17%)
  local copies, waits for them, and re-layouts  166 us (17%)
  starting transfers between devices  153 us (16%)
  other arithmetic  104 us (11%)
  Pallas kernels  88.9 us (9%)
  between operations  15.7 us (2%)
    ppermute x72, waiting for transfers between devices, send(): return lax.ppermute(array, ALL, permutation(move))  191 us
    ppermute x72, starting transfers between devices, send(): return lax.ppermute(array, ALL, permutation(move))  97.3 us
    unnamed x170, local copies, waits for them, and re-layouts  71.2 us
    dot_general x6, matrix products, nt_dot(): lax.dot_general(left, right, (((1,), (1,)), ((), ())), preferred_element_...  62 us
    pallas_call x1, Pallas kernels, attend_back(): pl.pallas_call(functools.partial(attend_back_kernel, first), grid_spec=pl...  55.2 us
    dot_general x6, matrix products, nn_dot(): lax.dot_general(left, right, (((1,), (0,)), ((), ())), preferred_element_...  53.7 us
    dot_general x4, matrix products, tn_dot(): lax.dot_general(left, right, (((0,), (0,)), ((), ())), preferred_element_...  51.1 us
    pallas_call x1, Pallas kernels, attend(): pl.pallas_call(attend_kernel, grid_spec=pltpu.PrefetchScalarGridSpec(num_...  33.6 us
  transfers between devices with their start and end apart: 88, of which 23 were waited for; matrix products, arithmetic and copies ran while one was open for 43% of the time, Pallas kernels for 9%

profile of v3, /device:TPU:1, one launch (start us, length us, event | category | flops | bytes accessed | tf_op | source)
XLA Modules:
  0.0 956.3 jit_solution(18158237190361493375)
XLA Ops:
  9.7 4.3 all-to-all-start
  16.1 13.3 %all-to-all-done.refs_1_ = bf16[4,64,2304]{2,1,0:T(8,128)(2,1)} async-done(((bf16[4,64,2304]{2,1,0:T(8,128)(2,1)}), bf16[4,64,2304]{2,1,0:T(8,128)(2,1)}, u32[]{:S(2)}, u32[]{:S(2)}) %all-to-all-start) | async-done | bytes 1179680 | tf_op jit(solution)/shard_map/all_to_all | solution.py:396
  31.9 4.6 all-to-all-start.1
  57.6 3.3 concatenate.90
  60.9 3.2 concatenate.91
  68.7 4.3 all-to-all-start.2
  81.3 6.4 all-to-all-done.2.refs_0_
  90.3 3.1 constant_dynamic-update-slice_fusion.8
  97.3 6.7 all-to-all-start.3
  106.3 13.6 %collective-permute-done.3 = bf16[256,2304]{1,0:T(8,128)(2,1)} collective-permute-done((bf16[256,2304]{1,0:T(8,128)(2,1)}, bf16[256,2304]{1,0:T(8,128)(2,1)}, u32[]{:S(2)}, u32[]{:S(2)}) %collective-permute-start.3) | collective-permute-done | bytes 1179680 | tf_op jit(solution)/shard_map/ppermute | solution.py:364
  128.9 5.0 collective-permute-done.5
  147.1 16.9 %all-to-all-done.3 = bf16[4,64,2304]{2,1,0:T(8,128)(2,1)S(1)} async-done(((bf16[4,64,2304]{2,1,0:T(8,128)(2,1)}), bf16[4,64,2304]{2,1,0:T(8,128)(2,1)S(1)}, u32[]{:S(2)}, u32[]{:S(2)}) %all-to-all-start.3) | async-done | bytes 1179680 | tf_op jit(solution)/shard_map/all_to_all | solution.py:399
  165.4 4.6 collective-permute-start.12
  172.2 7.9 copy.245.refs_0_
  182.7 7.8 collective-permute-done.11.refs_1_
  192.5 4.8 collective-permute-start.18
  205.5 15.9 %fusion.70.raw_ref.refs_1_ = f32[2048,1024]{1,0:T(8,128)} fusion(bf16[2048,2304]{1,0:T(8,128)(2,1)} %after.44, bf16[2304,1024]{1,0:T(8,128)(2,1)} %all-gather.5.cloned.1.call-done), kind=kOutput, calls=%fused_computation.297 | convolution fusion | flops 9663676416 | bytes 22544384 | tf_op jit(solution)/shard_map/dot_general | solution.py:98
  221.4 3.6 all-gather.7.cloned.1.call-done.refs_0_
  225.0 4.3 all-to-all-start.4
  229.4 33.6 %attend.1 = (bf16[2048,384]{1,0:T(8,128)(2,1)S(1)}, bf16[3,2048,384]{2,1,0:T(8,128)(2,1)S(1)}) custom-call(s32[33]{0:T(128)S(1)} %pad_add_fusion.index_ref, f32[2048,1024]{1,0:T(8,128)} %fusion.70.raw_ref.refs_1_, f32[1280,128]{1,0:T(8,128)S(1)} %get-tuple-element.137.cos_ref, f32[1280,128]{1,0:T(8,128)S(1)} %get-tuple-element.136.sin_ref), custom_call_target="tpu_custom_call" | custom-call | flops 35999997952 | bytes 1048576 | tf_op jit(solution)/shard_map/attend/pallas_call | solution.py:187
  300.8 19.0 %collective-permute-done.17.refs_0_ = bf16[256,2304]{1,0:T(8,128)(2,1)S(1)} collective-permute-done((bf16[256,2304]{1,0:T(8,128)(2,1)S(1)}, bf16[256,2304]{1,0:T(8,128)(2,1)S(1)}, u32[]{:S(2)}, u32[]{:S(2)}) %collective-permute-start.17) | collective-permute-done | bytes 1179680 | tf_op jit(solution)/shard_map/ppermute | solution.py:364
  320.8 24.4 %collective-permute-done.25.refs_0_ = bf16[256,2304]{1,0:T(8,128)(2,1)} collective-permute-done((bf16[256,2304]{1,0:T(8,128)(2,1)}, bf16[256,2304]{1,0:T(8,128)(2,1)}, u32[]{:S(2)}, u32[]{:S(2)}) %collective-permute-start.25) | collective-permute-done | bytes 1179680 | tf_op jit(solution)/shard_map/ppermute | solution.py:364
  346.5 4.2 multiply_reduce_fusion.2
  356.1 24.0 %collective-permute-done.28 = bf16[256,2304]{1,0:T(8,128)(2,1)} collective-permute-done((bf16[256,2304]{1,0:T(8,128)(2,1)}, bf16[256,2304]{1,0:T(8,128)(2,1)}, u32[]{:S(2)}, u32[]{:S(2)}) %collective-permute-start.28) | collective-permute-done | bytes 1179680 | tf_op jit(solution)/shard_map/ppermute | solution.py:364
  388.6 5.8 collective-permute-done.30
  403.9 19.5 %fusion.71 = f32[2048,1536]{1,0:T(8,128)S(1)} fusion(bf16[2048,2304]{1,0:T(8,128)(2,1)} %constant_dynamic-update-slice_fusion.18, bf16[2304,1536]{1,0:T(8,128)(2,1)} %all-gather.9.cloned.1.call-done), kind=kOutput, calls=%fused_computation.298 | convolution fusion | flops 14495514624 | bytes 29097984 | tf_op jit(solution)/shard_map/dot_general | solution.py:98
  423.4 4.6 copy-done.18
  430.1 13.9 %convolution_convert_fusion.6 = bf16[768,2304]{1,0:T(8,128)(2,1)} fusion(bf16[2048,768]{1,0:T(8,128)(2,1)S(1)} %multiply_convert_fusion.2.refs_0_, bf16[2048,2304]{1,0:T(8,128)(2,1)} %constant_dynamic-update-slice_fusion.9.refs_1_.refs_0_), kind=kOutput, calls=%fused_computation.16 | convolution fusion | flops 7249526784 | bytes 16121856 | tf_op jit(solution)/shard_map/dot_general | solution.py:94
  444.1 16.2 %multiply_convert_fusion = (bf16[2048,768]{1,0:T(8,128)(2,1)S(1)}, bf16[2048,768]{1,0:T(8,128)(2,1)S(1)}) fusion(f32[2048,1536]{1,0:T(8,128)} %copy-done.18, bf16[2048,2304]{1,0:T(8,128)(2,1)} %after.52, bf16[768,2304]{1,0:T(8,128)(2,1)} %all-gather.11.cloned.1.call-done), kind=kOutput, calls=%fused_computation.6 | convolution fusion | flops 7268204544 | bytes 31850496 | tf_op jit(solution)/shard_map/dot_general | solution.py:90
  460.3 12.8 %convolution_convert_fusion.2 = bf16[1024,2304]{1,0:T(8,128)(2,1)S(1)} fusion(bf16[2304,1536]{1,0:T(8,128)(2,1)} %all-gather.9.cloned.1.call-done, bf16[2048,768]{1,0:T(8,128)(2,1)S(1)} %get-tuple-element.34, bf16[2048,768]{1,0:T(8,128)(2,1)S(1)} %get-tuple-element.33), kind=kOutput, calls=%fused_computation.12 | convolution fusion | flops 7256408064 | bytes 18087936 | tf_op jit(solution)/shard_map/dot_general | solution.py:90
  476.5 10.6 %fusion.2 = f32[1024,2304]{1,0:T(8,128)S(1)} fusion(bf16[2304,1536]{1,0:T(8,128)(2,1)} %all-gather.9.cloned.1.call-done, bf16[2048,768]{1,0:T(8,128)(2,1)} %copy-done.36, bf16[2048,768]{1,0:T(8,128)(2,1)} %copy-done.35), kind=kOutput, calls=%fused_computation.23 | convolution fusion | flops 7254048768 | bytes 22806528 | tf_op jit(solution)/shard_map/dot_general | solution.py:90
  487.1 9.3 pad_maximum_fusion.refs_0_
  496.4 4.9 fusion.27
  504.0 19.3 %convolution_convert_fusion = bf16[2304,1536]{1,0:T(8,128)(2,1)S(1)} fusion(bf16[2048,2304]{1,0:T(8,128)(2,1)} %constant_dynamic-update-slice_fusion.18, bf16[2048,1536]{1,0:T(8,128)(2,1)} %after.54), kind=kOutput, calls=%fused_computation | convolution fusion | flops 14499053568 | bytes 22806528 | tf_op jit(solution)/shard_map/dot_general | solution.py:94
  523.3 3.4 copy.179
  526.8 3.5 collective-permute-done.38.refs_0_
  530.2 25.1 %collective-permute-done.40.refs_0_ = bf16[256,2304]{1,0:T(8,128)(2,1)} collective-permute-done((bf16[256,2304]{1,0:T(8,128)(2,1)}, bf16[256,2304]{1,0:T(8,128)(2,1)}, u32[]{:S(2)}, u32[]{:S(2)}) %collective-permute-start.40) | collective-permute-done | bytes 1179680 | tf_op jit(solution)/shard_map/ppermute | solution.py:364
  556.7 5.1 multiply_reduce_fusion
  568.4 6.3 convolution_convert_fusion.1
  578.1 6.6 fusion.37
  584.7 8.8 collective-permute-done.45
  599.2 7.1 fusion.22
  606.4 4.1 collective-permute-done.47
  618.0 4.0 fusion.72
  622.2 6.3 convolution_convert_fusion.7.refs_0_
  637.4 55.2 %attend_back.1.refs_0_ = bf16[2048,1024]{1,0:T(8,128)(2,1)} custom-call(s32[33]{0:T(128)S(1)} %pad_add_fusion.index_ref, bf16[3,2048,384]{2,1,0:T(8,128)(2,1)} %copy-done.5, bf16[2048,384]{1,0:T(8,128)(2,1)S(1)} %copy-done.2, f32[1280,128]{1,0:T(8,128)S(1)} %get-tuple-element.137.cos_ref, f32[1280,128]{1,0:T(8,128)S(1)} %get-tuple-element.136.sin_ref), custom_call_target="tpu_custom_call" | custom-call | bytes 1048576 | tf_op jit(solution)/shard_map/attend_back/pallas_call | solution.py:308
  692.7 4.9 all-to-all-start.5
  697.6 13.8 %convolution_convert_fusion.5 = bf16[2304,1024]{1,0:T(8,128)(2,1)S(1)} fusion(bf16[2048,2304]{1,0:T(8,128)(2,1)} %constant_dynamic-update-slice_fusion.refs_1_.refs_2_, bf16[2048,1024]{1,0:T(8,128)(2,1)} %after.63.refs_1_.refs_0_), kind=kOutput, calls=%fused_computation.15 | convolution fusion | flops 9666035712 | bytes 18350080 | tf_op jit(solution)/shard_map/dot_general | solution.py:94
  718.5 8.7 convolution_convert_fusion.4
  731.9 7.4 fusion.34
  747.8 21.0 %collective-permute-done.70 = bf16[72,2304]{1,0:T(8,128)(2,1)S(1)} collective-permute-done((bf16[72,2304]{1,0:T(8,128)(2,1)S(1)}, bf16[72,2304]{1,0:T(8,128)(2,1)S(1)}, u32[]{:S(2)}, u32[]{:S(2)}) %collective-permute-start.70) | collective-permute-done | bytes 331808 | tf_op jit(solution)/shard_map/ppermute | solution.py:364
  774.8 4.9 add_convert_fusion.refs_1_
  779.7 5.3 reshape.342
  788.3 3.2 reshape.355.refs_1_
  794.3 3.2 reshape.356.refs_2_
  797.9 26.1 %collective-permute-done.65.refs_0_ = bf16[256,2304]{1,0:T(8,128)(2,1)} collective-permute-done((bf16[256,2304]{1,0:T(8,128)(2,1)}, bf16[256,2304]{1,0:T(8,128)(2,1)}, u32[]{:S(2)}, u32[]{:S(2)}) %collective-permute-start.65) | collective-permute-done | bytes 1179680 | tf_op jit(solution)/shard_map/ppermute | solution.py:364
  824.0 5.1 fusion.10
  830.6 4.1 fusion.16.refs_0_
  834.7 4.0 all-to-all-start.6
  838.6 10.9 %collective-permute-start.71 = (bf16[180,2304]{1,0:T(8,128)(2,1)}, bf16[180,2304]{1,0:T(8,128)(2,1)}, u32[]{:S(2)}, u32[]{:S(2)}) collective-permute-start(bf16[180,2304]{1,0:T(8,128)(2,1)} %after.78), channel_id=1, source_target_pairs={{0,0},{1,4},{2,8},{3,12},{4,16},{5,20},{6,24},{7,28},{8,1},{9,5},{... | collective-permute-start | bytes 2488328 | tf_op jit(solution)/shard_map/ppermute | solution.py:364
  851.9 5.3 collective-permute-start.69
  860.8 5.9 collective-permute-start.66
  872.0 27.6 %all-to-all-done.6.refs_1_ = bf16[8,72,1024]{2,1,0:T(8,128)(2,1)S(1)} async-done(((bf16[8,72,1024]{2,1,0:T(8,128)(2,1)}), bf16[8,72,1024]{2,1,0:T(8,128)(2,1)S(1)}, u32[]{:S(2)}, u32[]{:S(2)}) %all-to-all-start.6) | async-done | bytes 1179680 | tf_op jit(solution)/shard_map/all_to_all | solution.py:636
  902.0 21.8 %all-to-all-start.7 = ((f32[32,1,144]{2,1,0:T(1,128)}), f32[32,1,144]{2,1,0:T(1,128)S(1)}, u32[]{:S(2)}, u32[]{:S(2)}) async-start(f32[32,1,144]{2,1,0:T(1,128)} %copy.202), calls=%async_computation.11 | async-start | bytes 65536 | tf_op jit(solution)/shard_map/all_to_all | solution.py:729
  (490 shorter events, 266.4 us)
Async XLA Ops:
  9.7 19.7 %all-to-all-start = ((bf16[4,64,2304]{2,1,0:T(8,128)(2,1)}), bf16[4,64,2304]{2,1,0:T(8,128)(2,1)}, u32[]{:S(2)}, u32[]{:S(2)}) async-start(bf16[4,64,2304]{2,1,0:T(8,128)(2,1)} %bitcast.191), calls=%async_computation | async-start | bytes 2359296 | tf_op jit(solution)/shard_map/all_to_all | solution.py:396
  31.9 36.9 %all-to-all-start.1 = ((bf16[4,72,2304]{2,1,0:T(8,128)(2,1)}), bf16[4,72,2304]{2,1,0:T(8,128)(2,1)}, u32[]{:S(2)}, u32[]{:S(2)}) async-start(bf16[4,72,2304]{2,1,0:T(8,128)(2,1)} %pad_maximum_fusion.2), calls=%async_computation.1 | async-start | bytes 2654208 | tf_op jit(solution)/shard_map/all_to_all | solution.py:464
  49.7 16.6 %collective-permute-start.13 = (bf16[288,1024]{1,0:T(8,128)(2,1)}, bf16[288,1024]{1,0:T(8,128)(2,1)}, u32[]{:S(2)}, u32[]{:S(2)}) collective-permute-start(bf16[288,1024]{1,0:T(8,128)(2,1)} %broadcast_select_fusion.6), channel_id=1, source_target_pairs={{0,1},{1,0},{2,3},{3,2},{4,5},{5,4},{6,7},{7,6},{8,9},{9,8},{10,11... | collective-permute-start | bytes 1769480 | tf_op jit(solution)/shard_map/ppermute | solution.py:364
  68.7 19.0 %all-to-all-start.2 = ((bf16[4,64,2304]{2,1,0:T(8,128)(2,1)}), bf16[4,64,2304]{2,1,0:T(8,128)(2,1)}, u32[]{:S(2)}, u32[]{:S(2)}) async-start(bf16[4,64,2304]{2,1,0:T(8,128)(2,1)} %bitcast.178), calls=%async_computation.2 | async-start | bytes 2359296 | tf_op jit(solution)/shard_map/all_to_all | solution.py:396
  73.0 132.5 %all-gather.5.cloned.1.call-start = ((), (), s32[]{:S(2)}) async-start(), calls=%async_computation.12 | async-start | bytes 5898240 | tf_op jit(solution)/shard_map/all_gather | solution.py:510
  93.4 26.5 %collective-permute-start.3 = (bf16[256,2304]{1,0:T(8,128)(2,1)}, bf16[256,2304]{1,0:T(8,128)(2,1)}, u32[]{:S(2)}, u32[]{:S(2)}) collective-permute-start(bf16[256,2304]{1,0:T(8,128)(2,1)} %get-tuple-element.32), channel_id=1, source_target_pairs={{0,8},{1,9},{2,10},{3,11},{4,12},{5,13},{6,14},{7,15},{8,0},{9,1},... | collective-permute-start | bytes 3538952 | tf_op jit(solution)/shard_map/ppermute | solution.py:364
  94.5 27.7 %collective-permute-start.4 = (bf16[256,2304]{1,0:T(8,128)(2,1)}, bf16[256,2304]{1,0:T(8,128)(2,1)S(1)}, u32[]{:S(2)}, u32[]{:S(2)}) collective-permute-start(bf16[256,2304]{1,0:T(8,128)(2,1)} %get-tuple-element.32), channel_id=1, source_target_pairs={{0,16},{1,17},{2,18},{3,19},{4,20},{5,21},{6,22},{7,23},{8,24},{9,... | collective-permute-start | bytes 3538952 | tf_op jit(solution)/shard_map/ppermute | solution.py:364
  94.9 52.2 %collective-permute-start.1 = (s32[1,16]{1,0:T(1,128)S(1)}, s32[1,16]{1,0:T(1,128)S(1)}, u32[]{:S(2)}, u32[]{:S(2)}) collective-permute-start(s32[1,16]{1,0:T(1,128)S(1)} %copy-done.65), channel_id=1, source_target_pairs={{0,0},{1,1},{2,8},{3,9},{4,16},{5,17},{6,24},{7,25},{8,2},{9,3},{1... | collective-permute-start | bytes 200 | tf_op jit(solution)/shard_map/ppermute | solution.py:364
  97.3 66.7 %all-to-all-start.3 = ((bf16[4,64,2304]{2,1,0:T(8,128)(2,1)}), bf16[4,64,2304]{2,1,0:T(8,128)(2,1)S(1)}, u32[]{:S(2)}, u32[]{:S(2)}) async-start(bf16[4,64,2304]{2,1,0:T(8,128)(2,1)} %after.42), calls=%async_computation.3 | async-start | bytes 2359296 | tf_op jit(solution)/shard_map/all_to_all | solution.py:399
  104.0 121.0 %all-gather.7.cloned.1.call-start = ((), (), s32[]{:S(2)}) async-start(), calls=%async_computation.13 | async-start | bytes 1658880 | tf_op jit(solution)/shard_map/all_gather | solution.py:510
  104.0 36.0 %collective-permute-start.7 = (bf16[256,2304]{1,0:T(8,128)(2,1)}, bf16[256,2304]{1,0:T(8,128)(2,1)S(1)}, u32[]{:S(2)}, u32[]{:S(2)}) collective-permute-start(bf16[256,2304]{1,0:T(8,128)(2,1)} %get-tuple-element.32), channel_id=1, source_target_pairs={{0,1},{1,0},{2,3},{3,2},{4,5},{5,4},{6,7},{7,6},{8,9},{9,8},{10,11... | collective-permute-start | bytes 3538952 | tf_op jit(solution)/shard_map/ppermute | solution.py:364
  122.6 18.5 %collective-permute-start.8 = (bf16[256,2304]{1,0:T(8,128)(2,1)}, bf16[256,2304]{1,0:T(8,128)(2,1)S(1)}, u32[]{:S(2)}, u32[]{:S(2)}) collective-permute-start(bf16[256,2304]{1,0:T(8,128)(2,1)} %collective-permute-done.3), channel_id=1, source_target_pairs={{0,1},{1,0},{2,3},{3,2},{4,5},{5,4},{6,7},{7,6},{8,9},{9,8},{10,11... | collective-permute-start | bytes 3538952 | tf_op jit(solution)/shard_map/ppermute | solution.py:364
  165.4 25.1 %collective-permute-start.11 = (bf16[256,2304]{1,0:T(8,128)(2,1)}, bf16[256,2304]{1,0:T(8,128)(2,1)}, u32[]{:S(2)}, u32[]{:S(2)}) collective-permute-start(bf16[256,2304]{1,0:T(8,128)(2,1)} %after.43), channel_id=1, source_target_pairs={{0,8},{1,9},{2,10},{3,11},{4,12},{5,13},{6,14},{7,15},{8,0},{9,1},... | collective-permute-start | bytes 3538952 | tf_op jit(solution)/shard_map/ppermute | solution.py:364
  165.4 31.8 %collective-permute-start.12 = (bf16[256,2304]{1,0:T(8,128)(2,1)}, bf16[256,2304]{1,0:T(8,128)(2,1)}, u32[]{:S(2)}, u32[]{:S(2)}) collective-permute-start(bf16[256,2304]{1,0:T(8,128)(2,1)} %after.43), channel_id=1, source_target_pairs={{0,16},{1,17},{2,18},{3,19},{4,20},{5,21},{6,22},{7,23},{8,24},{9,... | collective-permute-start | bytes 3538952 | tf_op jit(solution)/shard_map/ppermute | solution.py:364
  170.5 120.4 %collective-permute-start.20 = (bf16[256,2304]{1,0:T(8,128)(2,1)}, bf16[256,2304]{1,0:T(8,128)(2,1)}, u32[]{:S(2)}, u32[]{:S(2)}) collective-permute-start(bf16[256,2304]{1,0:T(8,128)(2,1)} %after.43), channel_id=1, source_target_pairs={{0,1},{1,0},{2,3},{3,2},{4,5},{5,4},{6,7},{7,6},{8,9},{9,8},{10,11... | collective-permute-start | bytes 3538952 | tf_op jit(solution)/shard_map/ppermute | solution.py:364
  180.1 223.7 %all-gather.9.cloned.1.call-start = ((), (), s32[]{:S(2)}) async-start(), calls=%async_computation.14 | async-start | bytes 8847360 | tf_op jit(solution)/shard_map/all_gather | solution.py:510
  192.5 85.0 %collective-permute-start.18 = (bf16[128,2304]{1,0:T(8,128)(2,1)}, bf16[128,2304]{1,0:T(8,128)(2,1)}, u32[]{:S(2)}, u32[]{:S(2)}) collective-permute-start(bf16[128,2304]{1,0:T(8,128)(2,1)} %slice.484), channel_id=1, source_target_pairs={{0,16},{1,17},{2,18},{3,19},{4,20},{5,21},{6,22},{7,23},{8,24},{9,... | collective-permute-start | bytes 1769480 | tf_op jit(solution)/shard_map/ppermute | solution.py:364
  199.2 80.8 %collective-permute-start.19 = (bf16[128,2304]{1,0:T(8,128)(2,1)}, bf16[128,2304]{1,0:T(8,128)(2,1)}, u32[]{:S(2)}, u32[]{:S(2)}) collective-permute-start(bf16[128,2304]{1,0:T(8,128)(2,1)} %slice.485), channel_id=1, source_target_pairs={{0,8},{1,9},{2,10},{3,11},{4,12},{5,13},{6,14},{7,15},{8,0},{9,1},... | collective-permute-start | bytes 1769480 | tf_op jit(solution)/shard_map/ppermute | solution.py:364
  200.5 92.9 %collective-permute-start.21 = (bf16[256,2304]{1,0:T(8,128)(2,1)}, bf16[256,2304]{1,0:T(8,128)(2,1)}, u32[]{:S(2)}, u32[]{:S(2)}) collective-permute-start(bf16[256,2304]{1,0:T(8,128)(2,1)} %collective-permute-done.11.refs_1_), channel_id=1, source_target_pairs={{0,1},{1,0},{2,3},{3,2},{4,5},{5,4},{6,7},{7,6},{8,9},{9,8},{10,11... | collective-permute-start | bytes 3538952 | tf_op jit(solution)/shard_map/ppermute | solution.py:364
  225.0 40.1 %all-to-all-start.4 = ((bf16[4,72,2304]{2,1,0:T(8,128)(2,1)}), bf16[4,72,2304]{2,1,0:T(8,128)(2,1)}, u32[]{:S(2)}, u32[]{:S(2)}) async-start(bf16[4,72,2304]{2,1,0:T(8,128)(2,1)} %bitcast.186), calls=%async_computation.4 | async-start | bytes 2654208 | tf_op jit(solution)/shard_map/all_to_all | solution.py:550
  229.3 214.8 %all-gather.11.cloned.1.call-start = ((), (), s32[]{:S(2)}) async-start(), calls=%async_computation.15 | async-start | bytes 4423680 | tf_op jit(solution)/shard_map/all_gather | solution.py:510
  286.7 58.6 %collective-permute-start.15 = (bf16[256,2304]{1,0:T(8,128)(2,1)}, bf16[256,2304]{1,0:T(8,128)(2,1)}, u32[]{:S(2)}, u32[]{:S(2)}) collective-permute-start(bf16[256,2304]{1,0:T(8,128)(2,1)} %get-tuple-element.61), channel_id=1, source_target_pairs={{0,1},{1,0},{2,3},{3,2},{4,5},{5,4},{6,7},{7,6},{8,9},{9,8},{10,11... | collective-permute-start | bytes 3538952 | tf_op jit(solution)/shard_map/ppermute | solution.py:364
  290.9 28.9 %collective-permute-start.17 = (bf16[256,2304]{1,0:T(8,128)(2,1)S(1)}, bf16[256,2304]{1,0:T(8,128)(2,1)S(1)}, u32[]{:S(2)}, u32[]{:S(2)}) collective-permute-start(bf16[256,2304]{1,0:T(8,128)(2,1)S(1)} %get-tuple-element.46), channel_id=1, source_target_pairs={{0,24},{1,25},{2,26},{3,27},{4,28},{5,29},{6,30},{7,31},{8,16},{9,... | collective-permute-start | bytes 3538952 | tf_op jit(solution)/shard_map/ppermute | solution.py:364
  293.4 51.8 %collective-permute-start.25 = (bf16[256,2304]{1,0:T(8,128)(2,1)}, bf16[256,2304]{1,0:T(8,128)(2,1)}, u32[]{:S(2)}, u32[]{:S(2)}) collective-permute-start(bf16[256,2304]{1,0:T(8,128)(2,1)} %get-tuple-element.48), channel_id=1, source_target_pairs={{0,8},{1,9},{2,10},{3,11},{4,12},{5,13},{6,14},{7,15},{8,0},{9,1},... | collective-permute-start | bytes 3538952 | tf_op jit(solution)/shard_map/ppermute | solution.py:364
  293.7 51.5 %collective-permute-start.27 = (bf16[256,2304]{1,0:T(8,128)(2,1)}, bf16[256,2304]{1,0:T(8,128)(2,1)}, u32[]{:S(2)}, u32[]{:S(2)}) collective-permute-start(bf16[256,2304]{1,0:T(8,128)(2,1)} %get-tuple-element.47), channel_id=1, source_target_pairs={{0,16},{1,17},{2,18},{3,19},{4,20},{5,21},{6,22},{7,23},{8,24},{9,... | collective-permute-start | bytes 3538952 | tf_op jit(solution)/shard_map/ppermute | solution.py:364
  353.1 27.0 %collective-permute-start.28 = (bf16[256,2304]{1,0:T(8,128)(2,1)}, bf16[256,2304]{1,0:T(8,128)(2,1)}, u32[]{:S(2)}, u32[]{:S(2)}) collective-permute-start(bf16[256,2304]{1,0:T(8,128)(2,1)} %get-tuple-element.28), channel_id=1, source_target_pairs={{0,8},{1,9},{2,10},{3,11},{4,12},{5,13},{6,14},{7,15},{8,0},{9,1},... | collective-permute-start | bytes 3538952 | tf_op jit(solution)/shard_map/ppermute | solution.py:364
  354.3 27.4 %collective-permute-start.29 = (bf16[256,2304]{1,0:T(8,128)(2,1)}, bf16[256,2304]{1,0:T(8,128)(2,1)S(1)}, u32[]{:S(2)}, u32[]{:S(2)}) collective-permute-start(bf16[256,2304]{1,0:T(8,128)(2,1)} %get-tuple-element.28), channel_id=1, source_target_pairs={{0,16},{1,17},{2,18},{3,19},{4,20},{5,21},{6,22},{7,23},{8,24},{9,... | collective-permute-start | bytes 3538952 | tf_op jit(solution)/shard_map/ppermute | solution.py:364
  354.6 279.2 %reduce-scatter.5.cloned.1.call-start = ((), (), s32[]{:S(2)}) async-start(), calls=%async_computation.16 | async-start | bytes 4423680 | tf_op jit(solution)/shard_map/reduce_scatter | solution.py:651
  354.6 44.8 %collective-permute-start.32 = (bf16[256,2304]{1,0:T(8,128)(2,1)}, bf16[256,2304]{1,0:T(8,128)(2,1)S(1)}, u32[]{:S(2)}, u32[]{:S(2)}) collective-permute-start(bf16[256,2304]{1,0:T(8,128)(2,1)} %get-tuple-element.28), channel_id=1, source_target_pairs={{0,1},{1,0},{2,3},{3,2},{4,5},{5,4},{6,7},{7,6},{8,9},{9,8},{10,11... | collective-permute-start | bytes 3538952 | tf_op jit(solution)/shard_map/ppermute | solution.py:364
  382.8 17.7 %collective-permute-start.33 = (bf16[256,2304]{1,0:T(8,128)(2,1)}, bf16[256,2304]{1,0:T(8,128)(2,1)S(1)}, u32[]{:S(2)}, u32[]{:S(2)}) collective-permute-start(bf16[256,2304]{1,0:T(8,128)(2,1)} %collective-permute-done.28), channel_id=1, source_target_pairs={{0,1},{1,0},{2,3},{3,2},{4,5},{5,4},{6,7},{7,6},{8,9},{9,8},{10,11... | collective-permute-start | bytes 3538952 | tf_op jit(solution)/shard_map/ppermute | solution.py:364
  444.0 248.6 %reduce-scatter.7.cloned.1.call-start = ((), (), s32[]{:S(2)}) async-start(), calls=%async_computation.17 | async-start | bytes 8847360 | tf_op jit(solution)/shard_map/reduce_scatter | solution.py:632
  475.4 21.0 %collective-permute-start.37 = (bf16[256,2304]{1,0:T(8,128)(2,1)}, bf16[256,2304]{1,0:T(8,128)(2,1)S(1)}, u32[]{:S(2)}, u32[]{:S(2)}) collective-permute-start(bf16[256,2304]{1,0:T(8,128)(2,1)} %get-tuple-element.60), channel_id=1, source_target_pairs={{0,1},{1,0},{2,3},{3,2},{4,5},{5,4},{6,7},{7,6},{8,9},{9,8},{10,11... | collective-permute-start | bytes 3538952 | tf_op jit(solution)/shard_map/ppermute | solution.py:364
  475.4 21.0 %collective-permute-start.39 = (bf16[256,2304]{1,0:T(8,128)(2,1)}, bf16[256,2304]{1,0:T(8,128)(2,1)}, u32[]{:S(2)}, u32[]{:S(2)}) collective-permute-start(bf16[256,2304]{1,0:T(8,128)(2,1)} %get-tuple-element.59), channel_id=1, source_target_pairs={{0,1},{1,0},{2,3},{3,2},{4,5},{5,4},{6,7},{7,6},{8,9},{9,8},{10,11... | collective-permute-start | bytes 3538952 | tf_op jit(solution)/shard_map/ppermute | solution.py:364
  475.9 20.5 %collective-permute-start.41 = (bf16[256,2304]{1,0:T(8,128)(2,1)}, bf16[256,2304]{1,0:T(8,128)(2,1)}, u32[]{:S(2)}, u32[]{:S(2)}) collective-permute-start(bf16[256,2304]{1,0:T(8,128)(2,1)} %get-tuple-element.58), channel_id=1, source_target_pairs={{0,1},{1,0},{2,3},{3,2},{4,5},{5,4},{6,7},{7,6},{8,9},{9,8},{10,11... | collective-permute-start | bytes 3538952 | tf_op jit(solution)/shard_map/ppermute | solution.py:364
  475.9 80.8 %collective-permute-start.36 = (bf16[256,2304]{1,0:T(8,128)(2,1)}, bf16[256,2304]{1,0:T(8,128)(2,1)}, u32[]{:S(2)}, u32[]{:S(2)}) collective-permute-start(bf16[256,2304]{1,0:T(8,128)(2,1)} %get-tuple-element.57), channel_id=1, source_target_pairs={{0,1},{1,0},{2,3},{3,2},{4,5},{5,4},{6,7},{7,6},{8,9},{9,8},{10,11... | collective-permute-start | bytes 3538952 | tf_op jit(solution)/shard_map/ppermute | solution.py:364
  501.3 28.9 %collective-permute-start.38 = (bf16[256,2304]{1,0:T(8,128)(2,1)}, bf16[256,2304]{1,0:T(8,128)(2,1)}, u32[]{:S(2)}, u32[]{:S(2)}) collective-permute-start(bf16[256,2304]{1,0:T(8,128)(2,1)} %get-tuple-element.42), channel_id=1, source_target_pairs={{0,24},{1,25},{2,26},{3,27},{4,28},{5,29},{6,30},{7,31},{8,16},{9,... | collective-permute-start | bytes 3538952 | tf_op jit(solution)/shard_map/ppermute | solution.py:364
  503.2 52.0 %collective-permute-start.40 = (bf16[256,2304]{1,0:T(8,128)(2,1)}, bf16[256,2304]{1,0:T(8,128)(2,1)}, u32[]{:S(2)}, u32[]{:S(2)}) collective-permute-start(bf16[256,2304]{1,0:T(8,128)(2,1)} %get-tuple-element.44), channel_id=1, source_target_pairs={{0,8},{1,9},{2,10},{3,11},{4,12},{5,13},{6,14},{7,15},{8,0},{9,1},... | collective-permute-start | bytes 3538952 | tf_op jit(solution)/shard_map/ppermute | solution.py:364
  503.5 52.2 %collective-permute-start.42 = (bf16[256,2304]{1,0:T(8,128)(2,1)}, bf16[256,2304]{1,0:T(8,128)(2,1)S(1)}, u32[]{:S(2)}, u32[]{:S(2)}) collective-permute-start(bf16[256,2304]{1,0:T(8,128)(2,1)} %get-tuple-element.43), channel_id=1, source_target_pairs={{0,16},{1,17},{2,18},{3,19},{4,20},{5,21},{6,22},{7,23},{8,24},{9,... | collective-permute-start | bytes 3538952 | tf_op jit(solution)/shard_map/ppermute | solution.py:364
  526.7 187.5 %reduce-scatter.9.cloned.1.call-start = ((), (), s32[]{:S(2)}) async-start(), calls=%async_computation.18 | async-start | bytes 1658880 | tf_op jit(solution)/shard_map/reduce_scatter | solution.py:670
  566.2 27.3 %collective-permute-start.45 = (bf16[256,2304]{1,0:T(8,128)(2,1)S(1)}, bf16[256,2304]{1,0:T(8,128)(2,1)S(1)}, u32[]{:S(2)}, u32[]{:S(2)}) collective-permute-start(bf16[256,2304]{1,0:T(8,128)(2,1)S(1)} %copy-done.30), channel_id=1, source_target_pairs={{0,8},{1,9},{2,10},{3,11},{4,12},{5,13},{6,14},{7,15},{8,0},{9,1},... | collective-permute-start | bytes 3538952 | tf_op jit(solution)/shard_map/ppermute | solution.py:364
  567.2 28.3 %collective-permute-start.46 = (bf16[256,2304]{1,0:T(8,128)(2,1)S(1)}, bf16[256,2304]{1,0:T(8,128)(2,1)S(1)}, u32[]{:S(2)}, u32[]{:S(2)}) collective-permute-start(bf16[256,2304]{1,0:T(8,128)(2,1)S(1)} %copy-done.30), channel_id=1, source_target_pairs={{0,16},{1,17},{2,18},{3,19},{4,20},{5,21},{6,22},{7,23},{8,24},{9,... | collective-permute-start | bytes 3538952 | tf_op jit(solution)/shard_map/ppermute | solution.py:364
  576.1 21.2 %collective-permute-start.44 = (bf16[256,2304]{1,0:T(8,128)(2,1)S(1)}, bf16[256,2304]{1,0:T(8,128)(2,1)S(1)}, u32[]{:S(2)}, u32[]{:S(2)}) collective-permute-start(bf16[256,2304]{1,0:T(8,128)(2,1)S(1)} %get-tuple-element.56), channel_id=1, source_target_pairs={{0,1},{1,0},{2,3},{3,2},{4,5},{5,4},{6,7},{7,6},{8,9},{9,8},{10,11... | collective-permute-start | bytes 3538952 | tf_op jit(solution)/shard_map/ppermute | solution.py:364
  577.0 21.5 %collective-permute-start.55 = (bf16[256,2304]{1,0:T(8,128)(2,1)S(1)}, bf16[256,2304]{1,0:T(8,128)(2,1)S(1)}, u32[]{:S(2)}, u32[]{:S(2)}) collective-permute-start(bf16[256,2304]{1,0:T(8,128)(2,1)S(1)} %get-tuple-element.55), channel_id=1, source_target_pairs={{0,1},{1,0},{2,3},{3,2},{4,5},{5,4},{6,7},{7,6},{8,9},{9,8},{10,11... | collective-permute-start | bytes 3538952 | tf_op jit(solution)/shard_map/ppermute | solution.py:364
  577.0 22.1 %collective-permute-start.57 = (bf16[256,2304]{1,0:T(8,128)(2,1)S(1)}, bf16[256,2304]{1,0:T(8,128)(2,1)S(1)}, u32[]{:S(2)}, u32[]{:S(2)}) collective-permute-start(bf16[256,2304]{1,0:T(8,128)(2,1)S(1)} %get-tuple-element.54), channel_id=1, source_target_pairs={{0,1},{1,0},{2,3},{3,2},{4,5},{5,4},{6,7},{7,6},{8,9},{9,8},{10,11... | collective-permute-start | bytes 3538952 | tf_op jit(solution)/shard_map/ppermute | solution.py:364
  593.5 20.0 %collective-permute-start.49 = (bf16[256,2304]{1,0:T(8,128)(2,1)S(1)}, bf16[256,2304]{1,0:T(8,128)(2,1)}, u32[]{:S(2)}, u32[]{:S(2)}) collective-permute-start(bf16[256,2304]{1,0:T(8,128)(2,1)S(1)} %copy-done.30), channel_id=1, source_target_pairs={{0,1},{1,0},{2,3},{3,2},{4,5},{5,4},{6,7},{7,6},{8,9},{9,8},{10,11... | collective-permute-start | bytes 3538952 | tf_op jit(solution)/shard_map/ppermute | solution.py:364
  599.1 17.1 %collective-permute-start.51 = (bf16[256,2304]{1,0:T(8,128)(2,1)S(1)}, bf16[256,2304]{1,0:T(8,128)(2,1)}, u32[]{:S(2)}, u32[]{:S(2)}) collective-permute-start(bf16[256,2304]{1,0:T(8,128)(2,1)S(1)} %collective-permute-done.46), channel_id=1, source_target_pairs={{0,1},{1,0},{2,3},{3,2},{4,5},{5,4},{6,7},{7,6},{8,9},{9,8},{10,11... | collective-permute-start | bytes 3538952 | tf_op jit(solution)/shard_map/ppermute | solution.py:364
  628.6 64.0 %collective-permute-start.58 = (bf16[256,2304]{1,0:T(8,128)(2,1)}, bf16[256,2304]{1,0:T(8,128)(2,1)}, u32[]{:S(2)}, u32[]{:S(2)}) collective-permute-start(bf16[256,2304]{1,0:T(8,128)(2,1)} %after.62), channel_id=1, source_target_pairs={{0,16},{1,17},{2,18},{3,19},{4,20},{5,21},{6,22},{7,23},{8,24},{9,... | collective-permute-start | bytes 3538952 | tf_op jit(solution)/shard_map/ppermute | solution.py:364
  629.2 63.4 %collective-permute-start.56 = (bf16[256,2304]{1,0:T(8,128)(2,1)}, bf16[256,2304]{1,0:T(8,128)(2,1)}, u32[]{:S(2)}, u32[]{:S(2)}) collective-permute-start(bf16[256,2304]{1,0:T(8,128)(2,1)} %after.61), channel_id=1, source_target_pairs={{0,8},{1,9},{2,10},{3,11},{4,12},{5,13},{6,14},{7,15},{8,0},{9,1},... | collective-permute-start | bytes 3538952 | tf_op jit(solution)/shard_map/ppermute | solution.py:364
  630.2 62.4 %collective-permute-start.53 = (bf16[256,2304]{1,0:T(8,128)(2,1)}, bf16[256,2304]{1,0:T(8,128)(2,1)}, u32[]{:S(2)}, u32[]{:S(2)}) collective-permute-start(bf16[256,2304]{1,0:T(8,128)(2,1)} %after.59), channel_id=1, source_target_pairs={{0,24},{1,25},{2,26},{3,27},{4,28},{5,29},{6,30},{7,31},{8,16},{9,... | collective-permute-start | bytes 3538952 | tf_op jit(solution)/shard_map/ppermute | solution.py:364
  692.7 24.5 %all-to-all-start.5 = ((bf16[8,72,1536]{2,1,0:T(8,128)(2,1)}), bf16[8,72,1536]{2,1,0:T(8,128)(2,1)S(1)}, u32[]{:S(2)}, u32[]{:S(2)}) async-start(bf16[8,72,1536]{2,1,0:T(8,128)(2,1)} %after.64), calls=%async_computation.8 | async-start | bytes 3538944 | tf_op jit(solution)/shard_map/all_to_all | solution.py:636
  697.6 137.1 %reduce-scatter.11.cloned.1.call-start = ((), (), s32[]{:S(2)}) async-start(), calls=%async_computation.19 | async-start | bytes 5898240 | tf_op jit(solution)/shard_map/reduce_scatter | solution.py:632
  743.6 28.4 %collective-permute-start.60 = (bf16[256,2304]{1,0:T(8,128)(2,1)S(1)}, bf16[256,2304]{1,0:T(8,128)(2,1)S(1)}, u32[]{:S(2)}, u32[]{:S(2)}) collective-permute-start(bf16[256,2304]{1,0:T(8,128)(2,1)S(1)} %get-tuple-element.37), channel_id=1, source_target_pairs={{0,8},{1,9},{2,10},{3,11},{4,12},{5,13},{6,14},{7,15},{8,0},{9,1},... | collective-permute-start | bytes 3538952 | tf_op jit(solution)/shard_map/ppermute | solution.py:364
  744.2 28.9 %collective-permute-start.43 = (bf16[256,2304]{1,0:T(8,128)(2,1)}, bf16[256,2304]{1,0:T(8,128)(2,1)}, u32[]{:S(2)}, u32[]{:S(2)}) collective-permute-start(bf16[256,2304]{1,0:T(8,128)(2,1)} %get-tuple-element.53), channel_id=1, source_target_pairs={{0,1},{1,0},{2,3},{3,2},{4,5},{5,4},{6,7},{7,6},{8,9},{9,8},{10,11... | collective-permute-start | bytes 3538952 | tf_op jit(solution)/shard_map/ppermute | solution.py:364
  744.9 23.8 %collective-permute-start.70 = (bf16[72,2304]{1,0:T(8,128)(2,1)S(1)}, bf16[72,2304]{1,0:T(8,128)(2,1)S(1)}, u32[]{:S(2)}, u32[]{:S(2)}) collective-permute-start(bf16[72,2304]{1,0:T(8,128)(2,1)S(1)} %bitcast.193), channel_id=1, source_target_pairs={{0,0},{1,4},{2,1},{3,5},{4,2},{5,6},{6,3},{7,7},{8,8},{9,12},{10,9... | collective-permute-start | bytes 995336 | tf_op jit(solution)/shard_map/ppermute | solution.py:364
  769.6 54.4 %collective-permute-start.61 = (bf16[256,2304]{1,0:T(8,128)(2,1)}, bf16[256,2304]{1,0:T(8,128)(2,1)}, u32[]{:S(2)}, u32[]{:S(2)}) collective-permute-start(bf16[256,2304]{1,0:T(8,128)(2,1)} %get-tuple-element.49), channel_id=1, source_target_pairs={{0,1},{1,0},{2,3},{3,2},{4,5},{5,4},{6,7},{7,6},{8,9},{9,8},{10,11... | collective-permute-start | bytes 3538952 | tf_op jit(solution)/shard_map/ppermute | solution.py:364
  769.6 28.3 %collective-permute-start.63 = (bf16[256,2304]{1,0:T(8,128)(2,1)}, bf16[256,2304]{1,0:T(8,128)(2,1)}, u32[]{:S(2)}, u32[]{:S(2)}) collective-permute-start(bf16[256,2304]{1,0:T(8,128)(2,1)} %get-tuple-element.35), channel_id=1, source_target_pairs={{0,24},{1,25},{2,26},{3,27},{4,28},{5,29},{6,30},{7,31},{8,16},{9,... | collective-permute-start | bytes 3538952 | tf_op jit(solution)/shard_map/ppermute | solution.py:364
  771.7 52.3 %collective-permute-start.65 = (bf16[256,2304]{1,0:T(8,128)(2,1)}, bf16[256,2304]{1,0:T(8,128)(2,1)}, u32[]{:S(2)}, u32[]{:S(2)}) collective-permute-start(bf16[256,2304]{1,0:T(8,128)(2,1)} %get-tuple-element.36), channel_id=1, source_target_pairs={{0,16},{1,17},{2,18},{3,19},{4,20},{5,21},{6,22},{7,23},{8,24},{9,... | collective-permute-start | bytes 3538952 | tf_op jit(solution)/shard_map/ppermute | solution.py:364
  834.7 64.9 %all-to-all-start.6 = ((bf16[8,72,1024]{2,1,0:T(8,128)(2,1)}), bf16[8,72,1024]{2,1,0:T(8,128)(2,1)S(1)}, u32[]{:S(2)}, u32[]{:S(2)}) async-start(bf16[8,72,1024]{2,1,0:T(8,128)(2,1)} %bitcast.181), calls=%async_computation.10 | async-start | bytes 2359296 | tf_op jit(solution)/shard_map/all_to_all | solution.py:636
  838.6 30.9 %collective-permute-start.71 = (bf16[180,2304]{1,0:T(8,128)(2,1)}, bf16[180,2304]{1,0:T(8,128)(2,1)}, u32[]{:S(2)}, u32[]{:S(2)}) collective-permute-start(bf16[180,2304]{1,0:T(8,128)(2,1)} %after.78), channel_id=1, source_target_pairs={{0,0},{1,4},{2,8},{3,12},{4,16},{5,20},{6,24},{7,28},{8,1},{9,5},{... | collective-permute-start | bytes 2488328 | tf_op jit(solution)/shard_map/ppermute | solution.py:364
  851.9 90.4 %collective-permute-start.69 = (bf16[1,128,2304]{2,1,0:T(8,128)(2,1)}, bf16[1,128,2304]{2,1,0:T(8,128)(2,1)S(1)}, u32[]{:S(2)}, u32[]{:S(2)}) collective-permute-start(bf16[1,128,2304]{2,1,0:T(8,128)(2,1)} %pad_maximum_fusion.11), channel_id=1, source_target_pairs={{0,6},{1,7},{2,12},{3,13},{4,18},{5,19},{6,24},{7,25},{8,4},{9,5},... | collective-permute-start | bytes 1769480 | tf_op jit(solution)/shard_map/ppermute | solution.py:364
  858.0 82.4 %collective-permute-start.68 = (bf16[1,128,2304]{2,1,0:T(8,128)(2,1)}, bf16[1,128,2304]{2,1,0:T(8,128)(2,1)}, u32[]{:S(2)}, u32[]{:S(2)}) collective-permute-start(bf16[1,128,2304]{2,1,0:T(8,128)(2,1)} %pad_maximum_fusion.10), channel_id=1, source_target_pairs={{0,4},{1,5},{2,14},{3,15},{4,16},{5,17},{6,26},{7,27},{8,6},{9,7},... | collective-permute-start | bytes 1769480 | tf_op jit(solution)/shard_map/ppermute | solution.py:364
  860.8 73.9 %collective-permute-start.66 = (bf16[1,128,2304]{2,1,0:T(8,128)(2,1)}, bf16[1,128,2304]{2,1,0:T(8,128)(2,1)}, u32[]{:S(2)}, u32[]{:S(2)}) collective-permute-start(bf16[1,128,2304]{2,1,0:T(8,128)(2,1)} %pad_maximum_fusion.8), channel_id=1, source_target_pairs={{0,0},{1,1},{2,10},{3,11},{4,20},{5,21},{6,30},{7,31},{8,2},{9,3},... | collective-permute-start | bytes 1769480 | tf_op jit(solution)/shard_map/ppermute | solution.py:364
  867.6 71.0 %collective-permute-start.67 = (bf16[1,128,2304]{2,1,0:T(8,128)(2,1)}, bf16[1,128,2304]{2,1,0:T(8,128)(2,1)}, u32[]{:S(2)}, u32[]{:S(2)}) collective-permute-start(bf16[1,128,2304]{2,1,0:T(8,128)(2,1)} %pad_maximum_fusion.9), channel_id=1, source_target_pairs={{0,2},{1,3},{2,8},{3,9},{4,22},{5,23},{6,28},{7,29},{8,0},{9,1},{1... | collective-permute-start | bytes 1769480 | tf_op jit(solution)/shard_map/ppermute | solution.py:364
  902.0 46.3 %all-to-all-start.7 = ((f32[32,1,144]{2,1,0:T(1,128)}), f32[32,1,144]{2,1,0:T(1,128)S(1)}, u32[]{:S(2)}, u32[]{:S(2)}) async-start(f32[32,1,144]{2,1,0:T(1,128)} %copy.202), calls=%async_computation.11 | async-start | bytes 65536 | tf_op jit(solution)/shard_map/all_to_all | solution.py:729
  (93 other events, 1043.6 us)
Sparse Core Ops, SparseCore 0:
  76.0 116.2 all-gather.4
  194.4 30.5 all-gather.6
  226.6 128.0 all-gather.8
  356.1 67.9 all-gather.10
  444.2 64.5 reduce-scatter.4
  526.8 121.9 reduce-scatter.6
  651.7 31.9 reduce-scatter.8
  714.3 87.1 reduce-scatter.10

commit v4 on v3

--- a/solution.py
+++ b/solution.py
@@ -616,13 +616,9 @@
 
         down_local = tn_dot(act, grad_m).astype(BF).reshape(n_tok, ff_tall, width)
         grad_act = nt_dot(after(grad_m, down_local), down_w)
-        grad_both = jnp.concatenate(
-            [
-                (grad_act * up_val * (sigma * (1.0 + gate * (1.0 - sigma)))).astype(BF),
-                (grad_act * silu).astype(BF),
-            ],
-            axis=1,
-        )
+        grad_gate = (grad_act * up_val * (sigma * (1.0 + gate * (1.0 - sigma)))).astype(BF)
+        grad_up = (grad_act * silu).astype(BF)
+
         def spread_rows(grad):
             columns = grad.shape[1]
             grad = grad.astype(BF).reshape(n_grp, n_tok, width // (n_grp * n_tok), columns)
@@ -632,15 +628,34 @@
             grad = lax.psum_scatter(grad, "tok", scatter_dimension=0, tiled=True)
             return grad.reshape(ranks, width // (ranks * n_tok), grad.shape[2])
 
-        def to_owners(grad):
+        def to_owners(grad, weight, spare):
+            weight = weight.reshape(n_grp, n_tok, width // (n_grp * n_tok), grad.shape[2])
+            weight = lax.dynamic_index_in_dim(weight, t, 1, keepdims=False).reshape(grad.shape)
+            total = jnp.sum(grad.astype(F32) * weight.astype(F32), axis=2, keepdims=True)
+            high = total.astype(BF)
+            low = (total - high.astype(F32)).astype(BF)
+            column = lax.broadcasted_iota(jnp.int32, grad.shape, 2)
+            grad = jnp.where(column == spare, high, jnp.where(column == spare + 1, low, grad))
             return lax.all_to_all(grad, LAYER, 0, 0, tiled=True)
 
-        pick = halves(grad_both)
-        parts = layer_send(pair_sum(lambda side, pick=pick: nt_dot(pick(side)[0], ff_weight)))
-        ff_local = spread_rows(tn_dot(h_two, after(grad_both, parts[0])))
+        def gain_of(got, spare):
+            return jnp.sum(got[..., spare : spare + 2].astype(F32), axis=(0, 2))
+
+        pick = halves(grad_gate, grad_up)
+        parts = layer_send(
+            pair_sum(
+                lambda side, pick=pick: nt_dot(pick(side)[0], ff_weight[:, :ff_wide])
+                + nt_dot(pick(side)[1], ff_weight[:, ff_wide:])
+            )
+        )
+        ff_local = spread_rows(
+            tn_dot(
+                h_two,
+                jnp.concatenate([after(grad_gate, parts[0]), after(grad_up, parts[0])], axis=1),
+            )
+        )
         grad_h2 = layer_add(parts, ff_local)
         ff_rows = sum_rows(ff_local)
-        gain_two_sum = jnp.sum(grad_h2 * normed_two, axis=0)
         pulled = grad_h2 * gain_two[None, :]
         grad_second = (
             grad_out
@@ -674,36 +689,41 @@
         grads = after(grads, ff_rows, *feed_parts[2])
         qkv_local = spread_rows(tn_dot(h_one, grads))
         qkv_rows = sum_rows(qkv_local)
-        got = to_owners(after(ff_rows, grads))
-        down_grad = send(
-            after(down_rows, qkv_rows),
-            lambda g, t, f: (t, (n_grp * f + g) // n_fs, (n_grp * f + g) % n_fs),
-        )
-        pick = halves(after(grads, qkv_local, output_grad, got))
+        ff_got = to_owners(after(ff_rows, grads), ff_weight, ff_piece)
+        pick = halves(after(grads, qkv_local, output_grad, ff_got))
         parts = layer_send(pair_sum(lambda side, pick=pick: nt_dot(pick(side)[0], qkv_weight)))
         feed = layer_add(feed_parts, parts[2][1])
         layer_output = (second_in + RESIDUAL * feed).astype(BF)
-        got = after(got, layer_output).reshape(n_grp, n_fs, -1, 2, n_tok, ff_tall)
-        gate_grad, up_grad = (
-            got[:, :, :, which, :, :ff_piece]
-            .transpose(2, 3, 1, 0, 4)
-            .reshape(-1, ff_width)
-            .astype(F32)
-            for which in range(2)
-        )
-        grad_h1 = layer_add(parts, (gate_grad, up_grad))
-        gain_one_sum = jnp.sum(grad_h1 * normed_one, axis=0)
+        grad_h1 = layer_add(parts)
         pulled = grad_h1 * gain_one[None, :]
         input_grad = (
             grad_second
             + scale_one * pulled
             - scale_one**3 * hidden * jnp.mean(pulled * hidden, axis=1, keepdims=True)
         )
-        input_grad = after(input_grad.astype(BF), qkv_rows)
+        input_grad = input_grad.astype(BF)
+        input_grad = after(input_grad, qkv_rows)
+        used = 5 * 3 * HEAD_DIM
+        got = to_owners(qkv_rows, qkv_weight, used)
+        down_grad = send(
+            after(down_rows, got),
+            lambda g, t, f: (t, (n_grp * f + g) // n_fs, (n_grp * f + g) % n_fs),
+        )
         output_grad = send(
-            output_grad[0], lambda g, t, f: (g, (n_tok * f + t) // n_fs, (n_tok * f + t) % n_fs)
-        ).astype(F32)
-        got = to_owners(qkv_rows)
+            after(output_grad[0], got),
+            lambda g, t, f: (g, (n_tok * f + t) // n_fs, (n_tok * f + t) % n_fs),
+        )
+        gain_one_grad = gain_of(got, used)
+        ff_got = after(ff_got, got)
+        gain_two_grad = gain_of(ff_got, ff_piece)
+        wide = ff_got.reshape(n_grp, n_fs, -1, 2, n_tok, ff_tall)
+        gate_grad, up_grad = (
+            wide[:, :, :, which, :, :ff_piece]
+            .transpose(2, 3, 1, 0, 4)
+            .reshape(-1, ff_width)
+            .astype(F32)
+            for which in range(2)
+        )
         own_rows = got.shape[1]
         here = got.astype(F32).reshape(n_grp, n_fs, own_rows, got.shape[2])
 
@@ -720,23 +740,21 @@
             return whole.transpose(1, 0, 2).reshape(own_rows, width)
 
         qkv_grads = [projection_grad(which) for which in range(3)]
-        layer_output, input_grad = shuffle_out((layer_output, input_grad), qkv_grads)
+        layer_output, input_grad = shuffle_out((layer_output, input_grad), (qkv_grads, gate_grad, up_grad))
         input_grad = input_grad.astype(F32)
-        gains = jnp.stack([gain_one_sum, gain_two_sum], axis=1).reshape(
-            n_grp * n_tok * n_fs, -1
-        )
-        gains = after(gains, got)
-        gains = jnp.sum(lax.all_to_all(gains, ALL, 0, 0, tiled=True), axis=0).reshape(-1, 2)
+        mine = ((g * n_tok + t) * n_fs + f) * own_rows
+        gain_one_grad = gain_one_grad / lax.dynamic_slice_in_dim(gain_one, mine, own_rows)
+        gain_two_grad = gain_two_grad / lax.dynamic_slice_in_dim(gain_two, mine, own_rows)
         return (
             layer_output,
             input_grad,
             *qkv_grads,
-            output_grad,
+            output_grad.astype(F32),
             gate_grad,
             up_grad,
             down_grad.astype(F32),
-            gains[:, 0],
-            gains[:, 1],
+            gain_one_grad,
+            gain_two_grad,
         )
 
     return local

time: 969 us -> 944 us (0.974)
  waiting for transfers between devices: 262 us -> 248 us
  matrix products: 167 us -> 178 us
    all_to_all x1 -> x0, starting transfers between devices: 21.8 us -> none  [local(): lax.all_to_all(gains, ALL, 0, 0, tiled=True)]
    all_to_all x2, waiting for transfers between devices: 30.6 us -> 12.8 us  [to_owners(): return lax.all_to_all(grad, LAYER, 0, 0, tiled=True)]
    ppermute x72, starting transfers between devices: 97.3 us -> 110 us  [send(): return lax.ppermute(array, ALL, permutation(move))]
    dot_general x6 -> x8, matrix products: 62 us -> 73.3 us  [nt_dot(): lax.dot_general(left, right, (((1,), (1,)), ((), ())), preferred_element_...]
    unnamed x170 -> x166, local copies, waits for them, and re-layouts: 71.2 us -> 64.6 us
  transfers between devices with their start and end apart: 88 -> 87, of which waited for: 23 -> 25; matrix products, arithmetic and copies ran while one was open for 43% -> 44% of each run, Pallas kernels for 9% -> 10%
where the time goes in v4:
time: 944 us; the launch traced here: 932 us
  waiting for transfers between devices  248 us (26%)
  matrix products  178 us (19%)
  local copies, waits for them, and re-layouts  157 us (17%)
  starting transfers between devices  144 us (15%)
  other arithmetic  101 us (11%)
  Pallas kernels  88.6 us (9%)
  between operations  16 us (2%)
    ppermute x72, waiting for transfers between devices, send(): return lax.ppermute(array, ALL, permutation(move))  196 us
    ppermute x72, starting transfers between devices, send(): return lax.ppermute(array, ALL, permutation(move))  110 us
    dot_general x8, matrix products, nt_dot(): lax.dot_general(left, right, (((1,), (1,)), ((), ())), preferred_element_...  73.3 us
    unnamed x166, local copies, waits for them, and re-layouts  64.6 us
    pallas_call x1, Pallas kernels, attend_back(): pl.pallas_call(functools.partial(attend_back_kernel, first), grid_spec=pl...  55.2 us
    dot_general x6, matrix products, nn_dot(): lax.dot_general(left, right, (((1,), (0,)), ((), ())), preferred_element_...  53.5 us
    dot_general x4, matrix products, tn_dot(): lax.dot_general(left, right, (((0,), (0,)), ((), ())), preferred_element_...  51.1 us
    pallas_call x1, Pallas kernels, attend(): pl.pallas_call(attend_kernel, grid_spec=pltpu.PrefetchScalarGridSpec(num_...  33.4 us
  transfers between devices with their start and end apart: 87, of which 25 were waited for; matrix products, arithmetic and copies ran while one was open for 44% of the time, Pallas kernels for 10%

profile of v4, /device:TPU:1, one launch (start us, length us, event | category | flops | bytes accessed | tf_op | source)
XLA Modules:
  0.0 932.2 jit_solution(229987274575482880)
XLA Ops:
  9.7 4.3 all-to-all-start
  16.1 13.3 %all-to-all-done.refs_1_ = bf16[4,64,2304]{2,1,0:T(8,128)(2,1)} async-done(((bf16[4,64,2304]{2,1,0:T(8,128)(2,1)}), bf16[4,64,2304]{2,1,0:T(8,128)(2,1)}, u32[]{:S(2)}, u32[]{:S(2)}) %all-to-all-start) | async-done | bytes 1179680 | tf_op jit(solution)/shard_map/all_to_all | solution.py:396
  31.9 4.6 all-to-all-start.1
  51.4 3.0 constant_dynamic-slice_fusion.39
  54.5 3.1 constant_dynamic-slice_fusion.35
  57.6 3.3 concatenate.91
  60.9 3.2 concatenate.90
  68.7 4.3 all-to-all-start.2
  81.3 6.4 all-to-all-done.2.refs_0_
  97.2 6.7 all-to-all-start.3
  106.3 13.6 %collective-permute-done.3 = bf16[256,2304]{1,0:T(8,128)(2,1)} collective-permute-done((bf16[256,2304]{1,0:T(8,128)(2,1)}, bf16[256,2304]{1,0:T(8,128)(2,1)}, u32[]{:S(2)}, u32[]{:S(2)}) %collective-permute-start.3) | collective-permute-done | bytes 1179680 | tf_op jit(solution)/shard_map/ppermute | solution.py:364
  128.9 5.0 collective-permute-done.5
  147.0 14.1 %all-to-all-done.3 = bf16[4,64,2304]{2,1,0:T(8,128)(2,1)S(1)} async-done(((bf16[4,64,2304]{2,1,0:T(8,128)(2,1)}), bf16[4,64,2304]{2,1,0:T(8,128)(2,1)S(1)}, u32[]{:S(2)}, u32[]{:S(2)}) %all-to-all-start.3) | async-done | bytes 1179680 | tf_op jit(solution)/shard_map/all_to_all | solution.py:399
  163.6 6.4 collective-permute-start.12
  170.4 7.9 copy.177.refs_0_
  186.8 10.4 %collective-permute-start.18 = (bf16[128,2304]{1,0:T(8,128)(2,1)}, bf16[128,2304]{1,0:T(8,128)(2,1)}, u32[]{:S(2)}, u32[]{:S(2)}) collective-permute-start(bf16[128,2304]{1,0:T(8,128)(2,1)} %slice.502), channel_id=1, source_target_pairs={{0,16},{1,17},{2,18},{3,19},{4,20},{5,21},{6,22},{7,23},{8,24},{9,... | collective-permute-start | bytes 1769480 | tf_op jit(solution)/shard_map/ppermute | solution.py:364
  204.5 15.8 %fusion.78.raw_ref.refs_1_ = f32[2048,1024]{1,0:T(8,128)} fusion(bf16[2048,2304]{1,0:T(8,128)(2,1)} %after.42, bf16[2304,1024]{1,0:T(8,128)(2,1)} %all-gather.5.cloned.1.call-done), kind=kOutput, calls=%fused_computation.315 | convolution fusion | flops 9663676416 | bytes 22544384 | tf_op jit(solution)/shard_map/dot_general | solution.py:98
  220.3 4.7 all-gather.7.cloned.1.call-done.refs_0_
  225.0 4.3 all-to-all-start.4
  229.4 33.4 %attend.1 = (bf16[2048,384]{1,0:T(8,128)(2,1)S(1)}, bf16[3,2048,384]{2,1,0:T(8,128)(2,1)S(1)}) custom-call(s32[33]{0:T(128)S(1)} %pad_add_fusion.index_ref, f32[2048,1024]{1,0:T(8,128)} %fusion.78.raw_ref.refs_1_, f32[1280,128]{1,0:T(8,128)S(1)} %get-tuple-element.137.cos_ref, f32[1280,128]{1,0:T(8,128)S(1)} %get-tuple-element.136.sin_ref), custom_call_target="tpu_custom_call" | custom-call | flops 35999997952 | bytes 1048576 | tf_op jit(solution)/shard_map/attend/pallas_call | solution.py:187
  299.3 18.1 %collective-permute-done.27.refs_0_ = bf16[256,2304]{1,0:T(8,128)(2,1)S(1)} collective-permute-done((bf16[256,2304]{1,0:T(8,128)(2,1)S(1)}, bf16[256,2304]{1,0:T(8,128)(2,1)S(1)}, u32[]{:S(2)}, u32[]{:S(2)}) %collective-permute-start.27) | collective-permute-done | bytes 1179680 | tf_op jit(solution)/shard_map/ppermute | solution.py:364
  318.6 25.4 %collective-permute-done.17.refs_0_ = bf16[256,2304]{1,0:T(8,128)(2,1)} collective-permute-done((bf16[256,2304]{1,0:T(8,128)(2,1)}, bf16[256,2304]{1,0:T(8,128)(2,1)}, u32[]{:S(2)}, u32[]{:S(2)}) %collective-permute-start.17) | collective-permute-done | bytes 1179680 | tf_op jit(solution)/shard_map/ppermute | solution.py:364
  344.0 4.2 multiply_reduce_fusion.1
  354.7 22.8 %collective-permute-done.28 = bf16[256,2304]{1,0:T(8,128)(2,1)} collective-permute-done((bf16[256,2304]{1,0:T(8,128)(2,1)}, bf16[256,2304]{1,0:T(8,128)(2,1)}, u32[]{:S(2)}, u32[]{:S(2)}) %collective-permute-start.28) | collective-permute-done | bytes 1179680 | tf_op jit(solution)/shard_map/ppermute | solution.py:364
  386.9 5.0 collective-permute-done.30
  392.3 3.2 collective-permute-start.35
  401.7 19.5 %fusion.79 = f32[2048,1536]{1,0:T(8,128)S(1)} fusion(bf16[2048,2304]{1,0:T(8,128)(2,1)} %constant_dynamic-update-slice_fusion.18, bf16[2304,1536]{1,0:T(8,128)(2,1)} %all-gather.9.cloned.1.call-done), kind=kOutput, calls=%fused_computation.316 | convolution fusion | flops 14495514624 | bytes 29097984 | tf_op jit(solution)/shard_map/dot_general | solution.py:98
  421.3 4.6 copy-done.19
  428.0 13.9 %convolution_convert_fusion.5 = bf16[768,2304]{1,0:T(8,128)(2,1)} fusion(bf16[2048,768]{1,0:T(8,128)(2,1)S(1)} %multiply_convert_fusion.2.refs_0_, bf16[2048,2304]{1,0:T(8,128)(2,1)} %constant_dynamic-update-slice_fusion.9.refs_1_.refs_0_), kind=kOutput, calls=%fused_computation.15 | convolution fusion | flops 7249526784 | bytes 16121856 | tf_op jit(solution)/shard_map/dot_general | solution.py:94
  442.0 16.4 %multiply_convert_fusion = (bf16[2048,768]{1,0:T(8,128)(2,1)S(1)}, bf16[2048,768]{1,0:T(8,128)(2,1)S(1)}) fusion(f32[2048,1536]{1,0:T(8,128)} %copy-done.19, bf16[2048,2304]{1,0:T(8,128)(2,1)} %after.50, bf16[768,2304]{1,0:T(8,128)(2,1)} %all-gather.11.cloned.1.call-done), kind=kOutput, calls=%fused_computation.6 | convolution fusion | flops 7268204544 | bytes 31850496 | tf_op jit(solution)/shard_map/dot_general | solution.py:90
  458.4 10.5 %fusion.7 = f32[1024,2304]{1,0:T(8,128)} fusion(bf16[2304,1536]{1,0:T(8,128)(2,1)} %all-gather.9.cloned.1.call-done, bf16[2048,768]{1,0:T(8,128)(2,1)S(1)} %get-tuple-element.34.refs_0_), kind=kOutput, calls=%fused_computation.25 | convolution fusion | flops 3623878656 | bytes 14548992 | tf_op jit(solution)/shard_map/dot_general | solution.py:90
  468.9 7.7 add_convert_fusion
  479.0 8.3 fusion.9
  487.3 7.7 convolution_add_fusion
  495.0 3.5 fusion.31
  503.0 19.3 %convolution_convert_fusion = bf16[2304,1536]{1,0:T(8,128)(2,1)S(1)} fusion(bf16[2048,2304]{1,0:T(8,128)(2,1)} %constant_dynamic-update-slice_fusion.18, bf16[2048,768]{1,0:T(8,128)(2,1)} %after.53, bf16[2048,768]{1,0:T(8,128)(2,1)} %after.52), kind=kOutput, calls=%fused_computation | convolution fusion | flops 14511636480 | bytes 22806528 | tf_op jit(solution)/shard_map/dot_general | solution.py:94
  522.4 3.5 copy.111
  528.6 25.8 %collective-permute-done.38.refs_0_ = bf16[256,2304]{1,0:T(8,128)(2,1)S(1)} collective-permute-done((bf16[256,2304]{1,0:T(8,128)(2,1)}, bf16[256,2304]{1,0:T(8,128)(2,1)S(1)}, u32[]{:S(2)}, u32[]{:S(2)}) %collective-permute-start.38) | collective-permute-done | bytes 1179680 | tf_op jit(solution)/shard_map/ppermute | solution.py:364
  555.5 4.9 multiply_reduce_fusion
  564.7 6.3 convolution_convert_fusion.1
  577.4 6.4 fusion.42
  583.8 6.4 collective-permute-done.45
  597.0 7.0 fusion.26
  614.4 4.0 fusion.80
  618.9 6.3 convolution_convert_fusion.6.refs_0_
  634.1 55.2 %attend_back.1.refs_0_ = bf16[2048,1024]{1,0:T(8,128)(2,1)} custom-call(s32[33]{0:T(128)S(1)} %pad_add_fusion.index_ref, bf16[3,2048,384]{2,1,0:T(8,128)(2,1)} %copy-done.5, bf16[2048,384]{1,0:T(8,128)(2,1)S(1)} %copy-done.2, f32[1280,128]{1,0:T(8,128)S(1)} %get-tuple-element.137.cos_ref, f32[1280,128]{1,0:T(8,128)S(1)} %get-tuple-element.136.sin_ref), custom_call_target="tpu_custom_call" | custom-call | bytes 1048576 | tf_op jit(solution)/shard_map/attend_back/pallas_call | solution.py:308
  693.6 4.6 all-to-all-start.5
  698.1 13.8 %convolution_convert_fusion.4 = bf16[2304,1024]{1,0:T(8,128)(2,1)S(1)} fusion(bf16[2048,2304]{1,0:T(8,128)(2,1)} %constant_dynamic-update-slice_fusion.refs_1_.refs_2_, bf16[2048,1024]{1,0:T(8,128)(2,1)} %after.62.refs_1_.refs_0_), kind=kOutput, calls=%fused_computation.14 | convolution fusion | flops 9666035712 | bytes 18350080 | tf_op jit(solution)/shard_map/dot_general | solution.py:94
  719.0 9.0 convolution_convert_fusion.3
  732.6 7.4 fusion.39
  751.3 20.4 %collective-permute-done.65 = bf16[256,2304]{1,0:T(8,128)(2,1)} collective-permute-done((bf16[256,2304]{1,0:T(8,128)(2,1)}, bf16[256,2304]{1,0:T(8,128)(2,1)}, u32[]{:S(2)}, u32[]{:S(2)}) %collective-permute-start.65) | collective-permute-done | bytes 1179680 | tf_op jit(solution)/shard_map/ppermute | solution.py:364
  771.7 26.1 %collective-permute-done.63 = bf16[256,2304]{1,0:T(8,128)(2,1)} collective-permute-done((bf16[256,2304]{1,0:T(8,128)(2,1)}, bf16[256,2304]{1,0:T(8,128)(2,1)}, u32[]{:S(2)}, u32[]{:S(2)}) %collective-permute-start.63) | collective-permute-done | bytes 1179680 | tf_op jit(solution)/shard_map/ppermute | solution.py:364
  797.8 5.2 fusion.20
  803.7 4.1 fusion.19.refs_0_
  807.8 4.9 add_convert_fusion.1
  816.3 6.0 collective-permute-start.66
  824.0 5.5 all-to-all-start.6
  836.0 4.7 collective-permute-start.69
  840.7 9.8 %all-to-all-done.6.refs_1_ = bf16[8,72,1024]{2,1,0:T(8,128)(2,1)S(1)} async-done(((bf16[8,72,1024]{2,1,0:T(8,128)(2,1)}), bf16[8,72,1024]{2,1,0:T(8,128)(2,1)S(1)}, u32[]{:S(2)}, u32[]{:S(2)}) %all-to-all-start.6) | async-done | bytes 1179680 | tf_op jit(solution)/shard_map/all_to_all | solution.py:639
  859.5 5.3 reshape.400
  868.2 3.2 reshape.408.refs_4_
  874.1 3.2 reshape.409.refs_5_
  877.3 13.3 %collective-permute-start.71 = (bf16[180,2304]{1,0:T(8,128)(2,1)}, bf16[180,2304]{1,0:T(8,128)(2,1)}, u32[]{:S(2)}, u32[]{:S(2)}) collective-permute-start(bf16[180,2304]{1,0:T(8,128)(2,1)} %after.75), channel_id=1, source_target_pairs={{0,0},{1,4},{2,8},{3,12},{4,16},{5,20},{6,24},{7,28},{8,1},{9,5},{... | collective-permute-start | bytes 2488328 | tf_op jit(solution)/shard_map/ppermute | solution.py:364
  905.1 16.5 %collective-permute-done.70 = bf16[72,2304]{1,0:T(8,128)(2,1)S(1)} collective-permute-done((bf16[72,2304]{1,0:T(8,128)(2,1)}, bf16[72,2304]{1,0:T(8,128)(2,1)S(1)}, u32[]{:S(2)}, u32[]{:S(2)}) %collective-permute-start.70) | collective-permute-done | bytes 331808 | tf_op jit(solution)/shard_map/ppermute | solution.py:364
  (490 shorter events, 269.6 us)
Async XLA Ops:
  9.7 19.7 %all-to-all-start = ((bf16[4,64,2304]{2,1,0:T(8,128)(2,1)}), bf16[4,64,2304]{2,1,0:T(8,128)(2,1)}, u32[]{:S(2)}, u32[]{:S(2)}) async-start(bf16[4,64,2304]{2,1,0:T(8,128)(2,1)} %bitcast.199), calls=%async_computation | async-start | bytes 2359296 | tf_op jit(solution)/shard_map/all_to_all | solution.py:396
  31.9 36.9 %all-to-all-start.1 = ((bf16[4,72,2304]{2,1,0:T(8,128)(2,1)}), bf16[4,72,2304]{2,1,0:T(8,128)(2,1)}, u32[]{:S(2)}, u32[]{:S(2)}) async-start(bf16[4,72,2304]{2,1,0:T(8,128)(2,1)} %pad_maximum_fusion.1), calls=%async_computation.1 | async-start | bytes 2654208 | tf_op jit(solution)/shard_map/all_to_all | solution.py:464
  49.7 16.6 %collective-permute-start.13 = (bf16[288,1024]{1,0:T(8,128)(2,1)}, bf16[288,1024]{1,0:T(8,128)(2,1)}, u32[]{:S(2)}, u32[]{:S(2)}) collective-permute-start(bf16[288,1024]{1,0:T(8,128)(2,1)} %broadcast_select_fusion.6), channel_id=1, source_target_pairs={{0,1},{1,0},{2,3},{3,2},{4,5},{5,4},{6,7},{7,6},{8,9},{9,8},{10,11... | collective-permute-start | bytes 1769480 | tf_op jit(solution)/shard_map/ppermute | solution.py:364
  68.7 19.0 %all-to-all-start.2 = ((bf16[4,64,2304]{2,1,0:T(8,128)(2,1)}), bf16[4,64,2304]{2,1,0:T(8,128)(2,1)}, u32[]{:S(2)}, u32[]{:S(2)}) async-start(bf16[4,64,2304]{2,1,0:T(8,128)(2,1)} %bitcast.185), calls=%async_computation.2 | async-start | bytes 2359296 | tf_op jit(solution)/shard_map/all_to_all | solution.py:396
  73.0 131.5 %all-gather.5.cloned.1.call-start = ((), (), s32[]{:S(2)}) async-start(), calls=%async_computation.11 | async-start | bytes 5898240 | tf_op jit(solution)/shard_map/all_gather | solution.py:510
  93.3 26.5 %collective-permute-start.3 = (bf16[256,2304]{1,0:T(8,128)(2,1)}, bf16[256,2304]{1,0:T(8,128)(2,1)}, u32[]{:S(2)}, u32[]{:S(2)}) collective-permute-start(bf16[256,2304]{1,0:T(8,128)(2,1)} %get-tuple-element.32), channel_id=1, source_target_pairs={{0,8},{1,9},{2,10},{3,11},{4,12},{5,13},{6,14},{7,15},{8,0},{9,1},... | collective-permute-start | bytes 3538952 | tf_op jit(solution)/shard_map/ppermute | solution.py:364
  94.5 27.7 %collective-permute-start.4 = (bf16[256,2304]{1,0:T(8,128)(2,1)}, bf16[256,2304]{1,0:T(8,128)(2,1)S(1)}, u32[]{:S(2)}, u32[]{:S(2)}) collective-permute-start(bf16[256,2304]{1,0:T(8,128)(2,1)} %get-tuple-element.32), channel_id=1, source_target_pairs={{0,16},{1,17},{2,18},{3,19},{4,20},{5,21},{6,22},{7,23},{8,24},{9,... | collective-permute-start | bytes 3538952 | tf_op jit(solution)/shard_map/ppermute | solution.py:364
  94.8 52.2 %collective-permute-start.1 = (s32[1,16]{1,0:T(1,128)S(1)}, s32[1,16]{1,0:T(1,128)S(1)}, u32[]{:S(2)}, u32[]{:S(2)}) collective-permute-start(s32[1,16]{1,0:T(1,128)S(1)} %copy-done.63), channel_id=1, source_target_pairs={{0,0},{1,1},{2,8},{3,9},{4,16},{5,17},{6,24},{7,25},{8,2},{9,3},{1... | collective-permute-start | bytes 200 | tf_op jit(solution)/shard_map/ppermute | solution.py:364
  97.2 63.9 %all-to-all-start.3 = ((bf16[4,64,2304]{2,1,0:T(8,128)(2,1)}), bf16[4,64,2304]{2,1,0:T(8,128)(2,1)S(1)}, u32[]{:S(2)}, u32[]{:S(2)}) async-start(bf16[4,64,2304]{2,1,0:T(8,128)(2,1)} %after.40), calls=%async_computation.3 | async-start | bytes 2359296 | tf_op jit(solution)/shard_map/all_to_all | solution.py:399
  103.9 121.1 %all-gather.7.cloned.1.call-start = ((), (), s32[]{:S(2)}) async-start(), calls=%async_computation.12 | async-start | bytes 1658880 | tf_op jit(solution)/shard_map/all_gather | solution.py:510
  103.9 36.0 %collective-permute-start.7 = (bf16[256,2304]{1,0:T(8,128)(2,1)}, bf16[256,2304]{1,0:T(8,128)(2,1)S(1)}, u32[]{:S(2)}, u32[]{:S(2)}) collective-permute-start(bf16[256,2304]{1,0:T(8,128)(2,1)} %get-tuple-element.32), channel_id=1, source_target_pairs={{0,1},{1,0},{2,3},{3,2},{4,5},{5,4},{6,7},{7,6},{8,9},{9,8},{10,11... | collective-permute-start | bytes 3538952 | tf_op jit(solution)/shard_map/ppermute | solution.py:364
  122.6 18.5 %collective-permute-start.8 = (bf16[256,2304]{1,0:T(8,128)(2,1)}, bf16[256,2304]{1,0:T(8,128)(2,1)S(1)}, u32[]{:S(2)}, u32[]{:S(2)}) collective-permute-start(bf16[256,2304]{1,0:T(8,128)(2,1)} %collective-permute-done.3), channel_id=1, source_target_pairs={{0,1},{1,0},{2,3},{3,2},{4,5},{5,4},{6,7},{7,6},{8,9},{9,8},{10,11... | collective-permute-start | bytes 3538952 | tf_op jit(solution)/shard_map/ppermute | solution.py:364
  162.5 22.3 %collective-permute-start.11 = (bf16[256,2304]{1,0:T(8,128)(2,1)}, bf16[256,2304]{1,0:T(8,128)(2,1)}, u32[]{:S(2)}, u32[]{:S(2)}) collective-permute-start(bf16[256,2304]{1,0:T(8,128)(2,1)} %after.41), channel_id=1, source_target_pairs={{0,8},{1,9},{2,10},{3,11},{4,12},{5,13},{6,14},{7,15},{8,0},{9,1},... | collective-permute-start | bytes 3538952 | tf_op jit(solution)/shard_map/ppermute | solution.py:364
  163.6 33.6 %collective-permute-start.12 = (bf16[256,2304]{1,0:T(8,128)(2,1)}, bf16[256,2304]{1,0:T(8,128)(2,1)S(1)}, u32[]{:S(2)}, u32[]{:S(2)}) collective-permute-start(bf16[256,2304]{1,0:T(8,128)(2,1)} %after.41), channel_id=1, source_target_pairs={{0,16},{1,17},{2,18},{3,19},{4,20},{5,21},{6,22},{7,23},{8,24},{9,... | collective-permute-start | bytes 3538952 | tf_op jit(solution)/shard_map/ppermute | solution.py:364
  178.4 111.0 %collective-permute-start.20 = (bf16[256,2304]{1,0:T(8,128)(2,1)}, bf16[256,2304]{1,0:T(8,128)(2,1)}, u32[]{:S(2)}, u32[]{:S(2)}) collective-permute-start(bf16[256,2304]{1,0:T(8,128)(2,1)} %after.41), channel_id=1, source_target_pairs={{0,1},{1,0},{2,3},{3,2},{4,5},{5,4},{6,7},{7,6},{8,9},{9,8},{10,11... | collective-permute-start | bytes 3538952 | tf_op jit(solution)/shard_map/ppermute | solution.py:364
  180.1 221.6 %all-gather.9.cloned.1.call-start = ((), (), s32[]{:S(2)}) async-start(), calls=%async_computation.13 | async-start | bytes 8847360 | tf_op jit(solution)/shard_map/all_gather | solution.py:510
  186.8 89.3 %collective-permute-start.18 = (bf16[128,2304]{1,0:T(8,128)(2,1)}, bf16[128,2304]{1,0:T(8,128)(2,1)}, u32[]{:S(2)}, u32[]{:S(2)}) collective-permute-start(bf16[128,2304]{1,0:T(8,128)(2,1)} %slice.502), channel_id=1, source_target_pairs={{0,16},{1,17},{2,18},{3,19},{4,20},{5,21},{6,22},{7,23},{8,24},{9,... | collective-permute-start | bytes 1769480 | tf_op jit(solution)/shard_map/ppermute | solution.py:364
  198.1 80.3 %collective-permute-start.19 = (bf16[128,2304]{1,0:T(8,128)(2,1)}, bf16[128,2304]{1,0:T(8,128)(2,1)}, u32[]{:S(2)}, u32[]{:S(2)}) collective-permute-start(bf16[128,2304]{1,0:T(8,128)(2,1)} %slice.503), channel_id=1, source_target_pairs={{0,8},{1,9},{2,10},{3,11},{4,12},{5,13},{6,14},{7,15},{8,0},{9,1},... | collective-permute-start | bytes 1769480 | tf_op jit(solution)/shard_map/ppermute | solution.py:364
  199.5 91.6 %collective-permute-start.21 = (bf16[256,2304]{1,0:T(8,128)(2,1)}, bf16[256,2304]{1,0:T(8,128)(2,1)}, u32[]{:S(2)}, u32[]{:S(2)}) collective-permute-start(bf16[256,2304]{1,0:T(8,128)(2,1)} %collective-permute-done.11.refs_1_), channel_id=1, source_target_pairs={{0,1},{1,0},{2,3},{3,2},{4,5},{5,4},{6,7},{7,6},{8,9},{9,8},{10,11... | collective-permute-start | bytes 3538952 | tf_op jit(solution)/shard_map/ppermute | solution.py:364
  225.0 39.9 %all-to-all-start.4 = ((bf16[4,72,2304]{2,1,0:T(8,128)(2,1)}), bf16[4,72,2304]{2,1,0:T(8,128)(2,1)}, u32[]{:S(2)}, u32[]{:S(2)}) async-start(bf16[4,72,2304]{2,1,0:T(8,128)(2,1)} %bitcast.191), calls=%async_computation.4 | async-start | bytes 2654208 | tf_op jit(solution)/shard_map/all_to_all | solution.py:550
  229.3 212.6 %all-gather.11.cloned.1.call-start = ((), (), s32[]{:S(2)}) async-start(), calls=%async_computation.14 | async-start | bytes 4423680 | tf_op jit(solution)/shard_map/all_gather | solution.py:510
  285.2 58.8 %collective-permute-start.15 = (bf16[256,2304]{1,0:T(8,128)(2,1)}, bf16[256,2304]{1,0:T(8,128)(2,1)}, u32[]{:S(2)}, u32[]{:S(2)}) collective-permute-start(bf16[256,2304]{1,0:T(8,128)(2,1)} %get-tuple-element.61), channel_id=1, source_target_pairs={{0,1},{1,0},{2,3},{3,2},{4,5},{5,4},{6,7},{7,6},{8,9},{9,8},{10,11... | collective-permute-start | bytes 3538952 | tf_op jit(solution)/shard_map/ppermute | solution.py:364
  289.4 28.0 %collective-permute-start.27 = (bf16[256,2304]{1,0:T(8,128)(2,1)S(1)}, bf16[256,2304]{1,0:T(8,128)(2,1)S(1)}, u32[]{:S(2)}, u32[]{:S(2)}) collective-permute-start(bf16[256,2304]{1,0:T(8,128)(2,1)S(1)} %get-tuple-element.47), channel_id=1, source_target_pairs={{0,16},{1,17},{2,18},{3,19},{4,20},{5,21},{6,22},{7,23},{8,24},{9,... | collective-permute-start | bytes 3538952 | tf_op jit(solution)/shard_map/ppermute | solution.py:364
  291.1 27.6 %collective-permute-start.25 = (bf16[256,2304]{1,0:T(8,128)(2,1)}, bf16[256,2304]{1,0:T(8,128)(2,1)}, u32[]{:S(2)}, u32[]{:S(2)}) collective-permute-start(bf16[256,2304]{1,0:T(8,128)(2,1)} %get-tuple-element.48), channel_id=1, source_target_pairs={{0,8},{1,9},{2,10},{3,11},{4,12},{5,13},{6,14},{7,15},{8,0},{9,1},... | collective-permute-start | bytes 3538952 | tf_op jit(solution)/shard_map/ppermute | solution.py:364
  292.3 51.7 %collective-permute-start.17 = (bf16[256,2304]{1,0:T(8,128)(2,1)}, bf16[256,2304]{1,0:T(8,128)(2,1)}, u32[]{:S(2)}, u32[]{:S(2)}) collective-permute-start(bf16[256,2304]{1,0:T(8,128)(2,1)} %get-tuple-element.46), channel_id=1, source_target_pairs={{0,24},{1,25},{2,26},{3,27},{4,28},{5,29},{6,30},{7,31},{8,16},{9,... | collective-permute-start | bytes 3538952 | tf_op jit(solution)/shard_map/ppermute | solution.py:364
  350.6 27.0 %collective-permute-start.28 = (bf16[256,2304]{1,0:T(8,128)(2,1)}, bf16[256,2304]{1,0:T(8,128)(2,1)}, u32[]{:S(2)}, u32[]{:S(2)}) collective-permute-start(bf16[256,2304]{1,0:T(8,128)(2,1)} %get-tuple-element.28), channel_id=1, source_target_pairs={{0,8},{1,9},{2,10},{3,11},{4,12},{5,13},{6,14},{7,15},{8,0},{9,1},... | collective-permute-start | bytes 3538952 | tf_op jit(solution)/shard_map/ppermute | solution.py:364
  351.7 27.8 %collective-permute-start.29 = (bf16[256,2304]{1,0:T(8,128)(2,1)}, bf16[256,2304]{1,0:T(8,128)(2,1)S(1)}, u32[]{:S(2)}, u32[]{:S(2)}) collective-permute-start(bf16[256,2304]{1,0:T(8,128)(2,1)} %get-tuple-element.28), channel_id=1, source_target_pairs={{0,16},{1,17},{2,18},{3,19},{4,20},{5,21},{6,22},{7,23},{8,24},{9,... | collective-permute-start | bytes 3538952 | tf_op jit(solution)/shard_map/ppermute | solution.py:364
  352.9 277.7 %reduce-scatter.5.cloned.1.call-start = ((), (), s32[]{:S(2)}) async-start(), calls=%async_computation.15 | async-start | bytes 4423680 | tf_op jit(solution)/shard_map/reduce_scatter | solution.py:666
  352.9 44.2 %collective-permute-start.32 = (bf16[256,2304]{1,0:T(8,128)(2,1)}, bf16[256,2304]{1,0:T(8,128)(2,1)S(1)}, u32[]{:S(2)}, u32[]{:S(2)}) collective-permute-start(bf16[256,2304]{1,0:T(8,128)(2,1)} %get-tuple-element.28), channel_id=1, source_target_pairs={{0,1},{1,0},{2,3},{3,2},{4,5},{5,4},{6,7},{7,6},{8,9},{9,8},{10,11... | collective-permute-start | bytes 3538952 | tf_op jit(solution)/shard_map/ppermute | solution.py:364
  380.8 17.6 %collective-permute-start.33 = (bf16[256,2304]{1,0:T(8,128)(2,1)}, bf16[256,2304]{1,0:T(8,128)(2,1)S(1)}, u32[]{:S(2)}, u32[]{:S(2)}) collective-permute-start(bf16[256,2304]{1,0:T(8,128)(2,1)} %collective-permute-done.28), channel_id=1, source_target_pairs={{0,1},{1,0},{2,3},{3,2},{4,5},{5,4},{6,7},{7,6},{8,9},{9,8},{10,11... | collective-permute-start | bytes 3538952 | tf_op jit(solution)/shard_map/ppermute | solution.py:364
  383.4 16.1 %collective-permute-start.34 = (bf16[256,2304]{1,0:T(8,128)(2,1)S(1)}, bf16[256,2304]{1,0:T(8,128)(2,1)S(1)}, u32[]{:S(2)}, u32[]{:S(2)}) collective-permute-start(bf16[256,2304]{1,0:T(8,128)(2,1)S(1)} %collective-permute-done.29), channel_id=1, source_target_pairs={{0,1},{1,0},{2,3},{3,2},{4,5},{5,4},{6,7},{7,6},{8,9},{9,8},{10,11... | collective-permute-start | bytes 3538952 | tf_op jit(solution)/shard_map/ppermute | solution.py:364
  441.9 247.5 %reduce-scatter.7.cloned.1.call-start = ((), (), s32[]{:S(2)}) async-start(), calls=%async_computation.16 | async-start | bytes 8847360 | tf_op jit(solution)/shard_map/reduce_scatter | solution.py:628
  477.9 17.0 %collective-permute-start.37 = (bf16[256,2304]{1,0:T(8,128)(2,1)S(1)}, bf16[256,2304]{1,0:T(8,128)(2,1)S(1)}, u32[]{:S(2)}, u32[]{:S(2)}) collective-permute-start(bf16[256,2304]{1,0:T(8,128)(2,1)S(1)} %get-tuple-element.60), channel_id=1, source_target_pairs={{0,1},{1,0},{2,3},{3,2},{4,5},{5,4},{6,7},{7,6},{8,9},{9,8},{10,11... | collective-permute-start | bytes 3538952 | tf_op jit(solution)/shard_map/ppermute | solution.py:364
  478.0 17.0 %collective-permute-start.41 = (bf16[256,2304]{1,0:T(8,128)(2,1)S(1)}, bf16[256,2304]{1,0:T(8,128)(2,1)S(1)}, u32[]{:S(2)}, u32[]{:S(2)}) collective-permute-start(bf16[256,2304]{1,0:T(8,128)(2,1)S(1)} %get-tuple-element.58), channel_id=1, source_target_pairs={{0,1},{1,0},{2,3},{3,2},{4,5},{5,4},{6,7},{7,6},{8,9},{9,8},{10,11... | collective-permute-start | bytes 3538952 | tf_op jit(solution)/shard_map/ppermute | solution.py:364
  478.4 16.5 %collective-permute-start.39 = (bf16[256,2304]{1,0:T(8,128)(2,1)S(1)}, bf16[256,2304]{1,0:T(8,128)(2,1)S(1)}, u32[]{:S(2)}, u32[]{:S(2)}) collective-permute-start(bf16[256,2304]{1,0:T(8,128)(2,1)S(1)} %get-tuple-element.59), channel_id=1, source_target_pairs={{0,1},{1,0},{2,3},{3,2},{4,5},{5,4},{6,7},{7,6},{8,9},{9,8},{10,11... | collective-permute-start | bytes 3538952 | tf_op jit(solution)/shard_map/ppermute | solution.py:364
  478.5 77.0 %collective-permute-start.36 = (bf16[256,2304]{1,0:T(8,128)(2,1)}, bf16[256,2304]{1,0:T(8,128)(2,1)}, u32[]{:S(2)}, u32[]{:S(2)}) collective-permute-start(bf16[256,2304]{1,0:T(8,128)(2,1)} %get-tuple-element.57), channel_id=1, source_target_pairs={{0,1},{1,0},{2,3},{3,2},{4,5},{5,4},{6,7},{7,6},{8,9},{9,8},{10,11... | collective-permute-start | bytes 3538952 | tf_op jit(solution)/shard_map/ppermute | solution.py:364
  500.4 27.9 %collective-permute-start.42 = (bf16[256,2304]{1,0:T(8,128)(2,1)}, bf16[256,2304]{1,0:T(8,128)(2,1)}, u32[]{:S(2)}, u32[]{:S(2)}) collective-permute-start(bf16[256,2304]{1,0:T(8,128)(2,1)} %get-tuple-element.43), channel_id=1, source_target_pairs={{0,16},{1,17},{2,18},{3,19},{4,20},{5,21},{6,22},{7,23},{8,24},{9,... | collective-permute-start | bytes 3538952 | tf_op jit(solution)/shard_map/ppermute | solution.py:364
  501.0 27.6 %collective-permute-start.40 = (bf16[256,2304]{1,0:T(8,128)(2,1)}, bf16[256,2304]{1,0:T(8,128)(2,1)}, u32[]{:S(2)}, u32[]{:S(2)}) collective-permute-start(bf16[256,2304]{1,0:T(8,128)(2,1)} %get-tuple-element.44), channel_id=1, source_target_pairs={{0,8},{1,9},{2,10},{3,11},{4,12},{5,13},{6,14},{7,15},{8,0},{9,1},... | collective-permute-start | bytes 3538952 | tf_op jit(solution)/shard_map/ppermute | solution.py:364
  501.8 52.6 %collective-permute-start.38 = (bf16[256,2304]{1,0:T(8,128)(2,1)}, bf16[256,2304]{1,0:T(8,128)(2,1)S(1)}, u32[]{:S(2)}, u32[]{:S(2)}) collective-permute-start(bf16[256,2304]{1,0:T(8,128)(2,1)} %get-tuple-element.42), channel_id=1, source_target_pairs={{0,24},{1,25},{2,26},{3,27},{4,28},{5,29},{6,30},{7,31},{8,16},{9,... | collective-permute-start | bytes 3538952 | tf_op jit(solution)/shard_map/ppermute | solution.py:364
  525.9 188.9 %reduce-scatter.9.cloned.1.call-start = ((), (), s32[]{:S(2)}) async-start(), calls=%async_computation.17 | async-start | bytes 1658880 | tf_op jit(solution)/shard_map/reduce_scatter | solution.py:685
  563.4 26.8 %collective-permute-start.45 = (bf16[256,2304]{1,0:T(8,128)(2,1)}, bf16[256,2304]{1,0:T(8,128)(2,1)S(1)}, u32[]{:S(2)}, u32[]{:S(2)}) collective-permute-start(bf16[256,2304]{1,0:T(8,128)(2,1)} %get-tuple-element.24.refs_1_), channel_id=1, source_target_pairs={{0,8},{1,9},{2,10},{3,11},{4,12},{5,13},{6,14},{7,15},{8,0},{9,1},... | collective-permute-start | bytes 3538952 | tf_op jit(solution)/shard_map/ppermute | solution.py:364
  564.6 28.3 %collective-permute-start.46 = (bf16[256,2304]{1,0:T(8,128)(2,1)}, bf16[256,2304]{1,0:T(8,128)(2,1)}, u32[]{:S(2)}, u32[]{:S(2)}) collective-permute-start(bf16[256,2304]{1,0:T(8,128)(2,1)} %get-tuple-element.24.refs_1_), channel_id=1, source_target_pairs={{0,16},{1,17},{2,18},{3,19},{4,20},{5,21},{6,22},{7,23},{8,24},{9,... | collective-permute-start | bytes 3538952 | tf_op jit(solution)/shard_map/ppermute | solution.py:364
  572.3 23.2 %collective-permute-start.57 = (bf16[256,2304]{1,0:T(8,128)(2,1)S(1)}, bf16[256,2304]{1,0:T(8,128)(2,1)S(1)}, u32[]{:S(2)}, u32[]{:S(2)}) collective-permute-start(bf16[256,2304]{1,0:T(8,128)(2,1)S(1)} %get-tuple-element.50), channel_id=1, source_target_pairs={{0,1},{1,0},{2,3},{3,2},{4,5},{5,4},{6,7},{7,6},{8,9},{9,8},{10,11... | collective-permute-start | bytes 3538952 | tf_op jit(solution)/shard_map/ppermute | solution.py:364
  574.0 22.3 %collective-permute-start.55 = (bf16[256,2304]{1,0:T(8,128)(2,1)S(1)}, bf16[256,2304]{1,0:T(8,128)(2,1)S(1)}, u32[]{:S(2)}, u32[]{:S(2)}) collective-permute-start(bf16[256,2304]{1,0:T(8,128)(2,1)S(1)} %get-tuple-element.51), channel_id=1, source_target_pairs={{0,1},{1,0},{2,3},{3,2},{4,5},{5,4},{6,7},{7,6},{8,9},{9,8},{10,11... | collective-permute-start | bytes 3538952 | tf_op jit(solution)/shard_map/ppermute | solution.py:364
  574.0 22.9 %collective-permute-start.44 = (bf16[256,2304]{1,0:T(8,128)(2,1)S(1)}, bf16[256,2304]{1,0:T(8,128)(2,1)S(1)}, u32[]{:S(2)}, u32[]{:S(2)}) collective-permute-start(bf16[256,2304]{1,0:T(8,128)(2,1)S(1)} %get-tuple-element.52), channel_id=1, source_target_pairs={{0,1},{1,0},{2,3},{3,2},{4,5},{5,4},{6,7},{7,6},{8,9},{9,8},{10,11... | collective-permute-start | bytes 3538952 | tf_op jit(solution)/shard_map/ppermute | solution.py:364
  590.2 21.7 %collective-permute-start.49 = (bf16[256,2304]{1,0:T(8,128)(2,1)}, bf16[256,2304]{1,0:T(8,128)(2,1)S(1)}, u32[]{:S(2)}, u32[]{:S(2)}) collective-permute-start(bf16[256,2304]{1,0:T(8,128)(2,1)} %get-tuple-element.24.refs_1_), channel_id=1, source_target_pairs={{0,1},{1,0},{2,3},{3,2},{4,5},{5,4},{6,7},{7,6},{8,9},{9,8},{10,11... | collective-permute-start | bytes 3538952 | tf_op jit(solution)/shard_map/ppermute | solution.py:364
  596.3 15.6 %collective-permute-start.50 = (bf16[256,2304]{1,0:T(8,128)(2,1)S(1)}, bf16[256,2304]{1,0:T(8,128)(2,1)S(1)}, u32[]{:S(2)}, u32[]{:S(2)}) collective-permute-start(bf16[256,2304]{1,0:T(8,128)(2,1)S(1)} %collective-permute-done.45), channel_id=1, source_target_pairs={{0,1},{1,0},{2,3},{3,2},{4,5},{5,4},{6,7},{7,6},{8,9},{9,8},{10,11... | collective-permute-start | bytes 3538952 | tf_op jit(solution)/shard_map/ppermute | solution.py:364
  625.4 63.9 %collective-permute-start.53 = (bf16[256,2304]{1,0:T(8,128)(2,1)}, bf16[256,2304]{1,0:T(8,128)(2,1)}, u32[]{:S(2)}, u32[]{:S(2)}) collective-permute-start(bf16[256,2304]{1,0:T(8,128)(2,1)} %after.58), channel_id=1, source_target_pairs={{0,24},{1,25},{2,26},{3,27},{4,28},{5,29},{6,30},{7,31},{8,16},{9,... | collective-permute-start | bytes 3538952 | tf_op jit(solution)/shard_map/ppermute | solution.py:364
  627.1 62.2 %collective-permute-start.56 = (bf16[256,2304]{1,0:T(8,128)(2,1)}, bf16[256,2304]{1,0:T(8,128)(2,1)}, u32[]{:S(2)}, u32[]{:S(2)}) collective-permute-start(bf16[256,2304]{1,0:T(8,128)(2,1)} %after.60), channel_id=1, source_target_pairs={{0,8},{1,9},{2,10},{3,11},{4,12},{5,13},{6,14},{7,15},{8,0},{9,1},... | collective-permute-start | bytes 3538952 | tf_op jit(solution)/shard_map/ppermute | solution.py:364
  627.4 61.9 %collective-permute-start.58 = (bf16[256,2304]{1,0:T(8,128)(2,1)}, bf16[256,2304]{1,0:T(8,128)(2,1)}, u32[]{:S(2)}, u32[]{:S(2)}) collective-permute-start(bf16[256,2304]{1,0:T(8,128)(2,1)} %after.61), channel_id=1, source_target_pairs={{0,16},{1,17},{2,18},{3,19},{4,20},{5,21},{6,22},{7,23},{8,24},{9,... | collective-permute-start | bytes 3538952 | tf_op jit(solution)/shard_map/ppermute | solution.py:364
  693.6 24.2 %all-to-all-start.5 = ((bf16[8,72,1536]{2,1,0:T(8,128)(2,1)}), bf16[8,72,1536]{2,1,0:T(8,128)(2,1)S(1)}, u32[]{:S(2)}, u32[]{:S(2)}) async-start(bf16[8,72,1536]{2,1,0:T(8,128)(2,1)} %select_select_fusion), calls=%async_computation.8 | async-start | bytes 3538944 | tf_op jit(solution)/shard_map/all_to_all | solution.py:639
  698.1 114.6 %reduce-scatter.11.cloned.1.call-start = ((), (), s32[]{:S(2)}) async-start(), calls=%async_computation.18 | async-start | bytes 5898240 | tf_op jit(solution)/shard_map/reduce_scatter | solution.py:628
  732.6 18.7 %collective-permute-start.61 = (bf16[256,2304]{1,0:T(8,128)(2,1)}, bf16[256,2304]{1,0:T(8,128)(2,1)}, u32[]{:S(2)}, u32[]{:S(2)}) collective-permute-start(bf16[256,2304]{1,0:T(8,128)(2,1)} %get-tuple-element.53), channel_id=1, source_target_pairs={{0,1},{1,0},{2,3},{3,2},{4,5},{5,4},{6,7},{7,6},{8,9},{9,8},{10,11... | collective-permute-start | bytes 3538952 | tf_op jit(solution)/shard_map/ppermute | solution.py:364
  744.6 27.0 %collective-permute-start.65 = (bf16[256,2304]{1,0:T(8,128)(2,1)}, bf16[256,2304]{1,0:T(8,128)(2,1)}, u32[]{:S(2)}, u32[]{:S(2)}) collective-permute-start(bf16[256,2304]{1,0:T(8,128)(2,1)} %get-tuple-element.36), channel_id=1, source_target_pairs={{0,16},{1,17},{2,18},{3,19},{4,20},{5,21},{6,22},{7,23},{8,24},{9,... | collective-permute-start | bytes 3538952 | tf_op jit(solution)/shard_map/ppermute | solution.py:364
  744.9 26.8 %collective-permute-start.60 = (bf16[256,2304]{1,0:T(8,128)(2,1)}, bf16[256,2304]{1,0:T(8,128)(2,1)S(1)}, u32[]{:S(2)}, u32[]{:S(2)}) collective-permute-start(bf16[256,2304]{1,0:T(8,128)(2,1)} %get-tuple-element.37), channel_id=1, source_target_pairs={{0,8},{1,9},{2,10},{3,11},{4,12},{5,13},{6,14},{7,15},{8,0},{9,1},... | collective-permute-start | bytes 3538952 | tf_op jit(solution)/shard_map/ppermute | solution.py:364
  745.7 52.1 %collective-permute-start.63 = (bf16[256,2304]{1,0:T(8,128)(2,1)}, bf16[256,2304]{1,0:T(8,128)(2,1)}, u32[]{:S(2)}, u32[]{:S(2)}) collective-permute-start(bf16[256,2304]{1,0:T(8,128)(2,1)} %get-tuple-element.35), channel_id=1, source_target_pairs={{0,24},{1,25},{2,26},{3,27},{4,28},{5,29},{6,30},{7,31},{8,16},{9,... | collective-permute-start | bytes 3538952 | tf_op jit(solution)/shard_map/ppermute | solution.py:364
  749.7 58.1 %collective-permute-start.43 = (bf16[256,2304]{1,0:T(8,128)(2,1)}, bf16[256,2304]{1,0:T(8,128)(2,1)}, u32[]{:S(2)}, u32[]{:S(2)}) collective-permute-start(bf16[256,2304]{1,0:T(8,128)(2,1)} %get-tuple-element.49), channel_id=1, source_target_pairs={{0,1},{1,0},{2,3},{3,2},{4,5},{5,4},{6,7},{7,6},{8,9},{9,8},{10,11... | collective-permute-start | bytes 3538952 | tf_op jit(solution)/shard_map/ppermute | solution.py:364
  816.3 74.3 %collective-permute-start.66 = (bf16[1,128,2304]{2,1,0:T(8,128)(2,1)}, bf16[1,128,2304]{2,1,0:T(8,128)(2,1)}, u32[]{:S(2)}, u32[]{:S(2)}) collective-permute-start(bf16[1,128,2304]{2,1,0:T(8,128)(2,1)} %pad_maximum_fusion.7), channel_id=1, source_target_pairs={{0,0},{1,1},{2,10},{3,11},{4,20},{5,21},{6,30},{7,31},{8,2},{9,3},... | collective-permute-start | bytes 1769480 | tf_op jit(solution)/shard_map/ppermute | solution.py:364
  824.0 26.5 %all-to-all-start.6 = ((bf16[8,72,1024]{2,1,0:T(8,128)(2,1)}), bf16[8,72,1024]{2,1,0:T(8,128)(2,1)S(1)}, u32[]{:S(2)}, u32[]{:S(2)}) async-start(bf16[8,72,1024]{2,1,0:T(8,128)(2,1)} %select_select_fusion.1), calls=%async_computation.10 | async-start | bytes 2359296 | tf_op jit(solution)/shard_map/all_to_all | solution.py:639
  830.4 62.4 %collective-permute-start.67 = (bf16[1,128,2304]{2,1,0:T(8,128)(2,1)}, bf16[1,128,2304]{2,1,0:T(8,128)(2,1)}, u32[]{:S(2)}, u32[]{:S(2)}) collective-permute-start(bf16[1,128,2304]{2,1,0:T(8,128)(2,1)} %pad_maximum_fusion.8), channel_id=1, source_target_pairs={{0,2},{1,3},{2,8},{3,9},{4,22},{5,23},{6,28},{7,29},{8,0},{9,1},{1... | collective-permute-start | bytes 1769480 | tf_op jit(solution)/shard_map/ppermute | solution.py:364
  833.2 60.7 %collective-permute-start.68 = (bf16[1,128,2304]{2,1,0:T(8,128)(2,1)}, bf16[1,128,2304]{2,1,0:T(8,128)(2,1)}, u32[]{:S(2)}, u32[]{:S(2)}) collective-permute-start(bf16[1,128,2304]{2,1,0:T(8,128)(2,1)} %pad_maximum_fusion.9), channel_id=1, source_target_pairs={{0,4},{1,5},{2,14},{3,15},{4,16},{5,17},{6,26},{7,27},{8,6},{9,7},... | collective-permute-start | bytes 1769480 | tf_op jit(solution)/shard_map/ppermute | solution.py:364
  836.0 59.1 %collective-permute-start.69 = (bf16[1,128,2304]{2,1,0:T(8,128)(2,1)}, bf16[1,128,2304]{2,1,0:T(8,128)(2,1)S(1)}, u32[]{:S(2)}, u32[]{:S(2)}) collective-permute-start(bf16[1,128,2304]{2,1,0:T(8,128)(2,1)} %pad_maximum_fusion.10), channel_id=1, source_target_pairs={{0,6},{1,7},{2,12},{3,13},{4,18},{5,19},{6,24},{7,25},{8,4},{9,5},... | collective-permute-start | bytes 1769480 | tf_op jit(solution)/shard_map/ppermute | solution.py:364
  877.3 45.2 %collective-permute-start.71 = (bf16[180,2304]{1,0:T(8,128)(2,1)}, bf16[180,2304]{1,0:T(8,128)(2,1)}, u32[]{:S(2)}, u32[]{:S(2)}) collective-permute-start(bf16[180,2304]{1,0:T(8,128)(2,1)} %after.75), channel_id=1, source_target_pairs={{0,0},{1,4},{2,8},{3,12},{4,16},{5,20},{6,24},{7,28},{8,1},{9,5},{... | collective-permute-start | bytes 2488328 | tf_op jit(solution)/shard_map/ppermute | solution.py:364
  898.7 22.9 %collective-permute-start.70 = (bf16[72,2304]{1,0:T(8,128)(2,1)}, bf16[72,2304]{1,0:T(8,128)(2,1)S(1)}, u32[]{:S(2)}, u32[]{:S(2)}) collective-permute-start(bf16[72,2304]{1,0:T(8,128)(2,1)} %after.74), channel_id=1, source_target_pairs={{0,0},{1,4},{2,1},{3,5},{4,2},{5,6},{6,3},{7,7},{8,8},{9,12},{10,9... | collective-permute-start | bytes 995336 | tf_op jit(solution)/shard_map/ppermute | solution.py:364
  (90 other events, 1165.2 us)
Sparse Core Ops, SparseCore 0:
  76.0 116.2 all-gather.4
  194.4 30.5 all-gather.6
  226.6 128.0 all-gather.8
  356.1 67.9 all-gather.10
  442.0 63.8 reduce-scatter.4
  526.0 121.6 reduce-scatter.6
  650.6 31.9 reduce-scatter.8
  714.9 83.8 reduce-scatter.10

commit v5 on v4

--- a/solution.py
+++ b/solution.py
@@ -400,19 +400,26 @@
 
         def shuffle_out(arrays, beside):
             parts = [array.reshape(n_tok, quarter, width) for array in arrays]
-            results = [jnp.zeros_like(part) for part in parts]
+            pieces = []
             for turn_by in range(n_grp):
                 away = g ^ t ^ turn_by
-                pieces = [lax.dynamic_index_in_dim(part, away, 0, keepdims=True) for part in parts]
+                piece = [lax.dynamic_index_in_dim(part, away, 0, keepdims=True) for part in parts]
                 piece = send(
-                    jnp.concatenate(pieces, axis=1),
+                    jnp.concatenate(piece, axis=1),
                     lambda g, t, f, turn_by=turn_by: (t, g ^ t ^ turn_by, f),
                 )
-                piece = after(piece, beside)
-                for i, result in enumerate(results):
-                    results[i] = lax.dynamic_update_slice_in_dim(
-                        result, piece[:, i * quarter : (i + 1) * quarter], away, 0
-                    )
+                pieces.append(after(piece, beside))
+
+            def arrived_from(place):
+                chosen = pieces[place]
+                for step in range(1, n_grp):
+                    chosen = jnp.where(g ^ t == step, pieces[place ^ step], chosen)
+                return chosen
+
+            found = jnp.concatenate([arrived_from(place) for place in range(n_grp)], axis=0)
+            results = [
+                found[:, i * quarter : (i + 1) * quarter] for i in range(len(arrays))
+            ]
             return [result.reshape(rows, width) for result in results]
 
 

time: 944 us -> 953 us (level)
  waiting for transfers between devices: 248 us -> 279 us
  starting transfers between devices: 144 us -> 129 us
    ppermute x72, waiting for transfers between devices: 196 us -> 213 us  [send(): return lax.ppermute(array, ALL, permutation(move))]
    ppermute x72, starting transfers between devices: 110 us -> 94.2 us  [send(): return lax.ppermute(array, ALL, permutation(move))]
    unnamed x166 -> x174, local copies, waits for them, and re-layouts: 64.6 us -> 66.5 us
  transfers between devices with their start and end apart: 87 -> 87, of which waited for: 25 -> 26; matrix products, arithmetic and copies ran while one was open for 44% -> 42% of each run, Pallas kernels for 10% -> 9%
where the time goes in v5:
time: 953 us; the launch traced here: 941 us
  waiting for transfers between devices  279 us (29%)
  matrix products  178 us (19%)
  local copies, waits for them, and re-layouts  151 us (16%)
  starting transfers between devices  129 us (14%)
  other arithmetic  98.3 us (10%)
  Pallas kernels  88.6 us (9%)
  between operations  16 us (2%)
    ppermute x72, waiting for transfers between devices, send(): return lax.ppermute(array, ALL, permutation(move))  213 us
    ppermute x72, starting transfers between devices, send(): return lax.ppermute(array, ALL, permutation(move))  94.2 us
    dot_general x8, matrix products, nt_dot(): lax.dot_general(left, right, (((1,), (1,)), ((), ())), preferred_element_...  73.4 us
    unnamed x174, local copies, waits for them, and re-layouts  66.5 us
    pallas_call x1, Pallas kernels, attend_back(): pl.pallas_call(functools.partial(attend_back_kernel, first), grid_spec=pl...  55.2 us
    dot_general x6, matrix products, nn_dot(): lax.dot_general(left, right, (((1,), (0,)), ((), ())), preferred_element_...  53.5 us
    dot_general x4, matrix products, tn_dot(): lax.dot_general(left, right, (((0,), (0,)), ((), ())), preferred_element_...  51.1 us
    pallas_call x1, Pallas kernels, attend(): pl.pallas_call(attend_kernel, grid_spec=pltpu.PrefetchScalarGridSpec(num_...  33.4 us
  transfers between devices with their start and end apart: 87, of which 26 were waited for; matrix products, arithmetic and copies ran while one was open for 42% of the time, Pallas kernels for 9%

profile of v5, /device:TPU:1, one launch (start us, length us, event | category | flops | bytes accessed | tf_op | source)
XLA Modules:
  0.0 940.8 jit_solution(8451095997145840542)
XLA Ops:
  9.7 4.3 all-to-all-start
  14.1 15.3 %all-to-all-done.refs_1_ = bf16[4,64,2304]{2,1,0:T(8,128)(2,1)} async-done(((bf16[4,64,2304]{2,1,0:T(8,128)(2,1)}), bf16[4,64,2304]{2,1,0:T(8,128)(2,1)}, u32[]{:S(2)}, u32[]{:S(2)}) %all-to-all-start) | async-done | bytes 1179680 | tf_op jit(solution)/shard_map/all_to_all | solution.py:396
  31.9 4.6 all-to-all-start.1
  50.9 4.6 constant_dynamic-slice_fusion.35
  55.5 3.3 concatenate.94
  58.8 3.2 concatenate.93
  67.8 4.3 all-to-all-start.2
  81.2 5.4 all-to-all-done.2.refs_0_
  95.3 7.5 all-to-all-start.3
  105.4 13.1 %collective-permute-done.3 = bf16[256,2304]{1,0:T(8,128)(2,1)} collective-permute-done((bf16[256,2304]{1,0:T(8,128)(2,1)}, bf16[256,2304]{1,0:T(8,128)(2,1)}, u32[]{:S(2)}, u32[]{:S(2)}) %collective-permute-start.3) | collective-permute-done | bytes 1179680 | tf_op jit(solution)/shard_map/ppermute | solution.py:364
  119.8 3.6 collective-permute-start.8
  126.9 5.3 collective-permute-done.5
  132.2 3.2 collective-permute-start.9
  144.5 18.7 %all-to-all-done.3 = bf16[4,64,2304]{2,1,0:T(8,128)(2,1)S(1)} async-done(((bf16[4,64,2304]{2,1,0:T(8,128)(2,1)}), bf16[4,64,2304]{2,1,0:T(8,128)(2,1)S(1)}, u32[]{:S(2)}, u32[]{:S(2)}) %all-to-all-start.3) | async-done | bytes 1179680 | tf_op jit(solution)/shard_map/all_to_all | solution.py:399
  164.6 3.3 collective-permute-start.12
  168.4 7.8 copy.177.refs_0_
  181.0 9.7 %collective-permute-done.11.refs_1_ = bf16[256,2304]{1,0:T(8,128)(2,1)} collective-permute-done((bf16[256,2304]{1,0:T(8,128)(2,1)}, bf16[256,2304]{1,0:T(8,128)(2,1)}, u32[]{:S(2)}, u32[]{:S(2)}) %collective-permute-start.11) | collective-permute-done | bytes 1179680 | tf_op jit(solution)/shard_map/ppermute | solution.py:364
  202.4 15.8 %fusion.79.raw_ref.refs_1_ = f32[2048,1024]{1,0:T(8,128)} fusion(bf16[2048,2304]{1,0:T(8,128)(2,1)} %after.42, bf16[2304,1024]{1,0:T(8,128)(2,1)} %all-gather.5.cloned.1.call-done), kind=kOutput, calls=%fused_computation.313 | convolution fusion | flops 9663676416 | bytes 22544384 | tf_op jit(solution)/shard_map/dot_general | solution.py:98
  218.2 4.7 all-gather.7.cloned.1.call-done.refs_0_
  222.9 4.3 all-to-all-start.4
  227.2 33.4 %attend.1 = (bf16[2048,384]{1,0:T(8,128)(2,1)S(1)}, bf16[3,2048,384]{2,1,0:T(8,128)(2,1)S(1)}) custom-call(s32[33]{0:T(128)S(1)} %pad_add_fusion.index_ref, f32[2048,1024]{1,0:T(8,128)} %fusion.79.raw_ref.refs_1_, f32[1280,128]{1,0:T(8,128)S(1)} %get-tuple-element.137.cos_ref, f32[1280,128]{1,0:T(8,128)S(1)} %get-tuple-element.136.sin_ref), custom_call_target="tpu_custom_call" | custom-call | flops 35999997952 | bytes 1048576 | tf_op jit(solution)/shard_map/attend/pallas_call | solution.py:187
  297.2 18.0 %collective-permute-done.27.refs_0_ = bf16[256,2304]{1,0:T(8,128)(2,1)S(1)} collective-permute-done((bf16[256,2304]{1,0:T(8,128)(2,1)S(1)}, bf16[256,2304]{1,0:T(8,128)(2,1)S(1)}, u32[]{:S(2)}, u32[]{:S(2)}) %collective-permute-start.27) | collective-permute-done | bytes 1179680 | tf_op jit(solution)/shard_map/ppermute | solution.py:364
  316.4 25.4 %collective-permute-done.17.refs_0_ = bf16[256,2304]{1,0:T(8,128)(2,1)} collective-permute-done((bf16[256,2304]{1,0:T(8,128)(2,1)}, bf16[256,2304]{1,0:T(8,128)(2,1)}, u32[]{:S(2)}, u32[]{:S(2)}) %collective-permute-start.17) | collective-permute-done | bytes 1179680 | tf_op jit(solution)/shard_map/ppermute | solution.py:364
  341.8 4.2 multiply_reduce_fusion.1
  352.5 22.8 %collective-permute-done.28 = bf16[256,2304]{1,0:T(8,128)(2,1)} collective-permute-done((bf16[256,2304]{1,0:T(8,128)(2,1)}, bf16[256,2304]{1,0:T(8,128)(2,1)}, u32[]{:S(2)}, u32[]{:S(2)}) %collective-permute-start.28) | collective-permute-done | bytes 1179680 | tf_op jit(solution)/shard_map/ppermute | solution.py:364
  384.7 5.0 collective-permute-done.30
  390.0 3.2 collective-permute-start.35
  399.4 19.5 %fusion.80 = f32[2048,1536]{1,0:T(8,128)S(1)} fusion(bf16[2048,2304]{1,0:T(8,128)(2,1)} %constant_dynamic-update-slice_fusion.18, bf16[2304,1536]{1,0:T(8,128)(2,1)} %all-gather.9.cloned.1.call-done), kind=kOutput, calls=%fused_computation.314 | convolution fusion | flops 14495514624 | bytes 29097984 | tf_op jit(solution)/shard_map/dot_general | solution.py:98
  418.9 4.6 copy-done.20
  425.7 13.9 %convolution_convert_fusion.5 = bf16[768,2304]{1,0:T(8,128)(2,1)} fusion(bf16[2048,768]{1,0:T(8,128)(2,1)S(1)} %multiply_convert_fusion.2.refs_0_, bf16[2048,2304]{1,0:T(8,128)(2,1)} %constant_dynamic-update-slice_fusion.9.refs_1_.refs_0_), kind=kOutput, calls=%fused_computation.15 | convolution fusion | flops 7249526784 | bytes 16121856 | tf_op jit(solution)/shard_map/dot_general | solution.py:94
  439.7 16.4 %multiply_convert_fusion = (bf16[2048,768]{1,0:T(8,128)(2,1)S(1)}, bf16[2048,768]{1,0:T(8,128)(2,1)S(1)}) fusion(f32[2048,1536]{1,0:T(8,128)} %copy-done.20, bf16[2048,2304]{1,0:T(8,128)(2,1)} %after.50, bf16[768,2304]{1,0:T(8,128)(2,1)} %all-gather.11.cloned.1.call-done), kind=kOutput, calls=%fused_computation.6 | convolution fusion | flops 7268204544 | bytes 31850496 | tf_op jit(solution)/shard_map/dot_general | solution.py:90
  456.0 10.6 %fusion.7 = f32[1024,2304]{1,0:T(8,128)} fusion(bf16[2304,1536]{1,0:T(8,128)(2,1)} %all-gather.9.cloned.1.call-done, bf16[2048,768]{1,0:T(8,128)(2,1)S(1)} %get-tuple-element.34.refs_0_), kind=kOutput, calls=%fused_computation.25 | convolution fusion | flops 3623878656 | bytes 14548992 | tf_op jit(solution)/shard_map/dot_general | solution.py:90
  466.6 7.7 add_convert_fusion
  476.7 8.4 fusion.9
  485.1 7.7 convolution_add_fusion
  492.8 3.5 fusion.31
  500.8 19.3 %convolution_convert_fusion = bf16[2304,1536]{1,0:T(8,128)(2,1)S(1)} fusion(bf16[2048,2304]{1,0:T(8,128)(2,1)} %constant_dynamic-update-slice_fusion.18, bf16[2048,768]{1,0:T(8,128)(2,1)} %after.53, bf16[2048,768]{1,0:T(8,128)(2,1)} %after.52), kind=kOutput, calls=%fused_computation | convolution fusion | flops 14511636480 | bytes 22806528 | tf_op jit(solution)/shard_map/dot_general | solution.py:94
  520.1 3.5 copy.111
  526.5 25.7 %collective-permute-done.38.refs_0_ = bf16[256,2304]{1,0:T(8,128)(2,1)S(1)} collective-permute-done((bf16[256,2304]{1,0:T(8,128)(2,1)}, bf16[256,2304]{1,0:T(8,128)(2,1)S(1)}, u32[]{:S(2)}, u32[]{:S(2)}) %collective-permute-start.38) | collective-permute-done | bytes 1179680 | tf_op jit(solution)/shard_map/ppermute | solution.py:364
  553.2 4.9 multiply_reduce_fusion
  562.4 6.3 convolution_convert_fusion.1
  575.0 6.4 fusion.42
  581.4 6.4 collective-permute-done.45
  594.8 6.9 fusion.26
  605.1 3.3 collective-permute-done.48
  612.2 4.0 fusion.81
  616.7 6.3 convolution_convert_fusion.6.refs_0_
  631.9 55.2 %attend_back.1.refs_0_ = bf16[2048,1024]{1,0:T(8,128)(2,1)} custom-call(s32[33]{0:T(128)S(1)} %pad_add_fusion.index_ref, bf16[3,2048,384]{2,1,0:T(8,128)(2,1)} %copy-done.5, bf16[2048,384]{1,0:T(8,128)(2,1)S(1)} %copy-done.2, f32[1280,128]{1,0:T(8,128)S(1)} %get-tuple-element.137.cos_ref, f32[1280,128]{1,0:T(8,128)S(1)} %get-tuple-element.136.sin_ref), custom_call_target="tpu_custom_call" | custom-call | bytes 1048576 | tf_op jit(solution)/shard_map/attend_back/pallas_call | solution.py:308
  691.4 4.5 all-to-all-start.5
  696.0 13.8 %convolution_convert_fusion.4 = bf16[2304,1024]{1,0:T(8,128)(2,1)S(1)} fusion(bf16[2048,2304]{1,0:T(8,128)(2,1)} %constant_dynamic-update-slice_fusion.refs_1_.refs_2_, bf16[2048,1024]{1,0:T(8,128)(2,1)} %after.62.refs_1_.refs_0_), kind=kOutput, calls=%fused_computation.14 | convolution fusion | flops 9666035712 | bytes 18350080 | tf_op jit(solution)/shard_map/dot_general | solution.py:94
  716.8 9.0 convolution_convert_fusion.3
  730.4 7.4 fusion.39
  748.7 20.2 %collective-permute-done.60.refs_1_ = bf16[256,2304]{1,0:T(8,128)(2,1)S(1)} collective-permute-done((bf16[256,2304]{1,0:T(8,128)(2,1)S(1)}, bf16[256,2304]{1,0:T(8,128)(2,1)S(1)}, u32[]{:S(2)}, u32[]{:S(2)}) %collective-permute-start.60) | collective-permute-done | bytes 1179680 | tf_op jit(solution)/shard_map/ppermute | solution.py:364
  770.0 26.6 %collective-permute-done.65 = bf16[256,2304]{1,0:T(8,128)(2,1)} collective-permute-done((bf16[256,2304]{1,0:T(8,128)(2,1)}, bf16[256,2304]{1,0:T(8,128)(2,1)}, u32[]{:S(2)}, u32[]{:S(2)}) %collective-permute-start.65) | collective-permute-done | bytes 1179680 | tf_op jit(solution)/shard_map/ppermute | solution.py:364
  796.6 3.8 fusion.20
  800.4 3.9 add_convert_fusion.1
  815.9 4.6 all-to-all-start.6
  826.3 5.3 collective-permute-start.68
  832.5 6.0 collective-permute-start.69
  838.5 17.8 %all-to-all-done.6.refs_1_ = bf16[8,72,1024]{2,1,0:T(8,128)(2,1)S(1)} async-done(((bf16[8,72,1024]{2,1,0:T(8,128)(2,1)}), bf16[8,72,1024]{2,1,0:T(8,128)(2,1)S(1)}, u32[]{:S(2)}, u32[]{:S(2)}) %all-to-all-start.6) | async-done | bytes 1179680 | tf_op jit(solution)/shard_map/all_to_all | solution.py:646
  865.3 5.3 reshape.400
  874.0 3.2 reshape.408.refs_4_
  892.3 8.1 collective-permute-start.70
  904.6 25.6 %collective-permute-done.70 = bf16[72,2304]{1,0:T(8,128)(2,1)S(1)} collective-permute-done((bf16[72,2304]{1,0:T(8,128)(2,1)}, bf16[72,2304]{1,0:T(8,128)(2,1)S(1)}, u32[]{:S(2)}, u32[]{:S(2)}) %collective-permute-start.70) | collective-permute-done | bytes 331808 | tf_op jit(solution)/shard_map/ppermute | solution.py:364
  (491 shorter events, 265.4 us)
Async XLA Ops:
  9.7 19.7 %all-to-all-start = ((bf16[4,64,2304]{2,1,0:T(8,128)(2,1)}), bf16[4,64,2304]{2,1,0:T(8,128)(2,1)}, u32[]{:S(2)}, u32[]{:S(2)}) async-start(bf16[4,64,2304]{2,1,0:T(8,128)(2,1)} %bitcast.199), calls=%async_computation | async-start | bytes 2359296 | tf_op jit(solution)/shard_map/all_to_all | solution.py:396
  31.9 35.9 %all-to-all-start.1 = ((bf16[4,72,2304]{2,1,0:T(8,128)(2,1)}), bf16[4,72,2304]{2,1,0:T(8,128)(2,1)}, u32[]{:S(2)}, u32[]{:S(2)}) async-start(bf16[4,72,2304]{2,1,0:T(8,128)(2,1)} %pad_maximum_fusion.2), calls=%async_computation.1 | async-start | bytes 2654208 | tf_op jit(solution)/shard_map/all_to_all | solution.py:471
  67.8 18.8 %all-to-all-start.2 = ((bf16[4,64,2304]{2,1,0:T(8,128)(2,1)}), bf16[4,64,2304]{2,1,0:T(8,128)(2,1)}, u32[]{:S(2)}, u32[]{:S(2)}) async-start(bf16[4,64,2304]{2,1,0:T(8,128)(2,1)} %bitcast.185), calls=%async_computation.2 | async-start | bytes 2359296 | tf_op jit(solution)/shard_map/all_to_all | solution.py:396
  72.0 130.4 %all-gather.5.cloned.1.call-start = ((), (), s32[]{:S(2)}) async-start(), calls=%async_computation.11 | async-start | bytes 5898240 | tf_op jit(solution)/shard_map/all_gather | solution.py:517
  92.2 26.3 %collective-permute-start.3 = (bf16[256,2304]{1,0:T(8,128)(2,1)}, bf16[256,2304]{1,0:T(8,128)(2,1)}, u32[]{:S(2)}, u32[]{:S(2)}) collective-permute-start(bf16[256,2304]{1,0:T(8,128)(2,1)} %get-tuple-element.32), channel_id=1, source_target_pairs={{0,8},{1,9},{2,10},{3,11},{4,12},{5,13},{6,14},{7,15},{8,0},{9,1},... | collective-permute-start | bytes 3538952 | tf_op jit(solution)/shard_map/ppermute | solution.py:364
  92.6 27.1 %collective-permute-start.4 = (bf16[256,2304]{1,0:T(8,128)(2,1)}, bf16[256,2304]{1,0:T(8,128)(2,1)S(1)}, u32[]{:S(2)}, u32[]{:S(2)}) collective-permute-start(bf16[256,2304]{1,0:T(8,128)(2,1)} %get-tuple-element.32), channel_id=1, source_target_pairs={{0,16},{1,17},{2,18},{3,19},{4,20},{5,21},{6,22},{7,23},{8,24},{9,... | collective-permute-start | bytes 3538952 | tf_op jit(solution)/shard_map/ppermute | solution.py:364
  92.8 51.6 %collective-permute-start.1 = (s32[1,16]{1,0:T(1,128)S(1)}, s32[1,16]{1,0:T(1,128)S(1)}, u32[]{:S(2)}, u32[]{:S(2)}) collective-permute-start(s32[1,16]{1,0:T(1,128)S(1)} %copy-done.67), channel_id=1, source_target_pairs={{0,0},{1,1},{2,8},{3,9},{4,16},{5,17},{6,24},{7,25},{8,2},{9,3},{1... | collective-permute-start | bytes 200 | tf_op jit(solution)/shard_map/ppermute | solution.py:364
  95.3 67.9 %all-to-all-start.3 = ((bf16[4,64,2304]{2,1,0:T(8,128)(2,1)}), bf16[4,64,2304]{2,1,0:T(8,128)(2,1)S(1)}, u32[]{:S(2)}, u32[]{:S(2)}) async-start(bf16[4,64,2304]{2,1,0:T(8,128)(2,1)} %after.40), calls=%async_computation.3 | async-start | bytes 2359296 | tf_op jit(solution)/shard_map/all_to_all | solution.py:399
  102.8 120.1 %all-gather.7.cloned.1.call-start = ((), (), s32[]{:S(2)}) async-start(), calls=%async_computation.12 | async-start | bytes 1658880 | tf_op jit(solution)/shard_map/all_gather | solution.py:517
  102.8 34.6 %collective-permute-start.7 = (bf16[256,2304]{1,0:T(8,128)(2,1)}, bf16[256,2304]{1,0:T(8,128)(2,1)S(1)}, u32[]{:S(2)}, u32[]{:S(2)}) collective-permute-start(bf16[256,2304]{1,0:T(8,128)(2,1)} %get-tuple-element.32), channel_id=1, source_target_pairs={{0,1},{1,0},{2,3},{3,2},{4,5},{5,4},{6,7},{7,6},{8,9},{9,8},{10,11... | collective-permute-start | bytes 3538952 | tf_op jit(solution)/shard_map/ppermute | solution.py:364
  119.7 15.7 %collective-permute-start.6 = (bf16[128,2304]{1,0:T(8,128)(2,1)S(1)}, bf16[128,2304]{1,0:T(8,128)(2,1)S(1)}, u32[]{:S(2)}, u32[]{:S(2)}) collective-permute-start(bf16[128,2304]{1,0:T(8,128)(2,1)S(1)} %slice.469), channel_id=1, source_target_pairs={{0,8},{1,9},{2,10},{3,11},{4,12},{5,13},{6,14},{7,15},{8,0},{9,1},... | collective-permute-start | bytes 1769480 | tf_op jit(solution)/shard_map/ppermute | solution.py:364
  119.8 18.8 %collective-permute-start.8 = (bf16[256,2304]{1,0:T(8,128)(2,1)}, bf16[256,2304]{1,0:T(8,128)(2,1)S(1)}, u32[]{:S(2)}, u32[]{:S(2)}) collective-permute-start(bf16[256,2304]{1,0:T(8,128)(2,1)} %collective-permute-done.3), channel_id=1, source_target_pairs={{0,1},{1,0},{2,3},{3,2},{4,5},{5,4},{6,7},{7,6},{8,9},{9,8},{10,11... | collective-permute-start | bytes 3538952 | tf_op jit(solution)/shard_map/ppermute | solution.py:364
  164.6 26.1 %collective-permute-start.11 = (bf16[256,2304]{1,0:T(8,128)(2,1)}, bf16[256,2304]{1,0:T(8,128)(2,1)}, u32[]{:S(2)}, u32[]{:S(2)}) collective-permute-start(bf16[256,2304]{1,0:T(8,128)(2,1)} %after.41), channel_id=1, source_target_pairs={{0,8},{1,9},{2,10},{3,11},{4,12},{5,13},{6,14},{7,15},{8,0},{9,1},... | collective-permute-start | bytes 3538952 | tf_op jit(solution)/shard_map/ppermute | solution.py:364
  164.6 30.5 %collective-permute-start.12 = (bf16[256,2304]{1,0:T(8,128)(2,1)}, bf16[256,2304]{1,0:T(8,128)(2,1)S(1)}, u32[]{:S(2)}, u32[]{:S(2)}) collective-permute-start(bf16[256,2304]{1,0:T(8,128)(2,1)} %after.41), channel_id=1, source_target_pairs={{0,16},{1,17},{2,18},{3,19},{4,20},{5,21},{6,22},{7,23},{8,24},{9,... | collective-permute-start | bytes 3538952 | tf_op jit(solution)/shard_map/ppermute | solution.py:364
  176.2 111.0 %collective-permute-start.20 = (bf16[256,2304]{1,0:T(8,128)(2,1)}, bf16[256,2304]{1,0:T(8,128)(2,1)}, u32[]{:S(2)}, u32[]{:S(2)}) collective-permute-start(bf16[256,2304]{1,0:T(8,128)(2,1)} %after.41), channel_id=1, source_target_pairs={{0,1},{1,0},{2,3},{3,2},{4,5},{5,4},{6,7},{7,6},{8,9},{9,8},{10,11... | collective-permute-start | bytes 3538952 | tf_op jit(solution)/shard_map/ppermute | solution.py:364
  177.9 221.5 %all-gather.9.cloned.1.call-start = ((), (), s32[]{:S(2)}) async-start(), calls=%async_computation.13 | async-start | bytes 8847360 | tf_op jit(solution)/shard_map/all_gather | solution.py:517
  192.6 81.3 %collective-permute-start.18 = (bf16[128,2304]{1,0:T(8,128)(2,1)}, bf16[128,2304]{1,0:T(8,128)(2,1)}, u32[]{:S(2)}, u32[]{:S(2)}) collective-permute-start(bf16[128,2304]{1,0:T(8,128)(2,1)} %slice.478), channel_id=1, source_target_pairs={{0,16},{1,17},{2,18},{3,19},{4,20},{5,21},{6,22},{7,23},{8,24},{9,... | collective-permute-start | bytes 1769480 | tf_op jit(solution)/shard_map/ppermute | solution.py:364
  196.1 80.3 %collective-permute-start.19 = (bf16[128,2304]{1,0:T(8,128)(2,1)}, bf16[128,2304]{1,0:T(8,128)(2,1)}, u32[]{:S(2)}, u32[]{:S(2)}) collective-permute-start(bf16[128,2304]{1,0:T(8,128)(2,1)} %slice.479), channel_id=1, source_target_pairs={{0,8},{1,9},{2,10},{3,11},{4,12},{5,13},{6,14},{7,15},{8,0},{9,1},... | collective-permute-start | bytes 1769480 | tf_op jit(solution)/shard_map/ppermute | solution.py:364
  197.5 91.5 %collective-permute-start.21 = (bf16[256,2304]{1,0:T(8,128)(2,1)}, bf16[256,2304]{1,0:T(8,128)(2,1)}, u32[]{:S(2)}, u32[]{:S(2)}) collective-permute-start(bf16[256,2304]{1,0:T(8,128)(2,1)} %collective-permute-done.11.refs_1_), channel_id=1, source_target_pairs={{0,1},{1,0},{2,3},{3,2},{4,5},{5,4},{6,7},{7,6},{8,9},{9,8},{10,11... | collective-permute-start | bytes 3538952 | tf_op jit(solution)/shard_map/ppermute | solution.py:364
  222.9 39.9 %all-to-all-start.4 = ((bf16[4,72,2304]{2,1,0:T(8,128)(2,1)}), bf16[4,72,2304]{2,1,0:T(8,128)(2,1)}, u32[]{:S(2)}, u32[]{:S(2)}) async-start(bf16[4,72,2304]{2,1,0:T(8,128)(2,1)} %bitcast.191), calls=%async_computation.4 | async-start | bytes 2654208 | tf_op jit(solution)/shard_map/all_to_all | solution.py:557
  227.2 212.5 %all-gather.11.cloned.1.call-start = ((), (), s32[]{:S(2)}) async-start(), calls=%async_computation.14 | async-start | bytes 4423680 | tf_op jit(solution)/shard_map/all_gather | solution.py:517
  283.0 58.8 %collective-permute-start.15 = (bf16[256,2304]{1,0:T(8,128)(2,1)}, bf16[256,2304]{1,0:T(8,128)(2,1)}, u32[]{:S(2)}, u32[]{:S(2)}) collective-permute-start(bf16[256,2304]{1,0:T(8,128)(2,1)} %get-tuple-element.61), channel_id=1, source_target_pairs={{0,1},{1,0},{2,3},{3,2},{4,5},{5,4},{6,7},{7,6},{8,9},{9,8},{10,11... | collective-permute-start | bytes 3538952 | tf_op jit(solution)/shard_map/ppermute | solution.py:364
  287.3 28.0 %collective-permute-start.27 = (bf16[256,2304]{1,0:T(8,128)(2,1)S(1)}, bf16[256,2304]{1,0:T(8,128)(2,1)S(1)}, u32[]{:S(2)}, u32[]{:S(2)}) collective-permute-start(bf16[256,2304]{1,0:T(8,128)(2,1)S(1)} %get-tuple-element.47), channel_id=1, source_target_pairs={{0,16},{1,17},{2,18},{3,19},{4,20},{5,21},{6,22},{7,23},{8,24},{9,... | collective-permute-start | bytes 3538952 | tf_op jit(solution)/shard_map/ppermute | solution.py:364
  288.9 27.5 %collective-permute-start.25 = (bf16[256,2304]{1,0:T(8,128)(2,1)}, bf16[256,2304]{1,0:T(8,128)(2,1)}, u32[]{:S(2)}, u32[]{:S(2)}) collective-permute-start(bf16[256,2304]{1,0:T(8,128)(2,1)} %get-tuple-element.48), channel_id=1, source_target_pairs={{0,8},{1,9},{2,10},{3,11},{4,12},{5,13},{6,14},{7,15},{8,0},{9,1},... | collective-permute-start | bytes 3538952 | tf_op jit(solution)/shard_map/ppermute | solution.py:364
  290.1 51.7 %collective-permute-start.17 = (bf16[256,2304]{1,0:T(8,128)(2,1)}, bf16[256,2304]{1,0:T(8,128)(2,1)}, u32[]{:S(2)}, u32[]{:S(2)}) collective-permute-start(bf16[256,2304]{1,0:T(8,128)(2,1)} %get-tuple-element.46), channel_id=1, source_target_pairs={{0,24},{1,25},{2,26},{3,27},{4,28},{5,29},{6,30},{7,31},{8,16},{9,... | collective-permute-start | bytes 3538952 | tf_op jit(solution)/shard_map/ppermute | solution.py:364
  348.4 27.0 %collective-permute-start.28 = (bf16[256,2304]{1,0:T(8,128)(2,1)}, bf16[256,2304]{1,0:T(8,128)(2,1)}, u32[]{:S(2)}, u32[]{:S(2)}) collective-permute-start(bf16[256,2304]{1,0:T(8,128)(2,1)} %get-tuple-element.28), channel_id=1, source_target_pairs={{0,8},{1,9},{2,10},{3,11},{4,12},{5,13},{6,14},{7,15},{8,0},{9,1},... | collective-permute-start | bytes 3538952 | tf_op jit(solution)/shard_map/ppermute | solution.py:364
  349.5 27.8 %collective-permute-start.29 = (bf16[256,2304]{1,0:T(8,128)(2,1)}, bf16[256,2304]{1,0:T(8,128)(2,1)S(1)}, u32[]{:S(2)}, u32[]{:S(2)}) collective-permute-start(bf16[256,2304]{1,0:T(8,128)(2,1)} %get-tuple-element.28), channel_id=1, source_target_pairs={{0,16},{1,17},{2,18},{3,19},{4,20},{5,21},{6,22},{7,23},{8,24},{9,... | collective-permute-start | bytes 3538952 | tf_op jit(solution)/shard_map/ppermute | solution.py:364
  350.7 277.6 %reduce-scatter.5.cloned.1.call-start = ((), (), s32[]{:S(2)}) async-start(), calls=%async_computation.15 | async-start | bytes 4423680 | tf_op jit(solution)/shard_map/reduce_scatter | solution.py:673
  350.8 44.2 %collective-permute-start.32 = (bf16[256,2304]{1,0:T(8,128)(2,1)}, bf16[256,2304]{1,0:T(8,128)(2,1)S(1)}, u32[]{:S(2)}, u32[]{:S(2)}) collective-permute-start(bf16[256,2304]{1,0:T(8,128)(2,1)} %get-tuple-element.28), channel_id=1, source_target_pairs={{0,1},{1,0},{2,3},{3,2},{4,5},{5,4},{6,7},{7,6},{8,9},{9,8},{10,11... | collective-permute-start | bytes 3538952 | tf_op jit(solution)/shard_map/ppermute | solution.py:364
  378.6 17.4 %collective-permute-start.33 = (bf16[256,2304]{1,0:T(8,128)(2,1)}, bf16[256,2304]{1,0:T(8,128)(2,1)S(1)}, u32[]{:S(2)}, u32[]{:S(2)}) collective-permute-start(bf16[256,2304]{1,0:T(8,128)(2,1)} %collective-permute-done.28), channel_id=1, source_target_pairs={{0,1},{1,0},{2,3},{3,2},{4,5},{5,4},{6,7},{7,6},{8,9},{9,8},{10,11... | collective-permute-start | bytes 3538952 | tf_op jit(solution)/shard_map/ppermute | solution.py:364
  381.3 15.9 %collective-permute-start.34 = (bf16[256,2304]{1,0:T(8,128)(2,1)S(1)}, bf16[256,2304]{1,0:T(8,128)(2,1)S(1)}, u32[]{:S(2)}, u32[]{:S(2)}) collective-permute-start(bf16[256,2304]{1,0:T(8,128)(2,1)S(1)} %collective-permute-done.29), channel_id=1, source_target_pairs={{0,1},{1,0},{2,3},{3,2},{4,5},{5,4},{6,7},{7,6},{8,9},{9,8},{10,11... | collective-permute-start | bytes 3538952 | tf_op jit(solution)/shard_map/ppermute | solution.py:364
  439.6 247.6 %reduce-scatter.7.cloned.1.call-start = ((), (), s32[]{:S(2)}) async-start(), calls=%async_computation.16 | async-start | bytes 8847360 | tf_op jit(solution)/shard_map/reduce_scatter | solution.py:635
  475.7 17.1 %collective-permute-start.37 = (bf16[256,2304]{1,0:T(8,128)(2,1)S(1)}, bf16[256,2304]{1,0:T(8,128)(2,1)S(1)}, u32[]{:S(2)}, u32[]{:S(2)}) collective-permute-start(bf16[256,2304]{1,0:T(8,128)(2,1)S(1)} %get-tuple-element.60), channel_id=1, source_target_pairs={{0,1},{1,0},{2,3},{3,2},{4,5},{5,4},{6,7},{7,6},{8,9},{9,8},{10,11... | collective-permute-start | bytes 3538952 | tf_op jit(solution)/shard_map/ppermute | solution.py:364
  475.7 17.0 %collective-permute-start.41 = (bf16[256,2304]{1,0:T(8,128)(2,1)S(1)}, bf16[256,2304]{1,0:T(8,128)(2,1)S(1)}, u32[]{:S(2)}, u32[]{:S(2)}) collective-permute-start(bf16[256,2304]{1,0:T(8,128)(2,1)S(1)} %get-tuple-element.58), channel_id=1, source_target_pairs={{0,1},{1,0},{2,3},{3,2},{4,5},{5,4},{6,7},{7,6},{8,9},{9,8},{10,11... | collective-permute-start | bytes 3538952 | tf_op jit(solution)/shard_map/ppermute | solution.py:364
  476.2 16.6 %collective-permute-start.39 = (bf16[256,2304]{1,0:T(8,128)(2,1)S(1)}, bf16[256,2304]{1,0:T(8,128)(2,1)S(1)}, u32[]{:S(2)}, u32[]{:S(2)}) collective-permute-start(bf16[256,2304]{1,0:T(8,128)(2,1)S(1)} %get-tuple-element.59), channel_id=1, source_target_pairs={{0,1},{1,0},{2,3},{3,2},{4,5},{5,4},{6,7},{7,6},{8,9},{9,8},{10,11... | collective-permute-start | bytes 3538952 | tf_op jit(solution)/shard_map/ppermute | solution.py:364
  476.2 77.0 %collective-permute-start.36 = (bf16[256,2304]{1,0:T(8,128)(2,1)}, bf16[256,2304]{1,0:T(8,128)(2,1)}, u32[]{:S(2)}, u32[]{:S(2)}) collective-permute-start(bf16[256,2304]{1,0:T(8,128)(2,1)} %get-tuple-element.57), channel_id=1, source_target_pairs={{0,1},{1,0},{2,3},{3,2},{4,5},{5,4},{6,7},{7,6},{8,9},{9,8},{10,11... | collective-permute-start | bytes 3538952 | tf_op jit(solution)/shard_map/ppermute | solution.py:364
  498.1 27.9 %collective-permute-start.42 = (bf16[256,2304]{1,0:T(8,128)(2,1)}, bf16[256,2304]{1,0:T(8,128)(2,1)}, u32[]{:S(2)}, u32[]{:S(2)}) collective-permute-start(bf16[256,2304]{1,0:T(8,128)(2,1)} %get-tuple-element.43), channel_id=1, source_target_pairs={{0,16},{1,17},{2,18},{3,19},{4,20},{5,21},{6,22},{7,23},{8,24},{9,... | collective-permute-start | bytes 3538952 | tf_op jit(solution)/shard_map/ppermute | solution.py:364
  498.9 27.6 %collective-permute-start.40 = (bf16[256,2304]{1,0:T(8,128)(2,1)}, bf16[256,2304]{1,0:T(8,128)(2,1)}, u32[]{:S(2)}, u32[]{:S(2)}) collective-permute-start(bf16[256,2304]{1,0:T(8,128)(2,1)} %get-tuple-element.44), channel_id=1, source_target_pairs={{0,8},{1,9},{2,10},{3,11},{4,12},{5,13},{6,14},{7,15},{8,0},{9,1},... | collective-permute-start | bytes 3538952 | tf_op jit(solution)/shard_map/ppermute | solution.py:364
  499.6 52.6 %collective-permute-start.38 = (bf16[256,2304]{1,0:T(8,128)(2,1)}, bf16[256,2304]{1,0:T(8,128)(2,1)S(1)}, u32[]{:S(2)}, u32[]{:S(2)}) collective-permute-start(bf16[256,2304]{1,0:T(8,128)(2,1)} %get-tuple-element.42), channel_id=1, source_target_pairs={{0,24},{1,25},{2,26},{3,27},{4,28},{5,29},{6,30},{7,31},{8,16},{9,... | collective-permute-start | bytes 3538952 | tf_op jit(solution)/shard_map/ppermute | solution.py:364
  523.7 188.8 %reduce-scatter.9.cloned.1.call-start = ((), (), s32[]{:S(2)}) async-start(), calls=%async_computation.17 | async-start | bytes 1658880 | tf_op jit(solution)/shard_map/reduce_scatter | solution.py:692
  561.1 26.8 %collective-permute-start.45 = (bf16[256,2304]{1,0:T(8,128)(2,1)}, bf16[256,2304]{1,0:T(8,128)(2,1)S(1)}, u32[]{:S(2)}, u32[]{:S(2)}) collective-permute-start(bf16[256,2304]{1,0:T(8,128)(2,1)} %get-tuple-element.24.refs_1_), channel_id=1, source_target_pairs={{0,8},{1,9},{2,10},{3,11},{4,12},{5,13},{6,14},{7,15},{8,0},{9,1},... | collective-permute-start | bytes 3538952 | tf_op jit(solution)/shard_map/ppermute | solution.py:364
  562.4 28.1 %collective-permute-start.46 = (bf16[256,2304]{1,0:T(8,128)(2,1)}, bf16[256,2304]{1,0:T(8,128)(2,1)}, u32[]{:S(2)}, u32[]{:S(2)}) collective-permute-start(bf16[256,2304]{1,0:T(8,128)(2,1)} %get-tuple-element.24.refs_1_), channel_id=1, source_target_pairs={{0,16},{1,17},{2,18},{3,19},{4,20},{5,21},{6,22},{7,23},{8,24},{9,... | collective-permute-start | bytes 3538952 | tf_op jit(solution)/shard_map/ppermute | solution.py:364
  570.1 23.3 %collective-permute-start.57 = (bf16[256,2304]{1,0:T(8,128)(2,1)S(1)}, bf16[256,2304]{1,0:T(8,128)(2,1)S(1)}, u32[]{:S(2)}, u32[]{:S(2)}) collective-permute-start(bf16[256,2304]{1,0:T(8,128)(2,1)S(1)} %get-tuple-element.50), channel_id=1, source_target_pairs={{0,1},{1,0},{2,3},{3,2},{4,5},{5,4},{6,7},{7,6},{8,9},{9,8},{10,11... | collective-permute-start | bytes 3538952 | tf_op jit(solution)/shard_map/ppermute | solution.py:364
  571.7 22.3 %collective-permute-start.55 = (bf16[256,2304]{1,0:T(8,128)(2,1)S(1)}, bf16[256,2304]{1,0:T(8,128)(2,1)S(1)}, u32[]{:S(2)}, u32[]{:S(2)}) collective-permute-start(bf16[256,2304]{1,0:T(8,128)(2,1)S(1)} %get-tuple-element.51), channel_id=1, source_target_pairs={{0,1},{1,0},{2,3},{3,2},{4,5},{5,4},{6,7},{7,6},{8,9},{9,8},{10,11... | collective-permute-start | bytes 3538952 | tf_op jit(solution)/shard_map/ppermute | solution.py:364
  571.7 23.0 %collective-permute-start.44 = (bf16[256,2304]{1,0:T(8,128)(2,1)S(1)}, bf16[256,2304]{1,0:T(8,128)(2,1)S(1)}, u32[]{:S(2)}, u32[]{:S(2)}) collective-permute-start(bf16[256,2304]{1,0:T(8,128)(2,1)S(1)} %get-tuple-element.52), channel_id=1, source_target_pairs={{0,1},{1,0},{2,3},{3,2},{4,5},{5,4},{6,7},{7,6},{8,9},{9,8},{10,11... | collective-permute-start | bytes 3538952 | tf_op jit(solution)/shard_map/ppermute | solution.py:364
  587.8 21.8 %collective-permute-start.49 = (bf16[256,2304]{1,0:T(8,128)(2,1)}, bf16[256,2304]{1,0:T(8,128)(2,1)S(1)}, u32[]{:S(2)}, u32[]{:S(2)}) collective-permute-start(bf16[256,2304]{1,0:T(8,128)(2,1)} %get-tuple-element.24.refs_1_), channel_id=1, source_target_pairs={{0,1},{1,0},{2,3},{3,2},{4,5},{5,4},{6,7},{7,6},{8,9},{9,8},{10,11... | collective-permute-start | bytes 3538952 | tf_op jit(solution)/shard_map/ppermute | solution.py:364
  594.0 15.7 %collective-permute-start.50 = (bf16[256,2304]{1,0:T(8,128)(2,1)S(1)}, bf16[256,2304]{1,0:T(8,128)(2,1)S(1)}, u32[]{:S(2)}, u32[]{:S(2)}) collective-permute-start(bf16[256,2304]{1,0:T(8,128)(2,1)S(1)} %collective-permute-done.45), channel_id=1, source_target_pairs={{0,1},{1,0},{2,3},{3,2},{4,5},{5,4},{6,7},{7,6},{8,9},{9,8},{10,11... | collective-permute-start | bytes 3538952 | tf_op jit(solution)/shard_map/ppermute | solution.py:364
  623.2 64.0 %collective-permute-start.53 = (bf16[256,2304]{1,0:T(8,128)(2,1)}, bf16[256,2304]{1,0:T(8,128)(2,1)}, u32[]{:S(2)}, u32[]{:S(2)}) collective-permute-start(bf16[256,2304]{1,0:T(8,128)(2,1)} %after.58), channel_id=1, source_target_pairs={{0,24},{1,25},{2,26},{3,27},{4,28},{5,29},{6,30},{7,31},{8,16},{9,... | collective-permute-start | bytes 3538952 | tf_op jit(solution)/shard_map/ppermute | solution.py:364
  625.0 62.2 %collective-permute-start.56 = (bf16[256,2304]{1,0:T(8,128)(2,1)}, bf16[256,2304]{1,0:T(8,128)(2,1)}, u32[]{:S(2)}, u32[]{:S(2)}) collective-permute-start(bf16[256,2304]{1,0:T(8,128)(2,1)} %after.60), channel_id=1, source_target_pairs={{0,8},{1,9},{2,10},{3,11},{4,12},{5,13},{6,14},{7,15},{8,0},{9,1},... | collective-permute-start | bytes 3538952 | tf_op jit(solution)/shard_map/ppermute | solution.py:364
  625.1 62.0 %collective-permute-start.58 = (bf16[256,2304]{1,0:T(8,128)(2,1)}, bf16[256,2304]{1,0:T(8,128)(2,1)}, u32[]{:S(2)}, u32[]{:S(2)}) collective-permute-start(bf16[256,2304]{1,0:T(8,128)(2,1)} %after.61), channel_id=1, source_target_pairs={{0,16},{1,17},{2,18},{3,19},{4,20},{5,21},{6,22},{7,23},{8,24},{9,... | collective-permute-start | bytes 3538952 | tf_op jit(solution)/shard_map/ppermute | solution.py:364
  691.4 24.2 %all-to-all-start.5 = ((bf16[8,72,1536]{2,1,0:T(8,128)(2,1)}), bf16[8,72,1536]{2,1,0:T(8,128)(2,1)S(1)}, u32[]{:S(2)}, u32[]{:S(2)}) async-start(bf16[8,72,1536]{2,1,0:T(8,128)(2,1)} %select_select_fusion), calls=%async_computation.8 | async-start | bytes 3538944 | tf_op jit(solution)/shard_map/all_to_all | solution.py:646
  696.0 112.0 %reduce-scatter.11.cloned.1.call-start = ((), (), s32[]{:S(2)}) async-start(), calls=%async_computation.18 | async-start | bytes 5898240 | tf_op jit(solution)/shard_map/reduce_scatter | solution.py:635
  742.1 26.8 %collective-permute-start.60 = (bf16[256,2304]{1,0:T(8,128)(2,1)S(1)}, bf16[256,2304]{1,0:T(8,128)(2,1)S(1)}, u32[]{:S(2)}, u32[]{:S(2)}) collective-permute-start(bf16[256,2304]{1,0:T(8,128)(2,1)S(1)} %get-tuple-element.37), channel_id=1, source_target_pairs={{0,8},{1,9},{2,10},{3,11},{4,12},{5,13},{6,14},{7,15},{8,0},{9,1},... | collective-permute-start | bytes 3538952 | tf_op jit(solution)/shard_map/ppermute | solution.py:364
  742.6 27.3 %collective-permute-start.61 = (bf16[256,2304]{1,0:T(8,128)(2,1)}, bf16[256,2304]{1,0:T(8,128)(2,1)}, u32[]{:S(2)}, u32[]{:S(2)}) collective-permute-start(bf16[256,2304]{1,0:T(8,128)(2,1)} %get-tuple-element.53), channel_id=1, source_target_pairs={{0,1},{1,0},{2,3},{3,2},{4,5},{5,4},{6,7},{7,6},{8,9},{9,8},{10,11... | collective-permute-start | bytes 3538952 | tf_op jit(solution)/shard_map/ppermute | solution.py:364
  743.4 53.2 %collective-permute-start.65 = (bf16[256,2304]{1,0:T(8,128)(2,1)}, bf16[256,2304]{1,0:T(8,128)(2,1)}, u32[]{:S(2)}, u32[]{:S(2)}) collective-permute-start(bf16[256,2304]{1,0:T(8,128)(2,1)} %get-tuple-element.36), channel_id=1, source_target_pairs={{0,16},{1,17},{2,18},{3,19},{4,20},{5,21},{6,22},{7,23},{8,24},{9,... | collective-permute-start | bytes 3538952 | tf_op jit(solution)/shard_map/ppermute | solution.py:364
  744.0 52.6 %collective-permute-start.63 = (bf16[256,2304]{1,0:T(8,128)(2,1)}, bf16[256,2304]{1,0:T(8,128)(2,1)}, u32[]{:S(2)}, u32[]{:S(2)}) collective-permute-start(bf16[256,2304]{1,0:T(8,128)(2,1)} %get-tuple-element.35), channel_id=1, source_target_pairs={{0,24},{1,25},{2,26},{3,27},{4,28},{5,29},{6,30},{7,31},{8,16},{9,... | collective-permute-start | bytes 3538952 | tf_op jit(solution)/shard_map/ppermute | solution.py:364
  745.8 54.6 %collective-permute-start.43 = (bf16[256,2304]{1,0:T(8,128)(2,1)}, bf16[256,2304]{1,0:T(8,128)(2,1)}, u32[]{:S(2)}, u32[]{:S(2)}) collective-permute-start(bf16[256,2304]{1,0:T(8,128)(2,1)} %get-tuple-element.49), channel_id=1, source_target_pairs={{0,1},{1,0},{2,3},{3,2},{4,5},{5,4},{6,7},{7,6},{8,9},{9,8},{10,11... | collective-permute-start | bytes 3538952 | tf_op jit(solution)/shard_map/ppermute | solution.py:364
  811.1 72.0 %collective-permute-start.66 = (bf16[1,128,2304]{2,1,0:T(8,128)(2,1)}, bf16[1,128,2304]{2,1,0:T(8,128)(2,1)S(1)}, u32[]{:S(2)}, u32[]{:S(2)}) collective-permute-start(bf16[1,128,2304]{2,1,0:T(8,128)(2,1)} %pad_maximum_fusion.8), channel_id=1, source_target_pairs={{0,6},{1,7},{2,12},{3,13},{4,18},{5,19},{6,24},{7,25},{8,4},{9,5},... | collective-permute-start | bytes 1769480 | tf_op jit(solution)/shard_map/ppermute | solution.py:364
  815.9 40.4 %all-to-all-start.6 = ((bf16[8,72,1024]{2,1,0:T(8,128)(2,1)}), bf16[8,72,1024]{2,1,0:T(8,128)(2,1)S(1)}, u32[]{:S(2)}, u32[]{:S(2)}) async-start(bf16[8,72,1024]{2,1,0:T(8,128)(2,1)} %select_select_fusion.1), calls=%async_computation.10 | async-start | bytes 2359296 | tf_op jit(solution)/shard_map/all_to_all | solution.py:646
  822.4 61.6 %collective-permute-start.67 = (bf16[1,128,2304]{2,1,0:T(8,128)(2,1)}, bf16[1,128,2304]{2,1,0:T(8,128)(2,1)}, u32[]{:S(2)}, u32[]{:S(2)}) collective-permute-start(bf16[1,128,2304]{2,1,0:T(8,128)(2,1)} %pad_maximum_fusion.9), channel_id=1, source_target_pairs={{0,4},{1,5},{2,14},{3,15},{4,16},{5,17},{6,26},{7,27},{8,6},{9,7},... | collective-permute-start | bytes 1769480 | tf_op jit(solution)/shard_map/ppermute | solution.py:364
  826.3 57.7 %collective-permute-start.68 = (bf16[1,128,2304]{2,1,0:T(8,128)(2,1)}, bf16[1,128,2304]{2,1,0:T(8,128)(2,1)}, u32[]{:S(2)}, u32[]{:S(2)}) collective-permute-start(bf16[1,128,2304]{2,1,0:T(8,128)(2,1)} %pad_maximum_fusion.10), channel_id=1, source_target_pairs={{0,2},{1,3},{2,8},{3,9},{4,22},{5,23},{6,28},{7,29},{8,0},{9,1},{1... | collective-permute-start | bytes 1769480 | tf_op jit(solution)/shard_map/ppermute | solution.py:364
  832.5 51.4 %collective-permute-start.69 = (bf16[1,128,2304]{2,1,0:T(8,128)(2,1)}, bf16[1,128,2304]{2,1,0:T(8,128)(2,1)}, u32[]{:S(2)}, u32[]{:S(2)}) collective-permute-start(bf16[1,128,2304]{2,1,0:T(8,128)(2,1)} %pad_maximum_fusion.11), channel_id=1, source_target_pairs={{0,0},{1,1},{2,10},{3,11},{4,20},{5,21},{6,30},{7,31},{8,2},{9,3},... | collective-permute-start | bytes 1769480 | tf_op jit(solution)/shard_map/ppermute | solution.py:364
  888.6 42.5 %collective-permute-start.71 = (bf16[180,2304]{1,0:T(8,128)(2,1)}, bf16[180,2304]{1,0:T(8,128)(2,1)}, u32[]{:S(2)}, u32[]{:S(2)}) collective-permute-start(bf16[180,2304]{1,0:T(8,128)(2,1)} %after.75), channel_id=1, source_target_pairs={{0,0},{1,4},{2,8},{3,12},{4,16},{5,20},{6,24},{7,28},{8,1},{9,5},{... | collective-permute-start | bytes 2488328 | tf_op jit(solution)/shard_map/ppermute | solution.py:364
  892.3 37.9 %collective-permute-start.70 = (bf16[72,2304]{1,0:T(8,128)(2,1)}, bf16[72,2304]{1,0:T(8,128)(2,1)S(1)}, u32[]{:S(2)}, u32[]{:S(2)}) collective-permute-start(bf16[72,2304]{1,0:T(8,128)(2,1)} %after.74), channel_id=1, source_target_pairs={{0,0},{1,4},{2,1},{3,5},{4,2},{5,6},{6,3},{7,7},{8,8},{9,12},{10,9... | collective-permute-start | bytes 995336 | tf_op jit(solution)/shard_map/ppermute | solution.py:364
  (94 other events, 1163.4 us)
Sparse Core Ops, SparseCore 0:
  75.0 115.1 all-gather.4
  192.3 30.5 all-gather.6
  224.5 128.0 all-gather.8
  354.0 67.9 all-gather.10
  439.7 63.8 reduce-scatter.4
  523.8 121.6 reduce-scatter.6
  648.4 31.9 reduce-scatter.8
  712.7 83.7 reduce-scatter.10
